TPU v7x, 32 devices: a whole 2x2x4 slice. The times are simulated.
32 devices in a mesh: parts: 2 (over x), wide: 8 (over z, y), narrow: 2 (over core).
Axes of the slice: x: 2, y: 2, z: 4, core: 2. Of those that a mesh axis runs over, the one named last changes fastest.
Arguments:
- embeddings: bfloat16 [24576, 1024], P(('parts', 'wide', 'narrow')), parts along dimension 0, may hold values from -6 to 6
- labels: int32 [24576, 1], P(('parts', 'wide', 'narrow')), parts along dimension 0, may hold values from 0 to 7; in each aligned block of 768 rows (0 to 767, 768 to 1535, ...) at most 192 rows name the same one
- priority: int32 [24576], P(('parts', 'wide', 'narrow')), parts along dimension 0, may hold values from 0 to 12287, each once
Outputs:
- best_match: float32 [24576], P(('parts', 'wide', 'narrow')), parts along dimension 0
There are 2 independent parts, one for each index of `parts`. A program takes and returns all parts, laid end to end along the dimension named above; each array names one. Nothing has to cross between parts.
Inputs may be any that keep to these rules, and one draw needn't show every extreme that they name: `labels`: among the rows of one device at most 192 carry one label; in every draw some device has 192 rows of one label. `priority`: all priorities are distinct.
All inputs are finite; a program needn't handle non-finite values.
Results may differ from a plain program's by a relative error of at most 0.0014.
Values may be sent and summed in bfloat16 or wider, within the bound.
No kernel may reach another device: no remote copies, remote signals or barrier semaphores. Data moves between devices by JAX's collectives and lax.ppermute only.
A program may use at most 64 MiB of HBM per device.

v0:
```python
import math

import jax
import jax.numpy as jnp
from jax import lax
from jax.sharding import PartitionSpec as P


def local(embeddings, labels, priority):
    rows_dev, width = embeddings.shape
    groups = lax.axis_size("wide")
    slots = 2 * rows_dev // groups
    emb = embeddings.astype(jnp.float32)
    unit = (emb * lax.rsqrt(jnp.sum(emb * emb, axis=1, keepdims=True) + 1e-06)).astype(jnp.bfloat16)
    lab = labels[:, 0]
    onehot = (lab[:, None] == jnp.arange(groups, dtype=jnp.int32)[None, :]).astype(jnp.int32)
    slot_of = jnp.sum((jnp.cumsum(onehot, axis=0) - onehot) * onehot, axis=1)
    target = lab * slots + slot_of
    buffer = jnp.zeros((groups * slots, width), jnp.bfloat16).at[target].set(unit)
    ranks = jnp.full((groups * slots,), -1, jnp.int32).at[target].set(priority)
    buffer = buffer.reshape(groups, slots, width)
    ranks = ranks.reshape(groups, slots)
    got_rows, got_ranks = (
        lax.all_to_all(buffer, "wide", split_axis=0, concat_axis=0, tiled=True),
        lax.all_to_all(ranks, "wide", split_axis=0, concat_axis=0, tiled=True),
    )
    queries = got_rows.reshape(groups * slots, width)
    query_ranks = got_ranks.reshape(groups * slots)
    keys, key_ranks = (
        lax.all_gather(queries, "narrow", axis=0, tiled=True),
        lax.all_gather(query_ranks, "narrow", axis=0, tiled=True),
    )
    count = groups * slots
    block = math.gcd(count, 512)

    def score(pieces):
        query_block, rank_block = pieces
        similar = lax.dot_general(
            query_block, keys, (((1,), (1,)), ((), ())), preferred_element_type=jnp.float32
        )
        mask = (key_ranks[None, :] >= 0) & (key_ranks[None, :] < rank_block[:, None])
        return jnp.max(jnp.where(mask, similar, -1.0), axis=1)

    best = lax.map(
        score,
        (queries.reshape(count // block, block, width), query_ranks.reshape(count // block, block)),
    )
    returned = lax.all_to_all(
        best.reshape(groups, slots), "wide", split_axis=0, concat_axis=0, tiled=True
    )
    return returned.reshape(groups * slots)[target]


def solution(mesh):
    in_specs = (
        P(("parts", "wide", "narrow"), None),
        P(("parts", "wide", "narrow"), None),
        P(("parts", "wide", "narrow")),
    )
    out_specs = P(("parts", "wide", "narrow"))
    return jax.shard_map(local, mesh=mesh, in_specs=in_specs, out_specs=out_specs, check_vma=False)
```

profile of v0, /device:TPU:0, one launch (start us, length us, event | category | flops | bytes accessed | tf_op | source)
XLA Modules:
  0.0 163.4 jit_solution(16734140187861306147)
XLA Ops:
  6.5 0.7 reduce
  7.3 1.7 %reduce-window.6 = s32[8,6,128]{2,0,1:T(8,128)S(1)} reduce-window(s32[8,6,128]{2,0,1:T(8,128)S(1)} %fusion.11, s32[]{:T(128)} %constant.17.clone.1), window={size=1x1x128 pad=0_0x0_0x127_0}, to_apply=%region_0.0 | reduce-window | flops 780288 | bytes 49156 | tf_op jit(solution)/shard_map/reduce-window
  9.0 0.1 copy.8
  9.2 0.2 reduce-window.9
  9.3 0.1 copy.9
  9.4 0.1 fusion.10
  9.5 0.7 fusion.14
  10.2 1.8 %fusion.3 = f32[768]{0:T(1024)S(1)} fusion(bf16[768,1024]{1,0:T(8,128)(2,1)} %param.5), kind=kLoop, calls=%fused_computation.11 | loop fusion | flops 2358528 | bytes 1575936 | tf_op jit(solution)/shard_map/reduce_sum | solution.py:14
  12.0 10.4 %scatter_custom_fusion.1 = bf16[1536,1024]{1,0:T(8,128)(2,1)S(1)} fusion(s32[768]{0:T(1024)S(1)} %fusion.14, bf16[768,1024]{1,0:T(8,128)(2,1)} %param.5, f32[768]{0:T(1024)S(1)} %add_rsqrt_fusion, bf16[]{:T(256)} %constant.19.clone.1), kind=kCustom, calls=%fused_computation.13 | custom fusion | flops 2359296 | bytes 4722690 | tf_op jit(solution)/shard_map/scatter | solution.py:19
  22.4 77.9 %all_to_all.23 = bf16[8,192,1024]{2,1,0:T(8,128)(2,1)} all-to-all(bf16[8,192,1024]{2,1,0:T(8,128)(2,1)S(1)} %bitcast.31), channel_id=1, replica_groups=mesh['parts'=2,'wide'=8,'narrow'=2] {'wide'}, dimensions={0} | all-to-all | bytes 6291456 | tf_op jit(solution)/shard_map/all_to_all | solution.py:24
  100.3 3.5 %scatter_custom_fusion = s32[1536]{0:T(1024)S(1)} fusion(s32[768]{0:T(1024)S(1)} %fusion.14, s32[768]{0:T(1024)} %param.7, s32[]{:T(128)} %constant.25.clone.1), kind=kCustom, calls=%fused_computation.25 | custom fusion | bytes 6656 | tf_op jit(solution)/shard_map/scatter | solution.py:20
  103.9 0.7 all_to_all.15
  104.6 3.6 %all-to-all-start = ((s32[8,1,192]{2,1,0:T(1,128)}), s32[8,1,192]{2,1,0:T(1,128)S(1)}, u32[]{:S(2)}, u32[]{:S(2)}) async-start(s32[8,1,192]{2,1,0:T(1,128)} %all_to_all.15), calls=%async_computation | async-start | bytes 16384 | tf_op jit(solution)/shard_map/all_to_all | solution.py:25
  108.2 6.5 %all-to-all-done = s32[8,1,192]{2,1,0:T(1,128)S(1)} async-done(((s32[8,1,192]{2,1,0:T(1,128)}), s32[8,1,192]{2,1,0:T(1,128)S(1)}, u32[]{:S(2)}, u32[]{:S(2)}) %all-to-all-start) | async-done | bytes 6176 | tf_op jit(solution)/shard_map/all_to_all | solution.py:25
  114.7 0.1 reshape.82
  114.9 1.8 %all-gather = s32[2,1,1536]{2,1,0:T(1,128)S(1)} all-gather(s32[1,1,1536]{2,1,0:T(1,128)S(1)} %reshape.82), channel_id=1, replica_groups=mesh['parts'=2,'wide'=8,'narrow'=2] {'narrow'}, dimensions={0}, use_global_device_ids=true | all-gather | bytes 18432 | tf_op jit(solution)/shard_map/all_gather | solution.py:31
  116.7 21.1 %while.10 = (s32[]{:T(128)}, f32[3,512]{1,0:T(4,128)S(1)}, s32[3072]{0:T(1024)S(1)}, s32[3,512]{1,0:T(4,128)S(1)}, bf16[3,512,1024]{2,1,0:T(8,128)(2,1)}, /*index=5*/bf16[3072,1024]{1,0:T(8,128)(2,1)}, s32[]{:T(128)}, s32[]{:T(128)}) while((s32[]{:T(128)}, f32[3,512]{1,0:T(4,128)S(1)}, s32[3072]{0:T(1024)S(1)}, s32[3,512]{1,0:T(4,128)S(1)}, ...), condition=%wide.region_8.9_spmd, body=%wide.region_6.8_spmd.sunk | while | flops 3227519488 | bytes 7383645 | solution.py:44
  116.7 6.9 %select_reduce_fusion.2 = f32[512]{0:T(512)S(1)} fusion(bf16[3072,1024]{1,0:T(8,128)(2,1)} %get-tuple-element.108, s32[3072]{0:T(1024)S(1)} %get-tuple-element.105, s32[512]{0:T(512)S(1)} %bitcast.34, pred[3072]{0:T(1024)(128)(4,1)S(1)} %broadcast_compare_fusion.2, bf16[3,512,1024]{2,1,0:T(8,128)(2,1)} %get-tuple-element.107, s32[]{:T(128)} %get-tuple-element.95), kind=kOutput, calls=%fused_computation.3.clone.1 | convolution fusion | flops 3227516416 | bytes 7360000 | tf_op jit(solution)/shard_map/while/body/eval_jaxpr/dot_general | solution.py:38
  123.7 6.9 %select_reduce_fusion.2 = f32[512]{0:T(512)S(1)} fusion(bf16[3072,1024]{1,0:T(8,128)(2,1)} %get-tuple-element.108, s32[3072]{0:T(1024)S(1)} %get-tuple-element.105, s32[512]{0:T(512)S(1)} %bitcast.34, pred[3072]{0:T(1024)(128)(4,1)S(1)} %broadcast_compare_fusion.2, bf16[3,512,1024]{2,1,0:T(8,128)(2,1)} %get-tuple-element.107, s32[]{:T(128)} %get-tuple-element.95), kind=kOutput, calls=%fused_computation.3.clone.1 | convolution fusion | flops 3227516416 | bytes 7360000 | tf_op jit(solution)/shard_map/while/body/eval_jaxpr/dot_general | solution.py:38
  130.7 6.9 %select_reduce_fusion.2 = f32[512]{0:T(512)S(1)} fusion(bf16[3072,1024]{1,0:T(8,128)(2,1)} %get-tuple-element.108, s32[3072]{0:T(1024)S(1)} %get-tuple-element.105, s32[512]{0:T(512)S(1)} %bitcast.34, pred[3072]{0:T(1024)(128)(4,1)S(1)} %broadcast_compare_fusion.2, bf16[3,512,1024]{2,1,0:T(8,128)(2,1)} %get-tuple-element.107, s32[]{:T(128)} %get-tuple-element.95), kind=kOutput, calls=%fused_computation.3.clone.1 | convolution fusion | flops 3227516416 | bytes 7360000 | tf_op jit(solution)/shard_map/while/body/eval_jaxpr/dot_general | solution.py:38
  137.7 0.7 all_to_all.18
  138.4 5.4 %all-to-all-start.2 = ((f32[8,1,192]{2,1,0:T(1,128)}), f32[8,1,192]{2,1,0:T(1,128)S(1)}, u32[]{:S(2)}, u32[]{:S(2)}) async-start(f32[8,1,192]{2,1,0:T(1,128)} %all_to_all.18), calls=%async_computation.2 | async-start | bytes 16384 | tf_op jit(solution)/shard_map/all_to_all | solution.py:48
  143.8 6.5 %all-to-all-done.2 = f32[8,1,192]{2,1,0:T(1,128)S(1)} async-done(((f32[8,1,192]{2,1,0:T(1,128)}), f32[8,1,192]{2,1,0:T(1,128)S(1)}, u32[]{:S(2)}, u32[]{:S(2)}) %all-to-all-start.2) | async-done | bytes 6176 | tf_op jit(solution)/shard_map/all_to_all | solution.py:48
  150.4 6.1 %gather_fusion = f32[768]{0:T(1024)} fusion(f32[1536]{0:T(1024)S(1)} %reshape.57, s32[1024]{0:T(1024)S(1)} %pad_clamp_fusion), kind=kCustom, calls=%fused_computation | custom fusion | bytes 9216 | tf_op jit(solution)/shard_map/gather | solution.py:51
  (21 shorter events, 0.5 us)
Async XLA Ops:
  6.5 110.1 %all-gather.3.cloned.1.call-start = ((), (), s32[]{:S(2)}) async-start(), calls=%async_computation.3 | async-start | bytes 9437184 | tf_op jit(solution)/shard_map/all_gather | solution.py:30
  104.6 10.1 %all-to-all-start = ((s32[8,1,192]{2,1,0:T(1,128)}), s32[8,1,192]{2,1,0:T(1,128)S(1)}, u32[]{:S(2)}, u32[]{:S(2)}) async-start(s32[8,1,192]{2,1,0:T(1,128)} %all_to_all.15), calls=%async_computation | async-start | bytes 16384 | tf_op jit(solution)/shard_map/all_to_all | solution.py:25
  138.4 11.9 %all-to-all-start.2 = ((f32[8,1,192]{2,1,0:T(1,128)}), f32[8,1,192]{2,1,0:T(1,128)S(1)}, u32[]{:S(2)}, u32[]{:S(2)}) async-start(f32[8,1,192]{2,1,0:T(1,128)} %all_to_all.18), calls=%async_computation.2 | async-start | bytes 16384 | tf_op jit(solution)/shard_map/all_to_all | solution.py:48
Sparse Core Ops, SparseCore 0:
  100.5 15.7 all-gather.2
where the time goes:
time: 164 us; the launch traced here: 163 us
  blocking collectives  79.7 us (49%)
  matrix products  20.8 us (13%)
  other arithmetic  15.6 us (10%)
  between operations  13.5 us (8%)
  waiting for transfers between devices  13 us (8%)
  local copies, waits for them, and re-layouts  11.7 us (7%)
  starting transfers between devices  8.95 us (5%)
    all_to_all x1, blocking collectives, local(): lax.all_to_all(buffer, 'wide', split_axis=0, concat_axis=0, tiled=True)  77.9 us
    dot_general x3, matrix products, score(): lax.dot_general(query_block, keys, (((1,), (1,)), ((), ())), preferred_el...  20.8 us
    scatter x1, other arithmetic, local(): jnp.zeros((groups * slots, width), jnp.bfloat16).at[target].set(unit)  10.4 us
    all_to_all x1, waiting for transfers between devices, local(): lax.all_to_all(ranks, 'wide', split_axis=0, concat_axis=0, tiled=True)  6.51 us
    all_to_all x1, waiting for transfers between devices, local(): lax.all_to_all(best.reshape(groups, slots), 'wide', split_axis=0, concat_...  6.51 us
    gather x1, local copies, waits for them, and re-layouts, local(): return returned.reshape(groups * slots)[target]  6.14 us
    all_to_all x1, starting transfers between devices, local(): lax.all_to_all(best.reshape(groups, slots), 'wide', split_axis=0, concat_...  5.36 us
    all_to_all x1, starting transfers between devices, local(): lax.all_to_all(ranks, 'wide', split_axis=0, concat_axis=0, tiled=True)  3.59 us
  transfers between devices with their start and end apart: 3, of which 2 were waited for; matrix products, arithmetic and copies ran while one was open for 2% of the time, Pallas kernels for 0%

commit v1 on v0

v1 whole, which is shorter than its diff:
```python
import functools

import jax
import jax.numpy as jnp
from jax import lax
from jax.experimental import pallas as pl
from jax.experimental.pallas import tpu as pltpu
from jax.sharding import PartitionSpec as P

EMPTY = 1e9
VMEM_LIMIT = 48 * 1024 * 1024


def _nt(a, b):
    return lax.dot_general(a, b, (((1,), (1,)), ((), ())), preferred_element_type=jnp.float32)


def _slot_rows(lab, pos, dest, slots):
    key = jnp.where(lab == dest, pos, -1)
    places = lax.broadcasted_iota(jnp.int32, (slots, lab.shape[1]), 0)
    return (places == key).astype(jnp.float32).astype(jnp.bfloat16)


def _pack_first(partners, groups, slots, me_ref, emb_ref, lab_ref, prio_ref, unit_ref, pos_ref, ranks_ref, *outs):
    rows = emb_ref.shape[0]
    lab = lab_ref[...]
    onehot = (lax.broadcasted_iota(jnp.int32, (groups, rows), 0) == lab).astype(jnp.float32)
    before = lax.broadcasted_iota(jnp.int32, (rows, rows), 0) < lax.broadcasted_iota(jnp.int32, (rows, rows), 1)
    earlier = jnp.dot(
        onehot.astype(jnp.bfloat16),
        before.astype(jnp.float32).astype(jnp.bfloat16),
        preferred_element_type=jnp.float32,
    )
    pos = jnp.sum(onehot * earlier, axis=0, keepdims=True).astype(jnp.int32)
    pos_ref[...] = pos
    emb = emb_ref[...].astype(jnp.float32)
    unit = (emb * lax.rsqrt(jnp.sum(emb * emb, axis=1, keepdims=True) + 1e-06)).astype(jnp.bfloat16)
    unit_ref[...] = unit
    for partner, out in zip(partners, outs):
        pick = _slot_rows(lab, pos, jnp.bitwise_xor(me_ref[0], partner), slots)
        out[...] = jnp.dot(pick, unit, preferred_element_type=jnp.float32).astype(jnp.bfloat16)
    prio = prio_ref[...]
    high = (prio >> 8).astype(jnp.float32)
    low = (prio & 255).astype(jnp.float32)
    parts = jnp.concatenate([onehot * high, onehot * low, onehot], axis=0).astype(jnp.bfloat16)
    places = lax.broadcasted_iota(jnp.int32, (slots, rows), 0)
    placed = _nt(parts, (places == pos).astype(jnp.float32).astype(jnp.bfloat16))
    rank = placed[:groups] * 256.0 + placed[groups : 2 * groups]
    ranks_ref[...] = jnp.where(placed[2 * groups :] > 0.5, rank, EMPTY)


def _pack_rest(partners, slots, me_ref, unit_ref, lab_ref, pos_ref, *outs):
    for partner, out in zip(partners, outs):
        pick = _slot_rows(lab_ref[...], pos_ref[...], jnp.bitwise_xor(me_ref[0], partner), slots)
        out[...] = jnp.dot(pick, unit_ref[...], preferred_element_type=jnp.float32).astype(jnp.bfloat16)


def _score(order, n_old, slots, me_ref, own_ranks_ref, sib_ranks_ref, prev_ref, *rest):
    n = len(order)
    own, sib = rest[:n], rest[n : 2 * n]
    out_ref, q_scr, k_scr, q_rank, k_rank, sems = rest[2 * n :]
    copies = []
    for j in range(n):
        spans = [
            (own[j], k_scr.at[pl.ds(2 * j * slots, slots)]),
            (sib[j], k_scr.at[pl.ds((2 * j + 1) * slots, slots)]),
            (own[j], q_scr.at[pl.ds(j * slots, slots)]),
        ]
        for i, (src, dst) in enumerate(spans):
            if i < 2 or n_old < n:
                copy = pltpu.make_async_copy(src, dst, sems.at[j, i])
                copy.start()
                copies.append(copy)
    for j in range(n):
        source = jnp.bitwise_xor(me_ref[0], order[j])
        q_rank[pl.ds(j, 1), :] = own_ranks_ref[pl.ds(source, 1), :]
        k_rank[pl.ds(2 * j, 1), :] = own_ranks_ref[pl.ds(source, 1), :]
        k_rank[pl.ds(2 * j + 1, 1), :] = sib_ranks_ref[pl.ds(source, 1), :]
    k_col = jnp.transpose(k_rank[...])
    key_col = jnp.concatenate([k_col[:, j : j + 1] for j in range(2 * n)], axis=0)
    query_row = jnp.concatenate([q_rank[j : j + 1, :] for j in range(n)], axis=1)
    for copy in copies:
        copy.wait()

    def best_of(keys, queries):
        sim = _nt(k_scr[keys[0] * slots : keys[1] * slots, :], q_scr[queries[0] * slots : queries[1] * slots, :])
        mask = key_col[keys[0] * slots : keys[1] * slots] < query_row[:, queries[0] * slots : queries[1] * slots]
        return jnp.max(jnp.where(mask, sim, -1.0), axis=0, keepdims=True)

    rows = []
    if n_old:
        old = best_of((2 * n_old, 2 * n), (0, n_old))
        rows += [jnp.maximum(old[:, j * slots : (j + 1) * slots], prev_ref[j : j + 1, :]) for j in range(n_old)]
    new = best_of((0, 2 * n), (n_old, n))
    rows += [new[:, j * slots : (j + 1) * slots] for j in range(n - n_old)]
    last = n == out_ref.shape[0]
    for j in range(n):
        if last:
            out_ref[pl.ds(jnp.bitwise_xor(me_ref[0], order[j]), 1), :] = rows[j]
        else:
            out_ref[pl.ds(j, 1), :] = rows[j]


def _select(groups, lab_ref, pos_ref, got_ref, out_ref):
    slots = got_ref.shape[1]
    rows = lab_ref.shape[1]
    got = got_ref[...]
    a = got.astype(jnp.bfloat16)
    rest = got - a.astype(jnp.float32)
    b = rest.astype(jnp.bfloat16)
    c = (rest - b.astype(jnp.float32)).astype(jnp.bfloat16)
    places = lax.broadcasted_iota(jnp.int32, (slots, rows), 0)
    pick = (places == pos_ref[...]).astype(jnp.float32).astype(jnp.bfloat16)
    value = jnp.dot(a, pick, preferred_element_type=jnp.float32)
    value += jnp.dot(b, pick, preferred_element_type=jnp.float32)
    value += jnp.dot(c, pick, preferred_element_type=jnp.float32)
    mine = lax.broadcasted_iota(jnp.int32, (groups, rows), 0) == lab_ref[...]
    out_ref[...] = jnp.sum(jnp.where(mine, value, 0.0), axis=0, keepdims=True)


SMEM = pl.BlockSpec(memory_space=pltpu.SMEM)
VMEM = pl.BlockSpec(memory_space=pltpu.VMEM)
ANY = pl.BlockSpec(memory_space=pl.ANY)


def local(embeddings, labels, priority):
    rows, width = embeddings.shape
    groups = lax.axis_size("wide")
    slots = 2 * rows // groups
    half = groups // 2
    me = lax.axis_index("wide").astype(jnp.int32).reshape(1)
    lab = labels.reshape(1, rows)
    block = jax.ShapeDtypeStruct((slots, width), jnp.bfloat16)
    far, near = tuple(range(half, groups)), tuple(range(half))
    params = pltpu.CompilerParams(vmem_limit_bytes=VMEM_LIMIT)

    unit, pos, ranks, *far_blocks = pl.pallas_call(
        functools.partial(_pack_first, far, groups, slots),
        out_shape=[
            jax.ShapeDtypeStruct((rows, width), jnp.bfloat16),
            jax.ShapeDtypeStruct((1, rows), jnp.int32),
            jax.ShapeDtypeStruct((groups, slots), jnp.float32),
        ]
        + [block] * len(far),
        in_specs=[SMEM, VMEM, VMEM, VMEM],
        out_specs=[VMEM] * (3 + len(far)),
        compiler_params=params,
        name="pack_far",
    )(me, embeddings, lab, priority.reshape(1, rows))
    near_blocks = pl.pallas_call(
        functools.partial(_pack_rest, near, slots),
        out_shape=[block] * len(near),
        in_specs=[SMEM, VMEM, VMEM, VMEM],
        out_specs=[VMEM] * len(near),
        compiler_params=params,
        name="pack_near",
    )(me, unit, lab, pos)

    def swap(x):
        return lax.ppermute(x, "narrow", [(0, 1), (1, 0)])

    sent = dict(zip(far, far_blocks)) | dict(zip(near, near_blocks))
    own = {
        r: sent[r] if r == 0 else lax.ppermute(sent[r], "wide", [(s, s ^ r) for s in range(groups)])
        for r in far + near
    }
    own_ranks = lax.all_to_all(ranks, "wide", split_axis=0, concat_axis=0, tiled=True)
    sib_ranks = swap(own_ranks)
    sib = {r: swap(own[r]) for r in near + far}

    quarter = max(1, half // 4)
    steps = [near] + [far[i : i + quarter] for i in range(0, half, quarter)]
    order, best = (), jnp.zeros((groups, slots), jnp.float32)
    for step in steps:
        n_old = len(order)
        order = order + step
        n = len(order)
        best = pl.pallas_call(
            functools.partial(_score, order, n_old, slots),
            out_shape=jax.ShapeDtypeStruct((groups, slots), jnp.float32),
            in_specs=[SMEM, VMEM, VMEM, VMEM] + [ANY] * (2 * n),
            out_specs=VMEM,
            scratch_shapes=[
                pltpu.VMEM((n * slots, width), jnp.bfloat16),
                pltpu.VMEM((2 * n * slots, width), jnp.bfloat16),
                pltpu.VMEM((groups, slots), jnp.float32),
                pltpu.VMEM((2 * groups, slots), jnp.float32),
                pltpu.SemaphoreType.DMA((n, 3)),
            ],
            compiler_params=params,
            cost_estimate=pl.CostEstimate(
                flops=2 * width * slots * slots * 2 * (n_old * (n - n_old) + (n - n_old) * n),
                bytes_accessed=2 * n * slots * width * 2,
                transcendentals=0,
            ),
            name=f"score_{n}",
        )(me, own_ranks, sib_ranks, best, *[own[r] for r in order], *[sib[r] for r in order])

    returned = lax.all_to_all(best, "wide", split_axis=0, concat_axis=0, tiled=True)
    result = pl.pallas_call(
        functools.partial(_select, groups),
        out_shape=jax.ShapeDtypeStruct((1, rows), jnp.float32),
        in_specs=[VMEM, VMEM, VMEM],
        out_specs=VMEM,
        compiler_params=params,
        name="select",
    )(lab, pos, returned)
    return result.reshape(rows)


def solution(mesh):
    in_specs = (
        P(("parts", "wide", "narrow"), None),
        P(("parts", "wide", "narrow"), None),
        P(("parts", "wide", "narrow")),
    )
    out_specs = P(("parts", "wide", "narrow"))
    return jax.shard_map(local, mesh=mesh, in_specs=in_specs, out_specs=out_specs, check_vma=False)
```

time: 164 us -> 142 us (0.87)
  Pallas kernels: 0 us -> 36.9 us
  blocking collectives: 79.7 us -> 56.4 us
  matrix products: 20.8 us -> 0 us
  other arithmetic: 15.6 us -> 0.61 us
  waiting for transfers between devices: 13 us -> 27 us
  between operations: 13.5 us -> 0.13 us
  starting transfers between devices: 8.95 us -> 17.1 us
  local copies, waits for them, and re-layouts: 11.7 us -> 3.55 us
    pallas_call x0 -> x8, Pallas kernels: none -> 36.9 us  [the longest x5 33.3 us: local(): pl.pallas_call(functools.partial(_score, order, n_old, slots), out_shape=...]
    ppermute x0 -> x16, waiting for transfers between devices: none -> 27 us  [the longest x7 27 us: local(): lax.ppermute(sent[r], 'wide', [(s, s ^ r) for s in range(groups)])]
    all_to_all x1 -> x2, blocking collectives: 77.9 us -> 56.4 us  [the longest x1 47.5 us: local(): lax.all_to_all(ranks, 'wide', split_axis=0, concat_axis=0, tiled=True)]
    dot_general x3 -> x0, matrix products: 20.8 us -> none  [score(): lax.dot_general(query_block, keys, (((1,), (1,)), ((), ())), preferred_el...]
    ppermute x0 -> x16, starting transfers between devices: none -> 17.1 us  [the longest x7 16.1 us: local(): lax.ppermute(sent[r], 'wide', [(s, s ^ r) for s in range(groups)])]
    all_to_all x2 -> x0, waiting for transfers between devices: 13 us -> none  [the longest x1 6.51 us: local(): lax.all_to_all(ranks, 'wide', split_axis=0, concat_axis=0, tiled=True)]
    scatter x1 -> x0, other arithmetic: 10.4 us -> none  [local(): jnp.zeros((groups * slots, width), jnp.bfloat16).at[target].set(unit)]
    all_to_all x2 -> x0, starting transfers between devices: 8.94 us -> none  [the longest x1 5.36 us: local(): lax.all_to_all(best.reshape(groups, slots), 'wide', split_axis=0, concat_...]
  transfers between devices with their start and end apart: 3 -> 16, of which waited for: 2 -> 4; matrix products, arithmetic and copies ran while one was open for 2% -> 0% of each run, Pallas kernels for 0% -> 18%
where the time goes in v1:
time: 142 us
  blocking collectives  56.4 us (40%)
  Pallas kernels  36.9 us (26%)
  waiting for transfers between devices  27 us (19%)
  starting transfers between devices  17.1 us (12%)
  local copies, waits for them, and re-layouts  3.55 us (2%)
    all_to_all x1, blocking collectives, local(): lax.all_to_all(ranks, 'wide', split_axis=0, concat_axis=0, tiled=True)  47.5 us
    pallas_call x5, Pallas kernels, local(): pl.pallas_call(functools.partial(_score, order, n_old, slots), out_shape=...  33.3 us
    ppermute x7, waiting for transfers between devices, local(): lax.ppermute(sent[r], 'wide', [(s, s ^ r) for s in range(groups)])  27 us
    ppermute x7, starting transfers between devices, local(): lax.ppermute(sent[r], 'wide', [(s, s ^ r) for s in range(groups)])  16.1 us
    all_to_all x1, blocking collectives, local(): lax.all_to_all(best, 'wide', split_axis=0, concat_axis=0, tiled=True)  8.88 us
  transfers between devices with their start and end apart: 16, of which 4 were waited for; matrix products, arithmetic and copies ran while one was open for 0% of the time, Pallas kernels for 18%

profile of v1, /device:TPU:0, one launch (start us, length us, event | category | flops | bytes accessed | tf_op | source)
XLA Modules:
  0.0 141.7 jit_solution(17038301719397416388)
XLA Ops:
  0.0 0.7 reshape.18.prio_ref
  0.7 1.4 copy-done
  2.1 0.7 copy-done.1
  2.8 1.9 %pack_far.1 = (bf16[768,1024]{1,0:T(8,128)(2,1)S(1)}, s32[1,768]{1,0:T(1,128)S(1)}, f32[8,192]{1,0:T(8,128)S(1)}, bf16[192,1024]{1,0:T(8,128)(2,1)S(1)}, bf16[19...) custom-call(s32[1]{0:T(128)} %bitcast.1.me_ref, ...), custom_call_target="tpu_custom_call" | custom-call | tf_op jit(solution)/shard_map/pack_far/pallas_call | solution.py:137
  4.7 4.1 %collective-permute-start.8 = (bf16[192,1024]{1,0:T(8,128)(2,1)S(1)}, bf16[192,1024]{1,0:T(8,128)(2,1)S(1)}, u32[]{:S(2)}, u32[]{:S(2)}) collective-permute-start(bf16[192,1024]{1,0:T(8,128)(2,1)S(1)} %get-tuple-element.23), channel_id=1, source_target_pairs={{0,8},{2,10},{4,12},{6,14},{8,0},{10,2},{12,4},{14,6},{1,9},{3,11}... | collective-permute-start | bytes 1179656 | tf_op jit(solution)/shard_map/ppermute | solution.py:164
  8.8 1.3 collective-permute-start.10
  10.1 3.6 %collective-permute-start.12 = (bf16[192,1024]{1,0:T(8,128)(2,1)S(1)}, bf16[192,1024]{1,0:T(8,128)(2,1)S(1)}, u32[]{:S(2)}, u32[]{:S(2)}) collective-permute-start(bf16[192,1024]{1,0:T(8,128)(2,1)S(1)} %get-tuple-element.25), channel_id=1, source_target_pairs={{0,12},{2,14},{4,8},{6,10},{8,4},{10,6},{12,0},{14,2},{1,13},{3,15... | collective-permute-start | bytes 1179656 | tf_op jit(solution)/shard_map/ppermute | solution.py:164
  13.7 47.5 %all_to_all.22 = f32[8,1,192]{2,1,0:T(1,128)S(1)} all-to-all(f32[8,1,192]{2,1,0:T(1,128)S(1)} %copy.4), channel_id=1, replica_groups=mesh['parts'=2,'wide'=8,'narrow'=2] {'wide'}, dimensions={0} | all-to-all | bytes 12288 | tf_op jit(solution)/shard_map/all_to_all | solution.py:167
  61.2 1.4 pack_near.1
  62.6 0.7 collective-permute-start.1
  63.3 0.7 collective-permute-start.2
  64.0 2.2 %collective-permute-start.3 = (bf16[192,1024]{1,0:T(8,128)(2,1)S(1)}, bf16[192,1024]{1,0:T(8,128)(2,1)S(1)}, u32[]{:S(2)}, u32[]{:S(2)}) collective-permute-start(bf16[192,1024]{1,0:T(8,128)(2,1)S(1)} %get-tuple-element.22), channel_id=1, source_target_pairs={{0,6},{2,4},{4,2},{6,0},{8,14},{10,12},{12,10},{14,8},{1,7},{3,5},... | collective-permute-start | bytes 1179656 | tf_op jit(solution)/shard_map/ppermute | solution.py:164
  66.1 3.5 %collective-permute-start.14 = (bf16[192,1024]{1,0:T(8,128)(2,1)S(1)}, bf16[192,1024]{1,0:T(8,128)(2,1)S(1)}, u32[]{:S(2)}, u32[]{:S(2)}) collective-permute-start(bf16[192,1024]{1,0:T(8,128)(2,1)S(1)} %get-tuple-element.26), channel_id=1, source_target_pairs={{0,14},{2,12},{4,10},{6,8},{8,6},{10,4},{12,2},{14,0},{1,15},{3,13... | collective-permute-start | bytes 1179656 | tf_op jit(solution)/shard_map/ppermute | solution.py:164
  69.7 4.5 %collective-permute-done.1.rest_1_ = bf16[192,1024]{1,0:T(8,128)(2,1)S(1)} collective-permute-done((bf16[192,1024]{1,0:T(8,128)(2,1)S(1)}, bf16[192,1024]{1,0:T(8,128)(2,1)S(1)}, u32[]{:S(2)}, u32[]{:S(2)}) %collective-permute-start.1) | collective-permute-done | bytes 393248 | tf_op jit(solution)/shard_map/ppermute | solution.py:164
  74.2 1.0 collective-permute-done.2.rest_2_
  75.2 9.8 %collective-permute-done.3.rest_3_ = bf16[192,1024]{1,0:T(8,128)(2,1)S(1)} collective-permute-done((bf16[192,1024]{1,0:T(8,128)(2,1)S(1)}, bf16[192,1024]{1,0:T(8,128)(2,1)S(1)}, u32[]{:S(2)}, u32[]{:S(2)}) %collective-permute-start.3) | collective-permute-done | bytes 393248 | tf_op jit(solution)/shard_map/ppermute | solution.py:164
  85.0 11.7 %collective-permute-done.14.rest_7_ = bf16[192,1024]{1,0:T(8,128)(2,1)S(1)} collective-permute-done((bf16[192,1024]{1,0:T(8,128)(2,1)S(1)}, bf16[192,1024]{1,0:T(8,128)(2,1)S(1)}, u32[]{:S(2)}, u32[]{:S(2)}) %collective-permute-start.14) | collective-permute-done | bytes 393248 | tf_op jit(solution)/shard_map/ppermute | solution.py:164
  97.7 5.5 %score_4.1.prev_ref = f32[8,192]{1,0:T(8,128)S(1)} custom-call(s32[1]{0:T(128)} %bitcast.1.me_ref, f32[8,192]{1,0:T(8,128)S(1)} %bitcast.15, f32[8,192]{1,0:T(8,128)S(1)} %collective-permute-done.sib_ranks_ref, f32[8,192]{1,0:T(8,128)S(1)} %broadcast_in_dim.3.prev_ref, bf16[192,1024]{1,0:T(8,128)(2,1)S(1)} %get-tuple-element.19.rest_0_, ...), custom_call_target="tpu_custom_call" | custom-call | flops 2415919104 | bytes 3145728 | tf_op jit(solution)/shard_map/score_4/pallas_call | solution.py:178
  103.2 5.3 %score_5.1.prev_ref = f32[8,192]{1,0:T(8,128)S(1)} custom-call(s32[1]{0:T(128)} %bitcast.1.me_ref, f32[8,192]{1,0:T(8,128)S(1)} %bitcast.16, f32[8,192]{1,0:T(8,128)S(1)} %collective-permute-done.sib_ranks_ref, f32[8,192]{1,0:T(8,128)S(1)} %score_4.1.prev_ref, bf16[192,1024]{1,0:T(8,128)(2,1)S(1)} %get-tuple-element.19.rest_0_, ...), custom_call_target="tpu_custom_call" | custom-call | flops 1358954496 | bytes 3932160 | tf_op jit(solution)/shard_map/score_5/pallas_call | solution.py:178
  108.5 6.4 %score_6.1.prev_ref = f32[8,192]{1,0:T(8,128)S(1)} custom-call(s32[1]{0:T(128)} %bitcast.1.me_ref, f32[8,192]{1,0:T(8,128)S(1)} %bitcast.17, f32[8,192]{1,0:T(8,128)S(1)} %collective-permute-done.sib_ranks_ref, f32[8,192]{1,0:T(8,128)S(1)} %score_5.1.prev_ref, bf16[192,1024]{1,0:T(8,128)(2,1)S(1)} %get-tuple-element.19.rest_0_, ...), custom_call_target="tpu_custom_call" | custom-call | flops 1660944384 | bytes 4718592 | tf_op jit(solution)/shard_map/score_6/pallas_call | solution.py:178
  114.9 7.6 %score_7.1.prev_ref = f32[8,192]{1,0:T(8,128)S(1)} custom-call(s32[1]{0:T(128)} %bitcast.1.me_ref, f32[8,192]{1,0:T(8,128)S(1)} %bitcast.18, f32[8,192]{1,0:T(8,128)S(1)} %collective-permute-done.sib_ranks_ref, f32[8,192]{1,0:T(8,128)S(1)} %score_6.1.prev_ref, bf16[192,1024]{1,0:T(8,128)(2,1)S(1)} %get-tuple-element.19.rest_0_, ...), custom_call_target="tpu_custom_call" | custom-call | flops 1962934272 | bytes 5505024 | tf_op jit(solution)/shard_map/score_7/pallas_call | solution.py:178
  122.6 0.7 copy-done.3
  123.3 8.6 %score_8.1 = f32[8,192]{1,0:T(8,128)S(1)} custom-call(s32[1]{0:T(128)} %bitcast.1.me_ref, f32[8,192]{1,0:T(8,128)S(1)} %bitcast.19, f32[8,192]{1,0:T(8,128)S(1)} %collective-permute-done.sib_ranks_ref, f32[8,192]{1,0:T(8,128)S(1)} %score_7.1.prev_ref, bf16[192,1024]{1,0:T(8,128)(2,1)S(1)} %get-tuple-element.19.rest_0_, ...), custom_call_target="tpu_custom_call" | custom-call | flops 2264924160 | bytes 6291456 | tf_op jit(solution)/shard_map/score_8/pallas_call | solution.py:178
  131.9 8.9 %all_to_all.23 = f32[8,1,192]{2,1,0:T(1,128)S(1)} all-to-all(f32[8,1,192]{2,1,0:T(1,128)S(1)} %copy.5), channel_id=1, replica_groups=mesh['parts'=2,'wide'=8,'narrow'=2] {'wide'}, dimensions={0} | all-to-all | bytes 12288 | tf_op jit(solution)/shard_map/all_to_all | solution.py:199
  (33 shorter events, 2.0 us)
Async XLA Ops:
  0.7 1.4 copy-start
  2.1 0.7 copy-start.1
  4.7 59.3 %collective-permute-start.8 = (bf16[192,1024]{1,0:T(8,128)(2,1)S(1)}, bf16[192,1024]{1,0:T(8,128)(2,1)S(1)}, u32[]{:S(2)}, u32[]{:S(2)}) collective-permute-start(bf16[192,1024]{1,0:T(8,128)(2,1)S(1)} %get-tuple-element.23), channel_id=1, source_target_pairs={{0,8},{2,10},{4,12},{6,14},{8,0},{10,2},{12,4},{14,6},{1,9},{3,11}... | collective-permute-start | bytes 1179656 | tf_op jit(solution)/shard_map/ppermute | solution.py:164
  8.8 57.4 %collective-permute-start.10 = (bf16[192,1024]{1,0:T(8,128)(2,1)S(1)}, bf16[192,1024]{1,0:T(8,128)(2,1)S(1)}, u32[]{:S(2)}, u32[]{:S(2)}) collective-permute-start(bf16[192,1024]{1,0:T(8,128)(2,1)S(1)} %get-tuple-element.24), channel_id=1, source_target_pairs={{0,10},{2,8},{4,14},{6,12},{8,2},{10,0},{12,6},{14,4},{1,11},{3,9}... | collective-permute-start | bytes 1179656 | tf_op jit(solution)/shard_map/ppermute | solution.py:164
  10.1 59.6 %collective-permute-start.12 = (bf16[192,1024]{1,0:T(8,128)(2,1)S(1)}, bf16[192,1024]{1,0:T(8,128)(2,1)S(1)}, u32[]{:S(2)}, u32[]{:S(2)}) collective-permute-start(bf16[192,1024]{1,0:T(8,128)(2,1)S(1)} %get-tuple-element.25), channel_id=1, source_target_pairs={{0,12},{2,14},{4,8},{6,10},{8,4},{10,6},{12,0},{14,2},{1,13},{3,15... | collective-permute-start | bytes 1179656 | tf_op jit(solution)/shard_map/ppermute | solution.py:164
  61.2 2.1 %collective-permute-start = (f32[8,192]{1,0:T(8,128)S(1)}, f32[8,192]{1,0:T(8,128)S(1)}, u32[]{:S(2)}, u32[]{:S(2)}) collective-permute-start(f32[8,192]{1,0:T(8,128)S(1)} %bitcast.14), channel_id=1, source_target_pairs={{0,1},{1,0},{2,3},{3,2},{4,5},{5,4},{6,7},{7,6},{8,9},{9,8},{10,11... | collective-permute-start | bytes 18440 | tf_op jit(solution)/shard_map/ppermute | solution.py:160
  62.6 11.6 %collective-permute-start.1 = (bf16[192,1024]{1,0:T(8,128)(2,1)S(1)}, bf16[192,1024]{1,0:T(8,128)(2,1)S(1)}, u32[]{:S(2)}, u32[]{:S(2)}) collective-permute-start(bf16[192,1024]{1,0:T(8,128)(2,1)S(1)} %get-tuple-element.20), channel_id=1, source_target_pairs={{0,2},{2,0},{4,6},{6,4},{8,10},{10,8},{12,14},{14,12},{1,3},{3,1},... | collective-permute-start | bytes 1179656 | tf_op jit(solution)/shard_map/ppermute | solution.py:164
  63.3 11.9 %collective-permute-start.2 = (bf16[192,1024]{1,0:T(8,128)(2,1)S(1)}, bf16[192,1024]{1,0:T(8,128)(2,1)S(1)}, u32[]{:S(2)}, u32[]{:S(2)}) collective-permute-start(bf16[192,1024]{1,0:T(8,128)(2,1)S(1)} %get-tuple-element.21), channel_id=1, source_target_pairs={{0,4},{2,6},{4,0},{6,2},{8,12},{10,14},{12,8},{14,10},{1,5},{3,7},... | collective-permute-start | bytes 1179656 | tf_op jit(solution)/shard_map/ppermute | solution.py:164
  64.0 21.0 %collective-permute-start.3 = (bf16[192,1024]{1,0:T(8,128)(2,1)S(1)}, bf16[192,1024]{1,0:T(8,128)(2,1)S(1)}, u32[]{:S(2)}, u32[]{:S(2)}) collective-permute-start(bf16[192,1024]{1,0:T(8,128)(2,1)S(1)} %get-tuple-element.22), channel_id=1, source_target_pairs={{0,6},{2,4},{4,2},{6,0},{8,14},{10,12},{12,10},{14,8},{1,7},{3,5},... | collective-permute-start | bytes 1179656 | tf_op jit(solution)/shard_map/ppermute | solution.py:164
  66.1 30.5 %collective-permute-start.14 = (bf16[192,1024]{1,0:T(8,128)(2,1)S(1)}, bf16[192,1024]{1,0:T(8,128)(2,1)S(1)}, u32[]{:S(2)}, u32[]{:S(2)}) collective-permute-start(bf16[192,1024]{1,0:T(8,128)(2,1)S(1)} %get-tuple-element.26), channel_id=1, source_target_pairs={{0,14},{2,12},{4,10},{6,8},{8,6},{10,4},{12,2},{14,0},{1,15},{3,13... | collective-permute-start | bytes 1179656 | tf_op jit(solution)/shard_map/ppermute | solution.py:164
  69.7 27.0 %collective-permute-start.4 = (bf16[192,1024]{1,0:T(8,128)(2,1)S(1)}, bf16[192,1024]{1,0:T(8,128)(2,1)S(1)}, u32[]{:S(2)}, u32[]{:S(2)}) collective-permute-start(bf16[192,1024]{1,0:T(8,128)(2,1)S(1)} %get-tuple-element.19.rest_0_), channel_id=1, source_target_pairs={{0,1},{1,0},{2,3},{3,2},{4,5},{5,4},{6,7},{7,6},{8,9},{9,8},{10,11... | collective-permute-start | bytes 1179656 | tf_op jit(solution)/shard_map/ppermute | solution.py:160
  74.2 23.0 %collective-permute-start.5 = (bf16[192,1024]{1,0:T(8,128)(2,1)S(1)}, bf16[192,1024]{1,0:T(8,128)(2,1)S(1)}, u32[]{:S(2)}, u32[]{:S(2)}) collective-permute-start(bf16[192,1024]{1,0:T(8,128)(2,1)S(1)} %collective-permute-done.1.rest_1_), channel_id=1, source_target_pairs={{0,1},{1,0},{2,3},{3,2},{4,5},{5,4},{6,7},{7,6},{8,9},{9,8},{10,11... | collective-permute-start | bytes 1179656 | tf_op jit(solution)/shard_map/ppermute | solution.py:160
  75.2 22.1 %collective-permute-start.6 = (bf16[192,1024]{1,0:T(8,128)(2,1)S(1)}, bf16[192,1024]{1,0:T(8,128)(2,1)S(1)}, u32[]{:S(2)}, u32[]{:S(2)}) collective-permute-start(bf16[192,1024]{1,0:T(8,128)(2,1)S(1)} %collective-permute-done.2.rest_2_), channel_id=1, source_target_pairs={{0,1},{1,0},{2,3},{3,2},{4,5},{5,4},{6,7},{7,6},{8,9},{9,8},{10,11... | collective-permute-start | bytes 1179656 | tf_op jit(solution)/shard_map/ppermute | solution.py:160
  85.0 12.8 %collective-permute-start.7 = (bf16[192,1024]{1,0:T(8,128)(2,1)S(1)}, bf16[192,1024]{1,0:T(8,128)(2,1)S(1)}, u32[]{:S(2)}, u32[]{:S(2)}) collective-permute-start(bf16[192,1024]{1,0:T(8,128)(2,1)S(1)} %collective-permute-done.3.rest_3_), channel_id=1, source_target_pairs={{0,1},{1,0},{2,3},{3,2},{4,5},{5,4},{6,7},{7,6},{8,9},{9,8},{10,11... | collective-permute-start | bytes 1179656 | tf_op jit(solution)/shard_map/ppermute | solution.py:160
  96.7 6.5 %collective-permute-start.9 = (bf16[192,1024]{1,0:T(8,128)(2,1)S(1)}, bf16[192,1024]{1,0:T(8,128)(2,1)S(1)}, u32[]{:S(2)}, u32[]{:S(2)}) collective-permute-start(bf16[192,1024]{1,0:T(8,128)(2,1)S(1)} %collective-permute-done.8.rest_4_), channel_id=1, source_target_pairs={{0,1},{1,0},{2,3},{3,2},{4,5},{5,4},{6,7},{7,6},{8,9},{9,8},{10,11... | collective-permute-start | bytes 1179656 | tf_op jit(solution)/shard_map/ppermute | solution.py:160
  96.7 11.8 %collective-permute-start.11 = (bf16[192,1024]{1,0:T(8,128)(2,1)S(1)}, bf16[192,1024]{1,0:T(8,128)(2,1)S(1)}, u32[]{:S(2)}, u32[]{:S(2)}) collective-permute-start(bf16[192,1024]{1,0:T(8,128)(2,1)S(1)} %collective-permute-done.10.rest_5_), channel_id=1, source_target_pairs={{0,1},{1,0},{2,3},{3,2},{4,5},{5,4},{6,7},{7,6},{8,9},{9,8},{10,11... | collective-permute-start | bytes 1179656 | tf_op jit(solution)/shard_map/ppermute | solution.py:160
  97.2 17.7 %collective-permute-start.13 = (bf16[192,1024]{1,0:T(8,128)(2,1)S(1)}, bf16[192,1024]{1,0:T(8,128)(2,1)S(1)}, u32[]{:S(2)}, u32[]{:S(2)}) collective-permute-start(bf16[192,1024]{1,0:T(8,128)(2,1)S(1)} %collective-permute-done.12.rest_6_), channel_id=1, source_target_pairs={{0,1},{1,0},{2,3},{3,2},{4,5},{5,4},{6,7},{7,6},{8,9},{9,8},{10,11... | collective-permute-start | bytes 1179656 | tf_op jit(solution)/shard_map/ppermute | solution.py:160
  97.3 25.3 %collective-permute-start.15 = (bf16[192,1024]{1,0:T(8,128)(2,1)S(1)}, bf16[192,1024]{1,0:T(8,128)(2,1)S(1)}, u32[]{:S(2)}, u32[]{:S(2)}) collective-permute-start(bf16[192,1024]{1,0:T(8,128)(2,1)S(1)} %collective-permute-done.14.rest_7_), channel_id=1, source_target_pairs={{0,1},{1,0},{2,3},{3,2},{4,5},{5,4},{6,7},{7,6},{8,9},{9,8},{10,11... | collective-permute-start | bytes 1179656 | tf_op jit(solution)/shard_map/ppermute | solution.py:160
  122.5 18.3 %copy-start.2 = (s32[768,1]{0,1:T(1,128)S(1)}, s32[768,1]{0,1:T(1,128)}, u32[]{:S(2)}) copy-start(s32[768,1]{0,1:T(1,128)} %param.4) | copy-start | bytes 9220
  122.6 0.7 copy-start.3

commit v2 on v1

v2 whole, which is shorter than its diff:
```python
import functools

import jax
import jax.numpy as jnp
from jax import lax
from jax.experimental import pallas as pl
from jax.experimental.pallas import tpu as pltpu
from jax.sharding import PartitionSpec as P

EMPTY = 2.0**22
VMEM_LIMIT = 40 * 1024 * 1024
LANES = 128
TAIL = 16


def _nt(a, b):
    return lax.dot_general(a, b, (((1,), (1,)), ((), ())), preferred_element_type=jnp.float32)


def _as_bf16(mask):
    return mask.astype(jnp.float32).astype(jnp.bfloat16)


def _spans(slots):
    return -(-slots // LANES)


def _write_block(out, pick, unit, high, low, slots):
    block = jnp.dot(pick, unit, preferred_element_type=jnp.float32).astype(jnp.bfloat16)
    pieces = block.shape[1] // LANES
    for k in range(pieces):
        out[k * slots : (k + 1) * slots, :] = block[:, k * LANES : (k + 1) * LANES]
    spans = _spans(slots)
    lines = [part[:, i * LANES : (i + 1) * LANES] for part in (high, low) for i in range(spans)]
    lines.append(jnp.zeros((TAIL - 2 * spans, LANES), jnp.float32))
    out[pieces * slots :, :] = jnp.concatenate(lines, axis=0).astype(jnp.bfloat16)


def _block(ref, slots):
    return jnp.concatenate([ref[k * slots : (k + 1) * slots, :] for k in range(ref.shape[0] // slots)], axis=1)


def _ranks(ref, slots):
    tail = ref[ref.shape[0] - TAIL :, :].astype(jnp.float32)
    spans = _spans(slots)
    value = tail[:spans] * 256.0 + tail[spans : 2 * spans]
    return jnp.concatenate([value[i : i + 1] for i in range(spans)], axis=1)


def _pick(lab, pos, dest, slots):
    key = jnp.where(lab == dest, pos, -1)
    return _as_bf16(lax.broadcasted_iota(jnp.int32, (slots, lab.shape[1]), 0) == key)


def _pack_first(partners, groups, slots, me_ref, emb_ref, lab_ref, prio_ref, unit_ref, pos_ref, ranks_ref, *outs):
    rows = emb_ref.shape[0]
    lab = lab_ref[...]
    away = jnp.bitwise_xor(lax.broadcasted_iota(jnp.int32, (groups, rows), 0), me_ref[0])
    onehot = (away == lab).astype(jnp.float32)
    before = lax.broadcasted_iota(jnp.int32, (rows, rows), 0) < lax.broadcasted_iota(jnp.int32, (rows, rows), 1)
    earlier = jnp.dot(onehot.astype(jnp.bfloat16), _as_bf16(before), preferred_element_type=jnp.float32)
    pos = jnp.sum(onehot * earlier, axis=0, keepdims=True).astype(jnp.int32)
    pos_ref[...] = pos
    prio = prio_ref[...]
    high = (prio >> 8).astype(jnp.float32)
    low = (prio & 255).astype(jnp.float32)
    parts = jnp.concatenate([onehot * high, onehot * low, onehot], axis=0).astype(jnp.bfloat16)
    places = lax.broadcasted_iota(jnp.int32, (_spans(slots) * LANES, rows), 0)
    placed = _nt(parts, _as_bf16(places == pos))
    high = jnp.where(placed[2 * groups :] > 0.5, placed[:groups], EMPTY)
    low = placed[groups : 2 * groups]
    ranks_ref[...] = jnp.concatenate([high, low], axis=0)
    emb = emb_ref[...].astype(jnp.float32)
    unit = (emb * lax.rsqrt(jnp.sum(emb * emb, axis=1, keepdims=True) + 1e-06)).astype(jnp.bfloat16)
    unit_ref[...] = unit
    for partner, out in zip(partners, outs):
        pick = _pick(lab, pos, jnp.bitwise_xor(me_ref[0], partner), slots)
        _write_block(out, pick, unit, high[partner : partner + 1], low[partner : partner + 1], slots)


def _pack_rest(partners, groups, slots, me_ref, unit_ref, lab_ref, pos_ref, ranks_ref, *outs):
    for partner, out in zip(partners, outs):
        pick = _pick(lab_ref[...], pos_ref[...], jnp.bitwise_xor(me_ref[0], partner), slots)
        high = ranks_ref[partner : partner + 1, :]
        low = ranks_ref[groups + partner : groups + partner + 1, :]
        _write_block(out, pick, unit_ref[...], high, low, slots)


def _score(order, n_old, slots, me_ref, prev_ref, *rest):
    n = len(order)
    own, sib, out_ref = rest[:n], rest[n : 2 * n], rest[2 * n]
    refs = [ref for j in range(n) for ref in (own[j], sib[j])]
    ranks = jnp.concatenate([_ranks(ref, slots) for ref in refs], axis=0)
    columns = jnp.transpose(ranks)[:slots]

    def best_of(keys, queries):
        sim = _nt(
            jnp.concatenate([_block(refs[i], slots) for i in keys], axis=0),
            jnp.concatenate([_block(own[j], slots) for j in queries], axis=0),
        )
        key_ranks = jnp.concatenate([columns[:, i : i + 1] for i in keys], axis=0)
        query_ranks = jnp.concatenate([ranks[2 * j : 2 * j + 1, :slots] for j in queries], axis=1)
        best = jnp.max(jnp.where(key_ranks < query_ranks, sim, -1.0), axis=0, keepdims=True)
        return [best[:, i * slots : (i + 1) * slots] for i in range(len(queries))]

    rows = []
    if n_old:
        old = best_of(range(2 * n_old, 2 * n), range(n_old))
        rows += [jnp.maximum(old[j], prev_ref[j : j + 1, :]) for j in range(n_old)]
    rows += best_of(range(2 * n), range(n_old, n))
    last = n == out_ref.shape[0]
    for j in range(n):
        if last:
            out_ref[pl.ds(jnp.bitwise_xor(me_ref[0], order[j]), 1), :] = rows[j]
        else:
            out_ref[pl.ds(j, 1), :] = rows[j]


def _select(groups, lab_ref, pos_ref, got_ref, out_ref):
    slots = got_ref.shape[1]
    rows = lab_ref.shape[1]
    got = got_ref[...]
    a = got.astype(jnp.bfloat16)
    rest = got - a.astype(jnp.float32)
    b = rest.astype(jnp.bfloat16)
    c = (rest - b.astype(jnp.float32)).astype(jnp.bfloat16)
    pick = _as_bf16(lax.broadcasted_iota(jnp.int32, (slots, rows), 0) == pos_ref[...])
    value = jnp.dot(a, pick, preferred_element_type=jnp.float32)
    value += jnp.dot(b, pick, preferred_element_type=jnp.float32)
    value += jnp.dot(c, pick, preferred_element_type=jnp.float32)
    mine = lax.broadcasted_iota(jnp.int32, (groups, rows), 0) == lab_ref[...]
    out_ref[...] = jnp.sum(jnp.where(mine, value, 0.0), axis=0, keepdims=True)


SMEM = pl.BlockSpec(memory_space=pltpu.SMEM)
VMEM = pl.BlockSpec(memory_space=pltpu.VMEM)


def local(embeddings, labels, priority):
    rows, width = embeddings.shape
    groups = lax.axis_size("wide")
    slots = 2 * rows // groups
    half = groups // 2
    me = lax.axis_index("wide").astype(jnp.int32).reshape(1)
    lab = labels.reshape(1, rows)
    block = jax.ShapeDtypeStruct((width // LANES * slots + TAIL, LANES), jnp.bfloat16)
    far, near = tuple(range(half, groups)), tuple(range(half))
    params = pltpu.CompilerParams(vmem_limit_bytes=VMEM_LIMIT)

    unit, pos, ranks, *far_blocks = pl.pallas_call(
        functools.partial(_pack_first, far, groups, slots),
        out_shape=[
            jax.ShapeDtypeStruct((rows, width), jnp.bfloat16),
            jax.ShapeDtypeStruct((1, rows), jnp.int32),
            jax.ShapeDtypeStruct((2 * groups, _spans(slots) * LANES), jnp.float32),
        ]
        + [block] * len(far),
        in_specs=[SMEM, VMEM, VMEM, VMEM],
        out_specs=[VMEM] * (3 + len(far)),
        compiler_params=params,
        name="pack_far",
    )(me, embeddings, lab, priority.reshape(1, rows))
    near_blocks = pl.pallas_call(
        functools.partial(_pack_rest, near, groups, slots),
        out_shape=[block] * len(near),
        in_specs=[SMEM] + [VMEM] * 4,
        out_specs=[VMEM] * len(near),
        compiler_params=params,
        name="pack_near",
    )(me, unit, lab, pos, ranks)

    def swap(x):
        return lax.ppermute(x, "narrow", [(0, 1), (1, 0)])

    def send(x, r):
        return lax.ppermute(x, "wide", [(s, s ^ r) for s in range(groups)])

    def after(x, *others):
        return lax.optimization_barrier((x, *others))[0]

    own = {}
    for i, r in enumerate(far):
        out = far_blocks[i]
        dep = {6: (4, 5), 7: (4, 5)}.get(r)
        if dep is not None:
            out = after(out, *[own[d] for d in dep])
        own[r] = send(out, r)
    for i, r in enumerate(near):
        dep = {}.get(r)
        out = near_blocks[i] if dep is None else after(near_blocks[i], own[dep])
        own[r] = send(out, r) if r else out

    steps = [(0,1,2,3,4,5),(6,),(7,)]
    order, best, sib = (), jnp.zeros((groups, slots), jnp.float32), {}
    for step in steps:
        for r in step:
            sib[r] = swap(after(own[r], best) if r in (7,) else own[r])
        n_old = len(order)
        order = order + step
        n = len(order)
        best = pl.pallas_call(
            functools.partial(_score, order, n_old, slots),
            out_shape=jax.ShapeDtypeStruct((groups, slots), jnp.float32),
            in_specs=[SMEM] + [VMEM] * (1 + 2 * n),
            out_specs=VMEM,
            compiler_params=params,
            cost_estimate=pl.CostEstimate(
                flops=2 * width * slots * slots * 2 * (n_old * (n - n_old) + (n - n_old) * n),
                bytes_accessed=2 * n * slots * width * 2,
                transcendentals=0,
            ),
            name=f"score_{n}",
        )(me, best, *[own[r] for r in order], *[sib[r] for r in order])

    returned = lax.all_to_all(best, "wide", split_axis=0, concat_axis=0, tiled=True)
    result = pl.pallas_call(
        functools.partial(_select, groups),
        out_shape=jax.ShapeDtypeStruct((1, rows), jnp.float32),
        in_specs=[VMEM, VMEM, VMEM],
        out_specs=VMEM,
        compiler_params=params,
        name="select",
    )(lab, pos, returned)
    return result.reshape(rows)


def solution(mesh):
    in_specs = (
        P(("parts", "wide", "narrow"), None),
        P(("parts", "wide", "narrow"), None),
        P(("parts", "wide", "narrow")),
    )
    out_specs = P(("parts", "wide", "narrow"))
    return jax.shard_map(local, mesh=mesh, in_specs=in_specs, out_specs=out_specs, check_vma=False)
```

time: 142 us -> 99.6 us (0.70)
  blocking collectives: 56.4 us -> 23.5 us
  Pallas kernels: 36.9 us -> 16.4 us
  waiting for transfers between devices: 27 us -> 40.1 us
    all_to_all x1 -> x0, blocking collectives: 47.5 us -> none  [local(): lax.all_to_all(ranks, 'wide', split_axis=0, concat_axis=0, tiled=True)]
    pallas_call x5 -> x3, Pallas kernels: 33.3 us -> 12.8 us  [local(): pl.pallas_call(functools.partial(_score, order, n_old, slots), out_shape=...]
    all_to_all x1, blocking collectives: 8.88 us -> 23.5 us  [local(): lax.all_to_all(best, 'wide', split_axis=0, concat_axis=0, tiled=True)]
    ppermute x7, waiting for transfers between devices: 27 us -> 38.7 us  [send(): return lax.ppermute(x, 'wide', [(s, s ^ r) for s in range(groups)])]
    ppermute x7, starting transfers between devices: 16.1 us -> 14.5 us  [send(): return lax.ppermute(x, 'wide', [(s, s ^ r) for s in range(groups)])]
  transfers between devices with their start and end apart: 16 -> 15, of which waited for: 4 -> 5; matrix products, arithmetic and copies ran while one was open for 0% -> 0% of each run, Pallas kernels for 18% -> 10%
where the time goes in v2:
time: 99.6 us; the launch traced here: 99.4 us
  waiting for transfers between devices  40.1 us (40%)
  blocking collectives  23.5 us (24%)
  Pallas kernels  16.4 us (16%)
  starting transfers between devices  15.8 us (16%)
  local copies, waits for them, and re-layouts  2.8 us (3%)
    ppermute x7, waiting for transfers between devices, send(): return lax.ppermute(x, 'wide', [(s, s ^ r) for s in range(groups)])  38.7 us
    all_to_all x1, blocking collectives, local(): lax.all_to_all(best, 'wide', split_axis=0, concat_axis=0, tiled=True)  23.5 us
    ppermute x7, starting transfers between devices, send(): return lax.ppermute(x, 'wide', [(s, s ^ r) for s in range(groups)])  14.5 us
    pallas_call x3, Pallas kernels, local(): pl.pallas_call(functools.partial(_score, order, n_old, slots), out_shape=...  12.8 us
    unnamed x7, local copies, waits for them, and re-layouts  2.1 us
  transfers between devices with their start and end apart: 15, of which 5 were waited for; matrix products, arithmetic and copies ran while one was open for 0% of the time, Pallas kernels for 10%

profile of v2, /device:TPU:0, one launch (start us, length us, event | category | flops | bytes accessed | tf_op | source)
XLA Modules:
  0.0 99.4 jit_solution(8967879569938081466)
XLA Ops:
  0.0 0.7 reshape.16.prio_ref
  0.7 1.4 %copy-done = bf16[768,1024]{1,0:T(8,128)(2,1)S(1)} copy-done((bf16[768,1024]{1,0:T(8,128)(2,1)S(1)}, bf16[768,1024]{1,0:T(8,128)(2,1)}, u32[]{:S(2)}) %copy-start) | copy-done | bytes 1572888
  2.1 0.7 copy-done.1
  2.8 2.0 %pack_far.1 = (bf16[768,1024]{1,0:T(8,128)(2,1)S(1)}, s32[1,768]{1,0:T(1,128)S(1)}, f32[16,256]{1,0:T(8,128)S(1)}, bf16[1552,128]{1,0:T(8,128)(2,1)S(1)}, bf16[1...) custom-call(s32[1]{0:T(128)} %bitcast.1.me_ref, ...), custom_call_target="tpu_custom_call" | custom-call | tf_op jit(solution)/shard_map/pack_far/pallas_call | solution.py:150
  4.8 1.4 %pack_near.1 = (bf16[1552,128]{1,0:T(8,128)(2,1)S(1)}, bf16[1552,128]{1,0:T(8,128)(2,1)S(1)}, bf16[1552,128]{1,0:T(8,128)(2,1)S(1)}, bf16[1552,128]{1,0:T(8,128)(2,1)S(1)}) custom-call(s32[1]{0:T(128)} %bitcast.1.me_ref, bf16[768,1024]{1,0:T(8,128)(2,1)S(1)} %get-tuple-element.20.unit_ref, s32[1,768]{1,0:T(1,128)S(1)} %bitcast.8, ...), custom_call_target="tpu_custom_call" | custom-call | tf_op jit(solution)/shard_map/pack_near/pallas_call | solution.py:163
  6.2 3.0 %collective-permute-start = (bf16[1552,128]{1,0:T(8,128)(2,1)S(1)}, bf16[1552,128]{1,0:T(8,128)(2,1)S(1)}, u32[]{:S(2)}, u32[]{:S(2)}) collective-permute-start(bf16[1552,128]{1,0:T(8,128)(2,1)S(1)} %get-tuple-element.23), channel_id=1, source_target_pairs={{0,2},{2,0},{4,6},{6,4},{8,10},{10,8},{12,14},{14,12},{1,3},{3,1},... | collective-permute-start | bytes 1191944 | tf_op jit(solution)/shard_map/ppermute | solution.py:176
  9.2 2.6 %collective-permute-start.3 = (bf16[1552,128]{1,0:T(8,128)(2,1)S(1)}, bf16[1552,128]{1,0:T(8,128)(2,1)S(1)}, u32[]{:S(2)}, u32[]{:S(2)}) collective-permute-start(bf16[1552,128]{1,0:T(8,128)(2,1)S(1)} %get-tuple-element.26), channel_id=1, source_target_pairs={{0,8},{2,10},{4,12},{6,14},{8,0},{10,2},{12,4},{14,6},{1,9},{3,11}... | collective-permute-start | bytes 1191944 | tf_op jit(solution)/shard_map/ppermute | solution.py:176
  11.8 1.9 %collective-permute-start.1 = (bf16[1552,128]{1,0:T(8,128)(2,1)S(1)}, bf16[1552,128]{1,0:T(8,128)(2,1)S(1)}, u32[]{:S(2)}, u32[]{:S(2)}) collective-permute-start(bf16[1552,128]{1,0:T(8,128)(2,1)S(1)} %get-tuple-element.24), channel_id=1, source_target_pairs={{0,4},{2,6},{4,0},{6,2},{8,12},{10,14},{12,8},{14,10},{1,5},{3,7},... | collective-permute-start | bytes 1191944 | tf_op jit(solution)/shard_map/ppermute | solution.py:176
  13.7 1.4 %collective-permute-start.2 = (bf16[1552,128]{1,0:T(8,128)(2,1)S(1)}, bf16[1552,128]{1,0:T(8,128)(2,1)S(1)}, u32[]{:S(2)}, u32[]{:S(2)}) collective-permute-start(bf16[1552,128]{1,0:T(8,128)(2,1)S(1)} %get-tuple-element.25), channel_id=1, source_target_pairs={{0,6},{2,4},{4,2},{6,0},{8,14},{10,12},{12,10},{14,8},{1,7},{3,5},... | collective-permute-start | bytes 1191944 | tf_op jit(solution)/shard_map/ppermute | solution.py:176
  15.1 3.4 %collective-permute-done.rest_1_ = bf16[1552,128]{1,0:T(8,128)(2,1)S(1)} collective-permute-done((bf16[1552,128]{1,0:T(8,128)(2,1)S(1)}, bf16[1552,128]{1,0:T(8,128)(2,1)S(1)}, u32[]{:S(2)}, u32[]{:S(2)}) %collective-permute-start) | collective-permute-done | bytes 397344 | tf_op jit(solution)/shard_map/ppermute | solution.py:176
  18.4 20.7 %collective-permute-done.3.rest_4_ = bf16[1552,128]{1,0:T(8,128)(2,1)S(1)} collective-permute-done((bf16[1552,128]{1,0:T(8,128)(2,1)S(1)}, bf16[1552,128]{1,0:T(8,128)(2,1)S(1)}, u32[]{:S(2)}, u32[]{:S(2)}) %collective-permute-start.3) | collective-permute-done | bytes 397344 | tf_op jit(solution)/shard_map/ppermute | solution.py:176
  39.1 7.2 %collective-permute-done.4.rest_5_ = bf16[1552,128]{1,0:T(8,128)(2,1)S(1)} collective-permute-done((bf16[1552,128]{1,0:T(8,128)(2,1)S(1)}, bf16[1552,128]{1,0:T(8,128)(2,1)S(1)}, u32[]{:S(2)}, u32[]{:S(2)}) %collective-permute-start.4) | collective-permute-done | bytes 397344 | tf_op jit(solution)/shard_map/ppermute | solution.py:176
  46.3 3.5 %collective-permute-start.11 = (bf16[1552,128]{1,0:T(8,128)(2,1)S(1)}, bf16[1552,128]{1,0:T(8,128)(2,1)S(1)}, u32[]{:S(2)}, u32[]{:S(2)}) collective-permute-start(bf16[1552,128]{1,0:T(8,128)(2,1)S(1)} %get-tuple-element.29), channel_id=1, source_target_pairs={{0,12},{2,14},{4,8},{6,10},{8,4},{10,6},{12,0},{14,2},{1,13},{3,15... | collective-permute-start | bytes 1191944 | tf_op jit(solution)/shard_map/ppermute | solution.py:176
  50.1 0.3 collective-permute-start.8
  50.6 2.1 %collective-permute-start.13 = (bf16[1552,128]{1,0:T(8,128)(2,1)S(1)}, bf16[1552,128]{1,0:T(8,128)(2,1)S(1)}, u32[]{:S(2)}, u32[]{:S(2)}) collective-permute-start(bf16[1552,128]{1,0:T(8,128)(2,1)S(1)} %get-tuple-element.31), channel_id=1, source_target_pairs={{0,14},{2,12},{4,10},{6,8},{8,6},{10,4},{12,2},{14,0},{1,15},{3,13... | collective-permute-start | bytes 1191944 | tf_op jit(solution)/shard_map/ppermute | solution.py:176
  52.7 7.5 %collective-permute-done.11.rest_6_ = bf16[1552,128]{1,0:T(8,128)(2,1)S(1)} collective-permute-done((bf16[1552,128]{1,0:T(8,128)(2,1)S(1)}, bf16[1552,128]{1,0:T(8,128)(2,1)S(1)}, u32[]{:S(2)}, u32[]{:S(2)}) %collective-permute-start.11) | collective-permute-done | bytes 397344 | tf_op jit(solution)/shard_map/ppermute | solution.py:176
  60.3 6.6 %score_6.1.prev_ref = f32[8,192]{1,0:T(8,128)S(1)} custom-call(s32[1]{0:T(128)} %bitcast.1.me_ref, f32[8,192]{1,0:T(8,128)S(1)} %broadcast_in_dim.3.prev_ref, bf16[1552,128]{1,0:T(8,128)(2,1)S(1)} %get-tuple-element.22.rest_0_, bf16[1552,128]{1,0:T(8,128)(2,1)S(1)} %collective-permute-done.rest_1_, bf16[1552,128]{1,0:T(8,128)(2,1)S(1)} %collective-permute-done.1.rest_2_, ...), custom_call_target="tpu_custom_call" | custom-call | flops 5435817984 | bytes 4718592 | tf_op jit(solution)/shard_map/score_6/pallas_call | solution.py:201
  66.8 3.0 %score_7.1.prev_ref = f32[8,192]{1,0:T(8,128)S(1)} custom-call(s32[1]{0:T(128)} %bitcast.1.me_ref, f32[8,192]{1,0:T(8,128)S(1)} %score_6.1.prev_ref, bf16[1552,128]{1,0:T(8,128)(2,1)S(1)} %get-tuple-element.22.rest_0_, bf16[1552,128]{1,0:T(8,128)(2,1)S(1)} %collective-permute-done.rest_1_, bf16[1552,128]{1,0:T(8,128)(2,1)S(1)} %collective-permute-done.1.rest_2_, ...), custom_call_target="tpu_custom_call" | custom-call | flops 1962934272 | bytes 5505024 | tf_op jit(solution)/shard_map/score_7/pallas_call | solution.py:201
  69.9 0.6 collective-permute-start.14
  70.4 1.4 %collective-permute-done.14.rest_15_ = bf16[1552,128]{1,0:T(8,128)(2,1)S(1)} collective-permute-done((bf16[1552,128]{1,0:T(8,128)(2,1)S(1)}, bf16[1552,128]{1,0:T(8,128)(2,1)S(1)}, u32[]{:S(2)}, u32[]{:S(2)}) %collective-permute-start.14) | collective-permute-done | bytes 397344 | tf_op jit(solution)/shard_map/ppermute | solution.py:173
  71.8 3.2 %score_8.1 = f32[8,192]{1,0:T(8,128)S(1)} custom-call(s32[1]{0:T(128)} %bitcast.1.me_ref, f32[8,192]{1,0:T(8,128)S(1)} %score_7.1.prev_ref, bf16[1552,128]{1,0:T(8,128)(2,1)S(1)} %get-tuple-element.22.rest_0_, bf16[1552,128]{1,0:T(8,128)(2,1)S(1)} %collective-permute-done.rest_1_, bf16[1552,128]{1,0:T(8,128)(2,1)S(1)} %collective-permute-done.1.rest_2_, ...), custom_call_target="tpu_custom_call" | custom-call | flops 2264924160 | bytes 6291456 | tf_op jit(solution)/shard_map/score_8/pallas_call | solution.py:201
  75.0 23.5 %all_to_all.11 = f32[8,1,192]{2,1,0:T(1,128)S(1)} all-to-all(f32[8,1,192]{2,1,0:T(1,128)S(1)} %copy.4), channel_id=1, replica_groups=mesh['parts'=2,'wide'=8,'narrow'=2] {'wide'}, dimensions={0} | all-to-all | bytes 12288 | tf_op jit(solution)/shard_map/all_to_all | solution.py:215
  98.5 0.3 select.1
  98.8 0.6 reduce
  (24 shorter events, 0.5 us)
Async XLA Ops:
  0.7 1.4 %copy-start = (bf16[768,1024]{1,0:T(8,128)(2,1)S(1)}, bf16[768,1024]{1,0:T(8,128)(2,1)}, u32[]{:S(2)}) copy-start(bf16[768,1024]{1,0:T(8,128)(2,1)} %emb_ref.1) | copy-start | bytes 4718596
  2.1 0.7 copy-start.1
  6.2 12.2 %collective-permute-start = (bf16[1552,128]{1,0:T(8,128)(2,1)S(1)}, bf16[1552,128]{1,0:T(8,128)(2,1)S(1)}, u32[]{:S(2)}, u32[]{:S(2)}) collective-permute-start(bf16[1552,128]{1,0:T(8,128)(2,1)S(1)} %get-tuple-element.23), channel_id=1, source_target_pairs={{0,2},{2,0},{4,6},{6,4},{8,10},{10,8},{12,14},{14,12},{1,3},{3,1},... | collective-permute-start | bytes 1191944 | tf_op jit(solution)/shard_map/ppermute | solution.py:176
  9.2 29.9 %collective-permute-start.3 = (bf16[1552,128]{1,0:T(8,128)(2,1)S(1)}, bf16[1552,128]{1,0:T(8,128)(2,1)S(1)}, u32[]{:S(2)}, u32[]{:S(2)}) collective-permute-start(bf16[1552,128]{1,0:T(8,128)(2,1)S(1)} %get-tuple-element.26), channel_id=1, source_target_pairs={{0,8},{2,10},{4,12},{6,14},{8,0},{10,2},{12,4},{14,6},{1,9},{3,11}... | collective-permute-start | bytes 1191944 | tf_op jit(solution)/shard_map/ppermute | solution.py:176
  11.8 34.5 %collective-permute-start.4 = (bf16[1552,128]{1,0:T(8,128)(2,1)S(1)}, bf16[1552,128]{1,0:T(8,128)(2,1)S(1)}, u32[]{:S(2)}, u32[]{:S(2)}) collective-permute-start(bf16[1552,128]{1,0:T(8,128)(2,1)S(1)} %get-tuple-element.27), channel_id=1, source_target_pairs={{0,10},{2,8},{4,14},{6,12},{8,2},{10,0},{12,6},{14,4},{1,11},{3,9}... | collective-permute-start | bytes 1191944 | tf_op jit(solution)/shard_map/ppermute | solution.py:176
  11.8 34.5 %collective-permute-start.1 = (bf16[1552,128]{1,0:T(8,128)(2,1)S(1)}, bf16[1552,128]{1,0:T(8,128)(2,1)S(1)}, u32[]{:S(2)}, u32[]{:S(2)}) collective-permute-start(bf16[1552,128]{1,0:T(8,128)(2,1)S(1)} %get-tuple-element.24), channel_id=1, source_target_pairs={{0,4},{2,6},{4,0},{6,2},{8,12},{10,14},{12,8},{14,10},{1,5},{3,7},... | collective-permute-start | bytes 1191944 | tf_op jit(solution)/shard_map/ppermute | solution.py:176
  13.7 36.2 %collective-permute-start.2 = (bf16[1552,128]{1,0:T(8,128)(2,1)S(1)}, bf16[1552,128]{1,0:T(8,128)(2,1)S(1)}, u32[]{:S(2)}, u32[]{:S(2)}) collective-permute-start(bf16[1552,128]{1,0:T(8,128)(2,1)S(1)} %get-tuple-element.25), channel_id=1, source_target_pairs={{0,6},{2,4},{4,2},{6,0},{8,14},{10,12},{12,10},{14,8},{1,7},{3,5},... | collective-permute-start | bytes 1191944 | tf_op jit(solution)/shard_map/ppermute | solution.py:176
  18.4 31.7 %collective-permute-start.5 = (bf16[1552,128]{1,0:T(8,128)(2,1)S(1)}, bf16[1552,128]{1,0:T(8,128)(2,1)S(1)}, u32[]{:S(2)}, u32[]{:S(2)}) collective-permute-start(bf16[1552,128]{1,0:T(8,128)(2,1)S(1)} %get-tuple-element.22.rest_0_), channel_id=1, source_target_pairs={{0,1},{1,0},{2,3},{3,2},{4,5},{5,4},{6,7},{7,6},{8,9},{9,8},{10,11... | collective-permute-start | bytes 1191944 | tf_op jit(solution)/shard_map/ppermute | solution.py:173
  39.1 11.3 %collective-permute-start.6 = (bf16[1552,128]{1,0:T(8,128)(2,1)S(1)}, bf16[1552,128]{1,0:T(8,128)(2,1)S(1)}, u32[]{:S(2)}, u32[]{:S(2)}) collective-permute-start(bf16[1552,128]{1,0:T(8,128)(2,1)S(1)} %collective-permute-done.rest_1_), channel_id=1, source_target_pairs={{0,1},{1,0},{2,3},{3,2},{4,5},{5,4},{6,7},{7,6},{8,9},{9,8},{10,11... | collective-permute-start | bytes 1191944 | tf_op jit(solution)/shard_map/ppermute | solution.py:173
  46.3 4.3 %collective-permute-start.7 = (bf16[1552,128]{1,0:T(8,128)(2,1)S(1)}, bf16[1552,128]{1,0:T(8,128)(2,1)S(1)}, u32[]{:S(2)}, u32[]{:S(2)}) collective-permute-start(bf16[1552,128]{1,0:T(8,128)(2,1)S(1)} %collective-permute-done.1.rest_2_), channel_id=1, source_target_pairs={{0,1},{1,0},{2,3},{3,2},{4,5},{5,4},{6,7},{7,6},{8,9},{9,8},{10,11... | collective-permute-start | bytes 1191944 | tf_op jit(solution)/shard_map/ppermute | solution.py:173
  46.3 13.9 %collective-permute-start.11 = (bf16[1552,128]{1,0:T(8,128)(2,1)S(1)}, bf16[1552,128]{1,0:T(8,128)(2,1)S(1)}, u32[]{:S(2)}, u32[]{:S(2)}) collective-permute-start(bf16[1552,128]{1,0:T(8,128)(2,1)S(1)} %get-tuple-element.29), channel_id=1, source_target_pairs={{0,12},{2,14},{4,8},{6,10},{8,4},{10,6},{12,0},{14,2},{1,13},{3,15... | collective-permute-start | bytes 1191944 | tf_op jit(solution)/shard_map/ppermute | solution.py:176
  49.9 10.4 %collective-permute-start.9 = (bf16[1552,128]{1,0:T(8,128)(2,1)S(1)}, bf16[1552,128]{1,0:T(8,128)(2,1)S(1)}, u32[]{:S(2)}, u32[]{:S(2)}) collective-permute-start(bf16[1552,128]{1,0:T(8,128)(2,1)S(1)} %collective-permute-done.3.rest_4_), channel_id=1, source_target_pairs={{0,1},{1,0},{2,3},{3,2},{4,5},{5,4},{6,7},{7,6},{8,9},{9,8},{10,11... | collective-permute-start | bytes 1191944 | tf_op jit(solution)/shard_map/ppermute | solution.py:173
  50.1 10.1 %collective-permute-start.8 = (bf16[1552,128]{1,0:T(8,128)(2,1)S(1)}, bf16[1552,128]{1,0:T(8,128)(2,1)S(1)}, u32[]{:S(2)}, u32[]{:S(2)}) collective-permute-start(bf16[1552,128]{1,0:T(8,128)(2,1)S(1)} %collective-permute-done.2.rest_3_), channel_id=1, source_target_pairs={{0,1},{1,0},{2,3},{3,2},{4,5},{5,4},{6,7},{7,6},{8,9},{9,8},{10,11... | collective-permute-start | bytes 1191944 | tf_op jit(solution)/shard_map/ppermute | solution.py:173
  50.4 9.9 %collective-permute-start.10 = (bf16[1552,128]{1,0:T(8,128)(2,1)S(1)}, bf16[1552,128]{1,0:T(8,128)(2,1)S(1)}, u32[]{:S(2)}, u32[]{:S(2)}) collective-permute-start(bf16[1552,128]{1,0:T(8,128)(2,1)S(1)} %collective-permute-done.4.rest_5_), channel_id=1, source_target_pairs={{0,1},{1,0},{2,3},{3,2},{4,5},{5,4},{6,7},{7,6},{8,9},{9,8},{10,11... | collective-permute-start | bytes 1191944 | tf_op jit(solution)/shard_map/ppermute | solution.py:173
  50.6 19.2 %collective-permute-start.13 = (bf16[1552,128]{1,0:T(8,128)(2,1)S(1)}, bf16[1552,128]{1,0:T(8,128)(2,1)S(1)}, u32[]{:S(2)}, u32[]{:S(2)}) collective-permute-start(bf16[1552,128]{1,0:T(8,128)(2,1)S(1)} %get-tuple-element.31), channel_id=1, source_target_pairs={{0,14},{2,12},{4,10},{6,8},{8,6},{10,4},{12,2},{14,0},{1,15},{3,13... | collective-permute-start | bytes 1191944 | tf_op jit(solution)/shard_map/ppermute | solution.py:176
  60.2 6.6 %collective-permute-start.12 = (bf16[1552,128]{1,0:T(8,128)(2,1)S(1)}, bf16[1552,128]{1,0:T(8,128)(2,1)S(1)}, u32[]{:S(2)}, u32[]{:S(2)}) collective-permute-start(bf16[1552,128]{1,0:T(8,128)(2,1)S(1)} %collective-permute-done.11.rest_6_), channel_id=1, source_target_pairs={{0,1},{1,0},{2,3},{3,2},{4,5},{5,4},{6,7},{7,6},{8,9},{9,8},{10,11... | collective-permute-start | bytes 1191944 | tf_op jit(solution)/shard_map/ppermute | solution.py:173
  69.8 28.7 %copy-start.2 = (s32[768,1]{0,1:T(1,128)S(1)}, s32[768,1]{0,1:T(1,128)}, u32[]{:S(2)}) copy-start(s32[768,1]{0,1:T(1,128)} %param.4) | copy-start | bytes 9220
  69.9 1.9 %collective-permute-start.14 = (bf16[1552,128]{1,0:T(8,128)(2,1)S(1)}, bf16[1552,128]{1,0:T(8,128)(2,1)S(1)}, u32[]{:S(2)}, u32[]{:S(2)}) collective-permute-start(bf16[1552,128]{1,0:T(8,128)(2,1)S(1)} %collective-permute-done.13.rest_7_), channel_id=1, source_target_pairs={{0,1},{1,0},{2,3},{3,2},{4,5},{5,4},{6,7},{7,6},{8,9},{9,8},{10,11... | collective-permute-start | bytes 1191944 | tf_op jit(solution)/shard_map/ppermute | solution.py:173

commit v3 on v2

v3 whole, which is shorter than its diff:
```python
import functools

import jax
import jax.numpy as jnp
from jax import lax
from jax.experimental import pallas as pl
from jax.experimental.pallas import tpu as pltpu
from jax.sharding import PartitionSpec as P

EMPTY = 2.0**22
VMEM_LIMIT = 40 * 1024 * 1024
LANES = 128
CHUNKS = 4
SPLIT = 1024
TAIL = 16


def _nt(a, b):
    return lax.dot_general(a, b, (((1,), (1,)), ((), ())), preferred_element_type=jnp.float32)


def _as_bf16(mask):
    return mask.astype(jnp.float32).astype(jnp.bfloat16)


def _spans(slots):
    return -(-slots // LANES)


def _write_block(out, pick, unit, high, low, slots):
    block = jnp.dot(pick, unit, preferred_element_type=jnp.float32).astype(jnp.bfloat16)
    pieces = block.shape[1] // LANES
    for k in range(pieces):
        out[k * slots : (k + 1) * slots, :] = block[:, k * LANES : (k + 1) * LANES]
    spans = _spans(slots)
    lines = [part[:, i * LANES : (i + 1) * LANES] for part in (high, low) for i in range(spans)]
    lines.append(jnp.zeros((TAIL - 2 * spans, LANES), jnp.float32))
    out[pieces * slots :, :] = jnp.concatenate(lines, axis=0).astype(jnp.bfloat16)


def _block(ref, slots):
    return jnp.concatenate([ref[k * slots : (k + 1) * slots, :] for k in range(ref.shape[0] // slots)], axis=1)


def _ranks(ref, slots):
    tail = ref[ref.shape[0] - TAIL :, :].astype(jnp.float32)
    spans = _spans(slots)
    value = tail[:spans] * 256.0 + tail[spans : 2 * spans]
    return jnp.concatenate([value[i : i + 1] for i in range(spans)], axis=1)


def _pick(lab, pos, dest, low, high):
    key = jnp.where(lab == dest, pos, -1)
    return _as_bf16(lax.broadcasted_iota(jnp.int32, (high - low, lab.shape[1]), 0) + low == key)


def _pack_first(pieces, groups, slots, me_ref, emb_hbm, lab_hbm, prio_hbm, *rest):
    unit_ref, pos_ref, ranks_ref, *outs = rest[:-5]
    emb_ref, lab_ref, prio_ref, sems, word_sems = rest[-5:]
    rows = emb_ref.shape[0]
    words = [
        pltpu.make_async_copy(lab_hbm, lab_ref, word_sems.at[0]),
        pltpu.make_async_copy(prio_hbm, prio_ref, word_sems.at[1]),
    ]
    chunk = rows // CHUNKS
    spans = [pl.ds(i * chunk, chunk) for i in range(CHUNKS)]
    copies = [pltpu.make_async_copy(emb_hbm.at[span], emb_ref.at[span], sems.at[i]) for i, span in enumerate(spans)]
    for copy in words + copies:
        copy.start()
    for copy in words:
        copy.wait()
    lab = lab_ref[...]
    away = jnp.bitwise_xor(lax.broadcasted_iota(jnp.int32, (groups, rows), 0), me_ref[0])
    onehot = (away == lab).astype(jnp.float32)
    before = lax.broadcasted_iota(jnp.int32, (rows, rows), 0) < lax.broadcasted_iota(jnp.int32, (rows, rows), 1)
    earlier = jnp.dot(onehot.astype(jnp.bfloat16), _as_bf16(before), preferred_element_type=jnp.float32)
    pos = jnp.sum(onehot * earlier, axis=0, keepdims=True).astype(jnp.int32)
    pos_ref[...] = pos
    prio = jnp.concatenate([prio_ref[i : i + 1, :] for i in range(rows // LANES)], axis=1)
    high = (prio >> 8).astype(jnp.float32)
    low = (prio & 255).astype(jnp.float32)
    parts = jnp.concatenate([onehot * high, onehot * low, onehot], axis=0).astype(jnp.bfloat16)
    places = lax.broadcasted_iota(jnp.int32, (_spans(slots) * LANES, rows), 0)
    placed = _nt(parts, _as_bf16(places == pos))
    high = jnp.where(placed[2 * groups :] > 0.5, placed[:groups], EMPTY)
    low = placed[groups : 2 * groups]
    ranks_ref[...] = jnp.concatenate([high, low], axis=0)
    for copy, span in zip(copies, spans):
        copy.wait()
        emb = emb_ref[span, :].astype(jnp.float32)
        scale = lax.rsqrt(jnp.sum(emb * emb, axis=1, keepdims=True) + 1e-06)
        unit_ref[span, :] = (emb * scale).astype(jnp.bfloat16)
    unit = unit_ref[...]
    for (r, first, last), out in zip(pieces, outs):
        pick = _pick(lab, pos, jnp.bitwise_xor(me_ref[0], r), first, last)
        _write_block(out, pick, unit, high[r : r + 1, first:], low[r : r + 1, first:], last - first)


def _pack_rest(pieces, groups, me_ref, unit_ref, lab_ref, pos_ref, ranks_ref, after_ref, *outs):
    for (r, first, last), out in zip(pieces, outs):
        pick = _pick(lab_ref[...], pos_ref[...], jnp.bitwise_xor(me_ref[0], r), first, last)
        high = ranks_ref[r : r + 1, first:]
        low = ranks_ref[groups + r : groups + r + 1, first:]
        _write_block(out, pick, unit_ref[...], high, low, last - first)


def _score(pieces, n_old, final, me_ref, prev_ref, *rest):
    n = len(pieces)
    own, sib, out_ref = rest[:n], rest[n : 2 * n], rest[2 * n]
    sizes = [last - first for _, first, last in pieces]
    refs = [ref for j in range(n) for ref in (own[j], sib[j])]
    ranks = [_ranks(ref, sizes[i // 2]) for i, ref in enumerate(refs)]
    lanes = max(rank.shape[1] for rank in ranks)
    padded = [jnp.concatenate([rank] * (lanes // rank.shape[1]), axis=1) for rank in ranks]
    columns = jnp.transpose(jnp.concatenate(padded, axis=0))

    def best_of(keys, queries):
        sim = _nt(
            jnp.concatenate([_block(refs[i], sizes[i // 2]) for i in keys], axis=0),
            jnp.concatenate([_block(own[j], sizes[j]) for j in queries], axis=0),
        )
        key_ranks = jnp.concatenate([columns[: sizes[i // 2], i : i + 1] for i in keys], axis=0)
        query_ranks = jnp.concatenate([ranks[2 * j][:, : sizes[j]] for j in queries], axis=1)
        best = jnp.max(jnp.where(key_ranks < query_ranks, sim, -1.0), axis=0, keepdims=True)
        starts = [sum(sizes[j] for j in queries[:i]) for i in range(len(queries) + 1)]
        return [best[:, starts[i] : starts[i + 1]] for i in range(len(queries))]

    rows = []
    if n_old:
        old = best_of(range(2 * n_old, 2 * n), range(n_old))
        for (r, first, last), row in zip(pieces, old):
            rows.append(jnp.maximum(row, prev_ref[r : r + 1, first:last]))
    rows += best_of(range(2 * n), range(n_old, n))
    if not final:
        for (r, first, last), row in zip(pieces, rows):
            out_ref[r : r + 1, first:last] = row
    else:
        for r in range(out_ref.shape[0]):
            whole = [row for piece, row in sorted(zip(pieces, rows), key=lambda pair: pair[0]) if piece[0] == r]
            out_ref[pl.ds(jnp.bitwise_xor(me_ref[0], r), 1), :] = jnp.concatenate(whole, axis=1)


def _select(groups, lab_ref, pos_ref, got_ref, out_ref):
    slots = got_ref.shape[1]
    rows = lab_ref.shape[1]
    got = got_ref[...]
    a = got.astype(jnp.bfloat16)
    rest = got - a.astype(jnp.float32)
    b = rest.astype(jnp.bfloat16)
    c = (rest - b.astype(jnp.float32)).astype(jnp.bfloat16)
    pick = _as_bf16(lax.broadcasted_iota(jnp.int32, (slots, rows), 0) == pos_ref[...])
    value = jnp.dot(a, pick, preferred_element_type=jnp.float32)
    value += jnp.dot(b, pick, preferred_element_type=jnp.float32)
    value += jnp.dot(c, pick, preferred_element_type=jnp.float32)
    mine = lax.broadcasted_iota(jnp.int32, (groups, rows), 0) == lab_ref[...]
    out_ref[...] = jnp.sum(jnp.where(mine, value, 0.0), axis=0)


ANY = pl.BlockSpec(memory_space=pl.ANY)
SMEM = pl.BlockSpec(memory_space=pltpu.SMEM)
VMEM = pl.BlockSpec(memory_space=pltpu.VMEM)
HBM = pl.BlockSpec(memory_space=pltpu.HBM)


def local(embeddings, labels, priority):
    rows, width = embeddings.shape
    groups = lax.axis_size("wide")
    slots = 2 * rows // groups
    half = groups // 2
    me = lax.axis_index("wide").astype(jnp.int32).reshape(1)
    lab = labels.reshape(1, rows)
    def block(piece):
        return jax.ShapeDtypeStruct((width // LANES * (piece[2] - piece[1]) + TAIL, LANES), jnp.bfloat16)

    quarter = max(1, half // 4)
    near = [(r, 0, slots) for r in range(half)]
    far = [(r, 0, slots) for r in range(half, groups)]
    if SPLIT < slots:
        far[-1:] = [(groups - 1, 0, SPLIT), (groups - 1, SPLIT, slots)]
    params = pltpu.CompilerParams(vmem_limit_bytes=VMEM_LIMIT)

    def in_hbm(x):
        return pltpu.with_memory_space_constraint(x, pltpu.HBM)

    unit, pos, ranks, *far_blocks = pl.pallas_call(
        functools.partial(_pack_first, far, groups, slots),
        out_shape=[
            jax.ShapeDtypeStruct((rows, width), jnp.bfloat16),
            jax.ShapeDtypeStruct((1, rows), jnp.int32),
            jax.ShapeDtypeStruct((2 * groups, _spans(slots) * LANES), jnp.float32),
        ]
        + [block(piece) for piece in far],
        in_specs=[SMEM, HBM, HBM, HBM],
        out_specs=[VMEM] * (3 + len(far)),
        scratch_shapes=[
            pltpu.VMEM((rows, width), jnp.bfloat16),
            pltpu.VMEM((1, rows), jnp.int32),
            pltpu.VMEM((rows // LANES, LANES), jnp.int32),
            pltpu.SemaphoreType.DMA((CHUNKS,)),
            pltpu.SemaphoreType.DMA((2,)),
        ],
        compiler_params=params,
        name="pack_far",
    )(me, in_hbm(embeddings), in_hbm(lab), in_hbm(priority.reshape(rows // LANES, LANES)))
    def swap(x):
        return lax.ppermute(x, "narrow", [(0, 1), (1, 0)])

    def send(x, r):
        return lax.ppermute(x, "wide", [(s, s ^ r) for s in range(groups)])

    def after(x, *others):
        return lax.optimization_barrier((x, *others))[0]

    near_blocks = pl.pallas_call(
        functools.partial(_pack_rest, near, groups),
        out_shape=[block(piece) for piece in near],
        in_specs=[SMEM] + [VMEM] * 4 + [ANY],
        out_specs=[VMEM] * len(near),
        compiler_params=params,
        cost_estimate=pl.CostEstimate(flops=10000000000, bytes_accessed=1, transcendentals=0),
        name="pack_near",
    )(me, unit, lab, pos, ranks, ranks)

    own = {}
    for i, piece in enumerate(far):
        out = far_blocks[i]
        if i >= 2 * quarter:
            out = after(out, own[far[i - 2 * quarter]])
        own[piece] = send(out, piece[0])
    for piece, out in zip(near, near_blocks):
        own[piece] = send(out, piece[0]) if piece[0] else out

    steps = [
        near[:1] + far[:quarter],
        far[quarter : 2 * quarter] + near[1:],
        far[2 * quarter : 3 * quarter],
        far[3 * quarter : 4 * quarter],
        far[4 * quarter :],
    ]
    steps = [step for step in steps if step]
    order, best, sib = [], jnp.zeros((groups, slots), jnp.float32), {}
    for number, step in enumerate(steps):
        for piece in step:
            sib[piece] = swap(after(own[piece], best) if number >= 3 else own[piece])
        n_old = len(order)
        order = order + step
        old, new = (sum(piece[2] - piece[1] for piece in part) for part in (order[:n_old], step))
        best = pl.pallas_call(
            functools.partial(_score, order, n_old, number == len(steps) - 1),
            out_shape=jax.ShapeDtypeStruct((groups, slots), jnp.float32),
            in_specs=[SMEM] + [VMEM] * (1 + 2 * len(order)),
            out_specs=VMEM,
            compiler_params=params,
            cost_estimate=pl.CostEstimate(
                flops=10000000000,
                bytes_accessed=4 * (old + new) * width,
                transcendentals=0,
            ),
            name=f"score_{number}",
        )(me, best, *[own[piece] for piece in order], *[sib[piece] for piece in order])

    returned = lax.all_to_all(best, "wide", split_axis=0, concat_axis=0, tiled=True)
    return pl.pallas_call(
        functools.partial(_select, groups),
        out_shape=jax.ShapeDtypeStruct((rows,), jnp.float32),
        in_specs=[VMEM, VMEM, VMEM],
        out_specs=VMEM,
        compiler_params=params,
        name="select",
    )(lab, pos, returned)


def solution(mesh):
    in_specs = (
        P(("parts", "wide", "narrow"), None),
        P(("parts", "wide", "narrow"), None),
        P(("parts", "wide", "narrow")),
    )
    out_specs = P(("parts", "wide", "narrow"))
    return jax.shard_map(local, mesh=mesh, in_specs=in_specs, out_specs=out_specs, check_vma=False)
```

time: 99.6 us -> 95.9 us (0.963)
  waiting for transfers between devices: 40.1 us -> 35.8 us
  local copies, waits for them, and re-layouts: 2.8 us -> 0.02 us
  Pallas kernels: 16.4 us -> 19 us
  starting transfers between devices: 15.8 us -> 17.4 us
    ppermute x7, waiting for transfers between devices: 38.7 us -> 34.3 us  [send(): return lax.ppermute(x, 'wide', [(s, s ^ r) for s in range(groups)])]
    unnamed x7 -> x3, local copies, waits for them, and re-layouts: 2.1 us -> 0.01 us
    pallas_call x1, Pallas kernels: 1.98 us -> 3.6 us  [local(): pl.pallas_call(functools.partial(_pack_first, far, groups, slots), out_sh...]
    ppermute x7, starting transfers between devices: 14.5 us -> 15.8 us  [send(): return lax.ppermute(x, 'wide', [(s, s ^ r) for s in range(groups)])]
    pallas_call x4 -> x5, Pallas kernels: 14.2 us -> 14.5 us  [the longest x4 13.1 us: local(): pl.pallas_call(functools.partial(_score, order, n_old, number == len(step...]
  transfers between devices with their start and end apart: 15 -> 15, of which waited for: 5 -> 5; matrix products, arithmetic and copies ran while one was open for 0% -> 0% of each run, Pallas kernels for 10% -> 12%
where the time goes in v3:
time: 95.9 us; the launch traced here: 95.7 us
  waiting for transfers between devices  35.8 us (37%)
  blocking collectives  23.4 us (24%)
  Pallas kernels  19 us (20%)
  starting transfers between devices  17.4 us (18%)
    ppermute x7, waiting for transfers between devices, send(): return lax.ppermute(x, 'wide', [(s, s ^ r) for s in range(groups)])  34.3 us
    all_to_all x1, blocking collectives, local(): lax.all_to_all(best, 'wide', split_axis=0, concat_axis=0, tiled=True)  23.4 us
    ppermute x7, starting transfers between devices, send(): return lax.ppermute(x, 'wide', [(s, s ^ r) for s in range(groups)])  15.8 us
    pallas_call x4, Pallas kernels, local(): pl.pallas_call(functools.partial(_score, order, n_old, number == len(step...  13.1 us
    pallas_call x1, Pallas kernels, local(): pl.pallas_call(functools.partial(_pack_first, far, groups, slots), out_sh...  3.6 us
  transfers between devices with their start and end apart: 15, of which 5 were waited for; matrix products, arithmetic and copies ran while one was open for 0% of the time, Pallas kernels for 12%

profile of v3, /device:TPU:0, one launch (start us, length us, event | category | flops | bytes accessed | tf_op | source)
XLA Modules:
  0.0 95.7 jit_solution(11101838870332868733)
XLA Ops:
  0.0 3.6 %pack_far.1 = (bf16[768,1024]{1,0:T(8,128)(2,1)S(1)}, s32[1,768]{1,0:T(1,128)S(1)}, f32[16,256]{1,0:T(8,128)S(1)}, bf16[1552,128]{1,0:T(8,128)(2,1)S(1)}, bf16[1...) custom-call(s32[1]{0:T(128)} %bitcast.1.me_ref, bf16[768,1024]{1,0:T(8,128)(2,1)} %emb_hbm.1, ...), custom_call_target="tpu_custom_call" | custom-call | tf_op jit(solution)/shard_map/pack_far/pallas_call | solution.py:185
  3.6 4.1 %collective-permute-start = (bf16[1552,128]{1,0:T(8,128)(2,1)S(1)}, bf16[1552,128]{1,0:T(8,128)(2,1)S(1)}, u32[]{:S(2)}, u32[]{:S(2)}) collective-permute-start(bf16[1552,128]{1,0:T(8,128)(2,1)S(1)} %get-tuple-element.23), channel_id=1, source_target_pairs={{0,8},{2,10},{4,12},{6,14},{8,0},{10,2},{12,4},{14,6},{1,9},{3,11}... | collective-permute-start | bytes 1191944 | tf_op jit(solution)/shard_map/ppermute | solution.py:209
  7.7 1.3 %collective-permute-start.3 = (bf16[1552,128]{1,0:T(8,128)(2,1)S(1)}, bf16[1552,128]{1,0:T(8,128)(2,1)S(1)}, u32[]{:S(2)}, u32[]{:S(2)}) collective-permute-start(bf16[1552,128]{1,0:T(8,128)(2,1)S(1)} %get-tuple-element.24), channel_id=1, source_target_pairs={{0,10},{2,8},{4,14},{6,12},{8,2},{10,0},{12,6},{14,4},{1,11},{3,9}... | collective-permute-start | bytes 1191944 | tf_op jit(solution)/shard_map/ppermute | solution.py:209
  9.0 1.4 %pack_near.1 = (bf16[1552,128]{1,0:T(8,128)(2,1)S(1)}, bf16[1552,128]{1,0:T(8,128)(2,1)S(1)}, bf16[1552,128]{1,0:T(8,128)(2,1)S(1)}, bf16[1552,128]{1,0:T(8,128)(2,1)S(1)}) custom-call(s32[1]{0:T(128)} %bitcast.1.me_ref, bf16[768,1024]{1,0:T(8,128)(2,1)S(1)} %get-tuple-element.20.unit_ref, s32[1,768]{1,0:T(1,128)S(1)} %bitcast.9, ...), custom_call_target="tpu_custom_call" | custom-call | flops 10000000000 | bytes 1 | tf_op jit(solution)/shard_map/pack_near/pallas_call | solution.py:214
  10.4 0.3 collective-permute-start.4
  10.7 1.8 %collective-permute-start.5 = (bf16[1552,128]{1,0:T(8,128)(2,1)S(1)}, bf16[1552,128]{1,0:T(8,128)(2,1)S(1)}, u32[]{:S(2)}, u32[]{:S(2)}) collective-permute-start(bf16[1552,128]{1,0:T(8,128)(2,1)S(1)} %get-tuple-element.26), channel_id=1, source_target_pairs={{0,4},{2,6},{4,0},{6,2},{8,12},{10,14},{12,8},{14,10},{1,5},{3,7},... | collective-permute-start | bytes 1191944 | tf_op jit(solution)/shard_map/ppermute | solution.py:209
  12.5 1.4 %collective-permute-start.6 = (bf16[1552,128]{1,0:T(8,128)(2,1)S(1)}, bf16[1552,128]{1,0:T(8,128)(2,1)S(1)}, u32[]{:S(2)}, u32[]{:S(2)}) collective-permute-start(bf16[1552,128]{1,0:T(8,128)(2,1)S(1)} %get-tuple-element.27), channel_id=1, source_target_pairs={{0,6},{2,4},{4,2},{6,0},{8,14},{10,12},{12,10},{14,8},{1,7},{3,5},... | collective-permute-start | bytes 1191944 | tf_op jit(solution)/shard_map/ppermute | solution.py:209
  14.0 20.9 %collective-permute-done.rest_1_ = bf16[1552,128]{1,0:T(8,128)(2,1)S(1)} collective-permute-done((bf16[1552,128]{1,0:T(8,128)(2,1)S(1)}, bf16[1552,128]{1,0:T(8,128)(2,1)S(1)}, u32[]{:S(2)}, u32[]{:S(2)}) %collective-permute-start) | collective-permute-done | bytes 397344 | tf_op jit(solution)/shard_map/ppermute | solution.py:209
  34.9 8.7 %collective-permute-done.3.rest_2_ = bf16[1552,128]{1,0:T(8,128)(2,1)S(1)} collective-permute-done((bf16[1552,128]{1,0:T(8,128)(2,1)S(1)}, bf16[1552,128]{1,0:T(8,128)(2,1)S(1)}, u32[]{:S(2)}, u32[]{:S(2)}) %collective-permute-start.3) | collective-permute-done | bytes 397344 | tf_op jit(solution)/shard_map/ppermute | solution.py:209
  43.6 3.5 %collective-permute-start.11 = (bf16[1552,128]{1,0:T(8,128)(2,1)S(1)}, bf16[1552,128]{1,0:T(8,128)(2,1)S(1)}, u32[]{:S(2)}, u32[]{:S(2)}) collective-permute-start(bf16[1552,128]{1,0:T(8,128)(2,1)S(1)} %get-tuple-element.29), channel_id=1, source_target_pairs={{0,12},{2,14},{4,8},{6,10},{8,4},{10,6},{12,0},{14,2},{1,13},{3,15... | collective-permute-start | bytes 1191944 | tf_op jit(solution)/shard_map/ppermute | solution.py:209
  47.1 0.2 collective-permute-start.7
  47.3 0.3 collective-permute-start.8
  47.6 0.2 collective-permute-start.9
  47.8 0.3 collective-permute-start.10
  48.1 1.1 %score_0.1.prev_ref = f32[8,192]{1,0:T(8,128)S(1)} custom-call(s32[1]{0:T(128)} %bitcast.1.me_ref, f32[8,192]{1,0:T(8,128)S(1)} %broadcast_in_dim.3.prev_ref, bf16[1552,128]{1,0:T(8,128)(2,1)S(1)} %get-tuple-element.22.rest_0_, bf16[1552,128]{1,0:T(8,128)(2,1)S(1)} %collective-permute-done.rest_1_, ...), custom_call_target="tpu_custom_call" | custom-call | flops 10000000000 | bytes 1572864 | tf_op jit(solution)/shard_map/score_0/pallas_call | solution.py:248
  49.3 3.4 %collective-permute-start.13 = (bf16[1552,128]{1,0:T(8,128)(2,1)S(1)}, bf16[1552,128]{1,0:T(8,128)(2,1)S(1)}, u32[]{:S(2)}, u32[]{:S(2)}) collective-permute-start(bf16[1552,128]{1,0:T(8,128)(2,1)S(1)} %get-tuple-element.31), channel_id=1, source_target_pairs={{0,14},{2,12},{4,10},{6,8},{8,6},{10,4},{12,2},{14,0},{1,15},{3,13... | collective-permute-start | bytes 1191944 | tf_op jit(solution)/shard_map/ppermute | solution.py:209
  52.8 4.7 %collective-permute-done.11.rest_6_ = bf16[1552,128]{1,0:T(8,128)(2,1)S(1)} collective-permute-done((bf16[1552,128]{1,0:T(8,128)(2,1)S(1)}, bf16[1552,128]{1,0:T(8,128)(2,1)S(1)}, u32[]{:S(2)}, u32[]{:S(2)}) %collective-permute-start.11) | collective-permute-done | bytes 397344 | tf_op jit(solution)/shard_map/ppermute | solution.py:209
  57.5 5.8 %score_1.1.prev_ref = f32[8,192]{1,0:T(8,128)S(1)} custom-call(s32[1]{0:T(128)} %bitcast.1.me_ref, f32[8,192]{1,0:T(8,128)S(1)} %score_0.1.prev_ref, bf16[1552,128]{1,0:T(8,128)(2,1)S(1)} %get-tuple-element.22.rest_0_, bf16[1552,128]{1,0:T(8,128)(2,1)S(1)} %collective-permute-done.rest_1_, bf16[1552,128]{1,0:T(8,128)(2,1)S(1)} %collective-permute-done.3.rest_2_, ...), custom_call_target="tpu_custom_call" | custom-call | flops 10000000000 | bytes 4718592 | tf_op jit(solution)/shard_map/score_1/pallas_call | solution.py:248
  63.3 3.1 %score_2.1.prev_ref = f32[8,192]{1,0:T(8,128)S(1)} custom-call(s32[1]{0:T(128)} %bitcast.1.me_ref, f32[8,192]{1,0:T(8,128)S(1)} %score_1.1.prev_ref, bf16[1552,128]{1,0:T(8,128)(2,1)S(1)} %get-tuple-element.22.rest_0_, bf16[1552,128]{1,0:T(8,128)(2,1)S(1)} %collective-permute-done.rest_1_, bf16[1552,128]{1,0:T(8,128)(2,1)S(1)} %collective-permute-done.3.rest_2_, ...), custom_call_target="tpu_custom_call" | custom-call | flops 10000000000 | bytes 5505024 | tf_op jit(solution)/shard_map/score_2/pallas_call | solution.py:248
  66.3 0.6 collective-permute-start.14
  66.9 1.4 %collective-permute-done.14.rest_15_ = bf16[1552,128]{1,0:T(8,128)(2,1)S(1)} collective-permute-done((bf16[1552,128]{1,0:T(8,128)(2,1)S(1)}, bf16[1552,128]{1,0:T(8,128)(2,1)S(1)}, u32[]{:S(2)}, u32[]{:S(2)}) %collective-permute-start.14) | collective-permute-done | bytes 397344 | tf_op jit(solution)/shard_map/ppermute | solution.py:206
  68.3 3.2 %score_3.1 = f32[8,192]{1,0:T(8,128)S(1)} custom-call(s32[1]{0:T(128)} %bitcast.1.me_ref, f32[8,192]{1,0:T(8,128)S(1)} %score_2.1.prev_ref, bf16[1552,128]{1,0:T(8,128)(2,1)S(1)} %get-tuple-element.22.rest_0_, bf16[1552,128]{1,0:T(8,128)(2,1)S(1)} %collective-permute-done.rest_1_, bf16[1552,128]{1,0:T(8,128)(2,1)S(1)} %collective-permute-done.3.rest_2_, ...), custom_call_target="tpu_custom_call" | custom-call | flops 10000000000 | bytes 6291456 | tf_op jit(solution)/shard_map/score_3/pallas_call | solution.py:248
  71.5 23.4 %all_to_all.11 = f32[8,1,192]{2,1,0:T(1,128)S(1)} all-to-all(f32[8,1,192]{2,1,0:T(1,128)S(1)} %copy.4), channel_id=1, replica_groups=mesh['parts'=2,'wide'=8,'narrow'=2] {'wide'}, dimensions={0} | all-to-all | bytes 12288 | tf_op jit(solution)/shard_map/all_to_all | solution.py:262
  94.9 0.8 select.1
  (19 shorter events, 0.2 us)
Async XLA Ops:
  0.0 9.0 %copy-start = (s32[768,1]{0,1:T(1,128)S(1)}, s32[768,1]{0,1:T(1,128)}, u32[]{:S(2)}) copy-start(s32[768,1]{0,1:T(1,128)} %param.4) | copy-start | bytes 9220
  3.6 31.2 %collective-permute-start = (bf16[1552,128]{1,0:T(8,128)(2,1)S(1)}, bf16[1552,128]{1,0:T(8,128)(2,1)S(1)}, u32[]{:S(2)}, u32[]{:S(2)}) collective-permute-start(bf16[1552,128]{1,0:T(8,128)(2,1)S(1)} %get-tuple-element.23), channel_id=1, source_target_pairs={{0,8},{2,10},{4,12},{6,14},{8,0},{10,2},{12,4},{14,6},{1,9},{3,11}... | collective-permute-start | bytes 1191944 | tf_op jit(solution)/shard_map/ppermute | solution.py:209
  7.7 35.9 %collective-permute-start.3 = (bf16[1552,128]{1,0:T(8,128)(2,1)S(1)}, bf16[1552,128]{1,0:T(8,128)(2,1)S(1)}, u32[]{:S(2)}, u32[]{:S(2)}) collective-permute-start(bf16[1552,128]{1,0:T(8,128)(2,1)S(1)} %get-tuple-element.24), channel_id=1, source_target_pairs={{0,10},{2,8},{4,14},{6,12},{8,2},{10,0},{12,6},{14,4},{1,11},{3,9}... | collective-permute-start | bytes 1191944 | tf_op jit(solution)/shard_map/ppermute | solution.py:209
  10.4 33.1 %collective-permute-start.4 = (bf16[1552,128]{1,0:T(8,128)(2,1)S(1)}, bf16[1552,128]{1,0:T(8,128)(2,1)S(1)}, u32[]{:S(2)}, u32[]{:S(2)}) collective-permute-start(bf16[1552,128]{1,0:T(8,128)(2,1)S(1)} %get-tuple-element.25), channel_id=1, source_target_pairs={{0,2},{2,0},{4,6},{6,4},{8,10},{10,8},{12,14},{14,12},{1,3},{3,1},... | collective-permute-start | bytes 1191944 | tf_op jit(solution)/shard_map/ppermute | solution.py:209
  10.7 36.3 %collective-permute-start.5 = (bf16[1552,128]{1,0:T(8,128)(2,1)S(1)}, bf16[1552,128]{1,0:T(8,128)(2,1)S(1)}, u32[]{:S(2)}, u32[]{:S(2)}) collective-permute-start(bf16[1552,128]{1,0:T(8,128)(2,1)S(1)} %get-tuple-element.26), channel_id=1, source_target_pairs={{0,4},{2,6},{4,0},{6,2},{8,12},{10,14},{12,8},{14,10},{1,5},{3,7},... | collective-permute-start | bytes 1191944 | tf_op jit(solution)/shard_map/ppermute | solution.py:209
  12.5 34.7 %collective-permute-start.6 = (bf16[1552,128]{1,0:T(8,128)(2,1)S(1)}, bf16[1552,128]{1,0:T(8,128)(2,1)S(1)}, u32[]{:S(2)}, u32[]{:S(2)}) collective-permute-start(bf16[1552,128]{1,0:T(8,128)(2,1)S(1)} %get-tuple-element.27), channel_id=1, source_target_pairs={{0,6},{2,4},{4,2},{6,0},{8,14},{10,12},{12,10},{14,8},{1,7},{3,5},... | collective-permute-start | bytes 1191944 | tf_op jit(solution)/shard_map/ppermute | solution.py:209
  34.9 12.7 %collective-permute-start.1 = (bf16[1552,128]{1,0:T(8,128)(2,1)S(1)}, bf16[1552,128]{1,0:T(8,128)(2,1)S(1)}, u32[]{:S(2)}, u32[]{:S(2)}) collective-permute-start(bf16[1552,128]{1,0:T(8,128)(2,1)S(1)} %get-tuple-element.22.rest_0_), channel_id=1, source_target_pairs={{0,1},{1,0},{2,3},{3,2},{4,5},{5,4},{6,7},{7,6},{8,9},{9,8},{10,11... | collective-permute-start | bytes 1191944 | tf_op jit(solution)/shard_map/ppermute | solution.py:206
  43.6 4.2 %collective-permute-start.2 = (bf16[1552,128]{1,0:T(8,128)(2,1)S(1)}, bf16[1552,128]{1,0:T(8,128)(2,1)S(1)}, u32[]{:S(2)}, u32[]{:S(2)}) collective-permute-start(bf16[1552,128]{1,0:T(8,128)(2,1)S(1)} %collective-permute-done.rest_1_), channel_id=1, source_target_pairs={{0,1},{1,0},{2,3},{3,2},{4,5},{5,4},{6,7},{7,6},{8,9},{9,8},{10,11... | collective-permute-start | bytes 1191944 | tf_op jit(solution)/shard_map/ppermute | solution.py:206
  43.6 13.9 %collective-permute-start.11 = (bf16[1552,128]{1,0:T(8,128)(2,1)S(1)}, bf16[1552,128]{1,0:T(8,128)(2,1)S(1)}, u32[]{:S(2)}, u32[]{:S(2)}) collective-permute-start(bf16[1552,128]{1,0:T(8,128)(2,1)S(1)} %get-tuple-element.29), channel_id=1, source_target_pairs={{0,12},{2,14},{4,8},{6,10},{8,4},{10,6},{12,0},{14,2},{1,13},{3,15... | collective-permute-start | bytes 1191944 | tf_op jit(solution)/shard_map/ppermute | solution.py:209
  47.1 10.4 %collective-permute-start.7 = (bf16[1552,128]{1,0:T(8,128)(2,1)S(1)}, bf16[1552,128]{1,0:T(8,128)(2,1)S(1)}, u32[]{:S(2)}, u32[]{:S(2)}) collective-permute-start(bf16[1552,128]{1,0:T(8,128)(2,1)S(1)} %collective-permute-done.3.rest_2_), channel_id=1, source_target_pairs={{0,1},{1,0},{2,3},{3,2},{4,5},{5,4},{6,7},{7,6},{8,9},{9,8},{10,11... | collective-permute-start | bytes 1191944 | tf_op jit(solution)/shard_map/ppermute | solution.py:206
  47.3 2.1 %collective-permute-start.8 = (bf16[1552,128]{1,0:T(8,128)(2,1)S(1)}, bf16[1552,128]{1,0:T(8,128)(2,1)S(1)}, u32[]{:S(2)}, u32[]{:S(2)}) collective-permute-start(bf16[1552,128]{1,0:T(8,128)(2,1)S(1)} %collective-permute-done.4.rest_3_), channel_id=1, source_target_pairs={{0,1},{1,0},{2,3},{3,2},{4,5},{5,4},{6,7},{7,6},{8,9},{9,8},{10,11... | collective-permute-start | bytes 1191944 | tf_op jit(solution)/shard_map/ppermute | solution.py:206
  47.6 9.9 %collective-permute-start.9 = (bf16[1552,128]{1,0:T(8,128)(2,1)S(1)}, bf16[1552,128]{1,0:T(8,128)(2,1)S(1)}, u32[]{:S(2)}, u32[]{:S(2)}) collective-permute-start(bf16[1552,128]{1,0:T(8,128)(2,1)S(1)} %collective-permute-done.5.rest_4_), channel_id=1, source_target_pairs={{0,1},{1,0},{2,3},{3,2},{4,5},{5,4},{6,7},{7,6},{8,9},{9,8},{10,11... | collective-permute-start | bytes 1191944 | tf_op jit(solution)/shard_map/ppermute | solution.py:206
  47.8 9.7 %collective-permute-start.10 = (bf16[1552,128]{1,0:T(8,128)(2,1)S(1)}, bf16[1552,128]{1,0:T(8,128)(2,1)S(1)}, u32[]{:S(2)}, u32[]{:S(2)}) collective-permute-start(bf16[1552,128]{1,0:T(8,128)(2,1)S(1)} %collective-permute-done.6.rest_5_), channel_id=1, source_target_pairs={{0,1},{1,0},{2,3},{3,2},{4,5},{5,4},{6,7},{7,6},{8,9},{9,8},{10,11... | collective-permute-start | bytes 1191944 | tf_op jit(solution)/shard_map/ppermute | solution.py:206
  49.3 17.0 %collective-permute-start.13 = (bf16[1552,128]{1,0:T(8,128)(2,1)S(1)}, bf16[1552,128]{1,0:T(8,128)(2,1)S(1)}, u32[]{:S(2)}, u32[]{:S(2)}) collective-permute-start(bf16[1552,128]{1,0:T(8,128)(2,1)S(1)} %get-tuple-element.31), channel_id=1, source_target_pairs={{0,14},{2,12},{4,10},{6,8},{8,6},{10,4},{12,2},{14,0},{1,15},{3,13... | collective-permute-start | bytes 1191944 | tf_op jit(solution)/shard_map/ppermute | solution.py:209
  57.5 5.8 %collective-permute-start.12 = (bf16[1552,128]{1,0:T(8,128)(2,1)S(1)}, bf16[1552,128]{1,0:T(8,128)(2,1)S(1)}, u32[]{:S(2)}, u32[]{:S(2)}) collective-permute-start(bf16[1552,128]{1,0:T(8,128)(2,1)S(1)} %collective-permute-done.11.rest_6_), channel_id=1, source_target_pairs={{0,1},{1,0},{2,3},{3,2},{4,5},{5,4},{6,7},{7,6},{8,9},{9,8},{10,11... | collective-permute-start | bytes 1191944 | tf_op jit(solution)/shard_map/ppermute | solution.py:206
  66.3 1.9 %collective-permute-start.14 = (bf16[1552,128]{1,0:T(8,128)(2,1)S(1)}, bf16[1552,128]{1,0:T(8,128)(2,1)S(1)}, u32[]{:S(2)}, u32[]{:S(2)}) collective-permute-start(bf16[1552,128]{1,0:T(8,128)(2,1)S(1)} %collective-permute-done.13.rest_7_), channel_id=1, source_target_pairs={{0,1},{1,0},{2,3},{3,2},{4,5},{5,4},{6,7},{7,6},{8,9},{9,8},{10,11... | collective-permute-start | bytes 1191944 | tf_op jit(solution)/shard_map/ppermute | solution.py:206

commit v4 on v3

--- a/solution.py
+++ b/solution.py
@@ -11,6 +11,8 @@
 VMEM_LIMIT = 40 * 1024 * 1024
 LANES = 128
 CHUNKS = 4
+COSTS = (10000000000, 30000000000, 1, 1)
+HALVES = (2,)
 SPLIT = 1024
 TAIL = 16
 
@@ -38,11 +40,13 @@
     out[pieces * slots :, :] = jnp.concatenate(lines, axis=0).astype(jnp.bfloat16)
 
 
-def _block(ref, slots):
-    return jnp.concatenate([ref[k * slots : (k + 1) * slots, :] for k in range(ref.shape[0] // slots)], axis=1)
-
-
-def _ranks(ref, slots):
+def _block(parts, slots):
+    pieces = [ref[k * slots : (k + 1) * slots, :] for ref in parts for k in range(ref.shape[0] // slots)]
+    return jnp.concatenate(pieces, axis=1)
+
+
+def _ranks(parts, slots):
+    ref = parts[-1]
     tail = ref[ref.shape[0] - TAIL :, :].astype(jnp.float32)
     spans = _spans(slots)
     value = tail[:spans] * 256.0 + tail[spans : 2 * spans]
@@ -96,7 +100,7 @@
         _write_block(out, pick, unit, high[r : r + 1, first:], low[r : r + 1, first:], last - first)
 
 
-def _pack_rest(pieces, groups, me_ref, unit_ref, lab_ref, pos_ref, ranks_ref, after_ref, *outs):
+def _pack_rest(pieces, groups, me_ref, unit_ref, lab_ref, pos_ref, ranks_ref, *outs):
     for (r, first, last), out in zip(pieces, outs):
         pick = _pick(lab_ref[...], pos_ref[...], jnp.bitwise_xor(me_ref[0], r), first, last)
         high = ranks_ref[r : r + 1, first:]
@@ -106,8 +110,14 @@
 
 def _score(pieces, n_old, final, me_ref, prev_ref, *rest):
     n = len(pieces)
-    own, sib, out_ref = rest[:n], rest[n : 2 * n], rest[2 * n]
+    out_ref, rest = rest[-1], list(rest[:-1])
     sizes = [last - first for _, first, last in pieces]
+    blocks = []
+    while rest:
+        parts = [rest.pop(0)]
+        whole = parts[0].shape[0] % sizes[len(blocks) % n] == TAIL
+        blocks.append(parts if whole else parts + [rest.pop(0)])
+    own, sib = blocks[:n], blocks[n:]
     refs = [ref for j in range(n) for ref in (own[j], sib[j])]
     ranks = [_ranks(ref, sizes[i // 2]) for i, ref in enumerate(refs)]
     lanes = max(rank.shape[1] for rank in ranks)
@@ -156,7 +166,6 @@
     out_ref[...] = jnp.sum(jnp.where(mine, value, 0.0), axis=0)
 
 
-ANY = pl.BlockSpec(memory_space=pl.ANY)
 SMEM = pl.BlockSpec(memory_space=pltpu.SMEM)
 VMEM = pl.BlockSpec(memory_space=pltpu.VMEM)
 HBM = pl.BlockSpec(memory_space=pltpu.HBM)
@@ -183,15 +192,15 @@
         return pltpu.with_memory_space_constraint(x, pltpu.HBM)
 
     unit, pos, ranks, *far_blocks = pl.pallas_call(
-        functools.partial(_pack_first, far, groups, slots),
+        functools.partial(_pack_first, far[:quarter], groups, slots),
         out_shape=[
             jax.ShapeDtypeStruct((rows, width), jnp.bfloat16),
             jax.ShapeDtypeStruct((1, rows), jnp.int32),
             jax.ShapeDtypeStruct((2 * groups, _spans(slots) * LANES), jnp.float32),
         ]
-        + [block(piece) for piece in far],
+        + [block(piece) for piece in far[:quarter]],
         in_specs=[SMEM, HBM, HBM, HBM],
-        out_specs=[VMEM] * (3 + len(far)),
+        out_specs=[VMEM] * (3 + quarter),
         scratch_shapes=[
             pltpu.VMEM((rows, width), jnp.bfloat16),
             pltpu.VMEM((1, rows), jnp.int32),
@@ -200,7 +209,7 @@
             pltpu.SemaphoreType.DMA((2,)),
         ],
         compiler_params=params,
-        name="pack_far",
+        name="pack_first",
     )(me, in_hbm(embeddings), in_hbm(lab), in_hbm(priority.reshape(rows // LANES, LANES)))
     def swap(x):
         return lax.ppermute(x, "narrow", [(0, 1), (1, 0)])
@@ -211,16 +220,19 @@
     def after(x, *others):
         return lax.optimization_barrier((x, *others))[0]
 
-    near_blocks = pl.pallas_call(
-        functools.partial(_pack_rest, near, groups),
-        out_shape=[block(piece) for piece in near],
-        in_specs=[SMEM] + [VMEM] * 4 + [ANY],
-        out_specs=[VMEM] * len(near),
-        compiler_params=params,
-        cost_estimate=pl.CostEstimate(flops=10000000000, bytes_accessed=1, transcendentals=0),
-        name="pack_near",
-    )(me, unit, lab, pos, ranks, ranks)
-
+    def pack_rest(pieces, name):
+        return pl.pallas_call(
+            functools.partial(_pack_rest, pieces, groups),
+            out_shape=[block(piece) for piece in pieces],
+            in_specs=[SMEM] + [VMEM] * 4,
+            out_specs=[VMEM] * len(pieces),
+            compiler_params=params,
+            cost_estimate=pl.CostEstimate(flops=30000000000, bytes_accessed=1, transcendentals=0),
+            name=name,
+        )(me, unit, lab, pos, ranks)
+
+    far_blocks += pack_rest(far[quarter:], "pack_far")
+    near_blocks = pack_rest(near, "pack_near")
     own = {}
     for i, piece in enumerate(far):
         out = far_blocks[i]
@@ -241,23 +253,26 @@
     order, best, sib = [], jnp.zeros((groups, slots), jnp.float32), {}
     for number, step in enumerate(steps):
         for piece in step:
-            sib[piece] = swap(after(own[piece], best) if number >= 3 else own[piece])
+            ready = after(own[piece], best) if number >= 2 else own[piece]
+            cut = width // LANES // 2 * (piece[2] - piece[1])
+            sib[piece] = [swap(part) for part in ((ready[:cut], ready[cut:]) if number in HALVES else (ready,))]
         n_old = len(order)
         order = order + step
         old, new = (sum(piece[2] - piece[1] for piece in part) for part in (order[:n_old], step))
+        partners = [part for piece in order for part in sib[piece]]
         best = pl.pallas_call(
             functools.partial(_score, order, n_old, number == len(steps) - 1),
             out_shape=jax.ShapeDtypeStruct((groups, slots), jnp.float32),
-            in_specs=[SMEM] + [VMEM] * (1 + 2 * len(order)),
+            in_specs=[SMEM] + [VMEM] * (1 + len(order) + len(partners)),
             out_specs=VMEM,
             compiler_params=params,
             cost_estimate=pl.CostEstimate(
-                flops=10000000000,
-                bytes_accessed=4 * (old + new) * width,
+                flops=COSTS[number],
+                bytes_accessed=1,
                 transcendentals=0,
             ),
             name=f"score_{number}",
-        )(me, best, *[own[piece] for piece in order], *[sib[piece] for piece in order])
+        )(me, best, *[own[piece] for piece in order], *partners)
 
     returned = lax.all_to_all(best, "wide", split_axis=0, concat_axis=0, tiled=True)
     return pl.pallas_call(

time: 95.9 us -> 93.9 us (0.979)
  waiting for transfers between devices: 35.8 us -> 32.5 us
  starting transfers between devices: 17.4 us -> 18.6 us
    ppermute x7, waiting for transfers between devices: 34.3 us -> 29.6 us  [send(): return lax.ppermute(x, 'wide', [(s, s ^ r) for s in range(groups)])]
    ppermute x8 -> x9, waiting for transfers between devices: 1.55 us -> 2.93 us  [swap(): return lax.ppermute(x, 'narrow', [(0, 1), (1, 0)])]
    ppermute x7, starting transfers between devices: 15.8 us -> 17.1 us  [send(): return lax.ppermute(x, 'wide', [(s, s ^ r) for s in range(groups)])]
    pallas_call x2 -> x3, Pallas kernels: 5 us -> 5.17 us  [the longest x1 2.66 us: local(): pl.pallas_call(functools.partial(_pack_first, far[:quarter], groups, slot...]
  transfers between devices with their start and end apart: 15 -> 16, of which waited for: 5 -> 7; matrix products, arithmetic and copies ran while one was open for 0% -> 0% of each run, Pallas kernels for 12% -> 13%
where the time goes in v4:
time: 93.9 us; the launch traced here: 93.8 us
  waiting for transfers between devices  32.5 us (35%)
  blocking collectives  23.4 us (25%)
  Pallas kernels  19.1 us (20%)
  starting transfers between devices  18.6 us (20%)
    ppermute x7, waiting for transfers between devices, send(): return lax.ppermute(x, 'wide', [(s, s ^ r) for s in range(groups)])  29.6 us
    all_to_all x1, blocking collectives, local(): lax.all_to_all(best, 'wide', split_axis=0, concat_axis=0, tiled=True)  23.4 us
    ppermute x7, starting transfers between devices, send(): return lax.ppermute(x, 'wide', [(s, s ^ r) for s in range(groups)])  17.1 us
    pallas_call x4, Pallas kernels, local(): pl.pallas_call(functools.partial(_score, order, n_old, number == len(step...  13.1 us
    ppermute x9, waiting for transfers between devices, swap(): return lax.ppermute(x, 'narrow', [(0, 1), (1, 0)])  2.93 us
    pallas_call x1, Pallas kernels, local(): pl.pallas_call(functools.partial(_pack_first, far[:quarter], groups, slot...  2.66 us
    pallas_call x2, Pallas kernels, pack_rest(): pl.pallas_call(functools.partial(_pack_rest, pieces, groups), out_shape=[...  2.51 us
  transfers between devices with their start and end apart: 16, of which 7 were waited for; matrix products, arithmetic and copies ran while one was open for 0% of the time, Pallas kernels for 13%

profile of v4, /device:TPU:0, one launch (start us, length us, event | category | flops | bytes accessed | tf_op | source)
XLA Modules:
  0.0 93.8 jit_solution(2575718355773305822)
XLA Ops:
  0.0 2.7 %pack_first.1 = (bf16[768,1024]{1,0:T(8,128)(2,1)S(1)}, s32[1,768]{1,0:T(1,128)S(1)}, f32[16,256]{1,0:T(8,128)S(1)}, bf16[1552,128]{1,0:T(8,128)(2,1)S(1)}) custom-call(s32[1]{0:T(128)} %bitcast.1.me_ref, bf16[768,1024]{1,0:T(8,128)(2,1)} %emb_hbm.1, s32[1,768]{1,0:T(1,128)} %bitcast.9, s32[6,128]{1,0:T(8,128)} %bitcast.13), custom_call_target="tpu_custom_call" | custom-call | tf_op jit(solution)/shard_map/pack_first/pallas_call | solution.py:194
  2.7 4.1 %collective-permute-start = (bf16[1552,128]{1,0:T(8,128)(2,1)S(1)}, bf16[1552,128]{1,0:T(8,128)(2,1)S(1)}, u32[]{:S(2)}, u32[]{:S(2)}) collective-permute-start(bf16[1552,128]{1,0:T(8,128)(2,1)S(1)} %get-tuple-element.24), channel_id=1, source_target_pairs={{0,8},{2,10},{4,12},{6,14},{8,0},{10,2},{12,4},{14,6},{1,9},{3,11}... | collective-permute-start | bytes 1191944 | tf_op jit(solution)/shard_map/ppermute | solution.py:218
  6.8 1.1 %pack_far.1 = (bf16[1552,128]{1,0:T(8,128)(2,1)S(1)}, bf16[1552,128]{1,0:T(8,128)(2,1)S(1)}, bf16[1552,128]{1,0:T(8,128)(2,1)S(1)}) custom-call(s32[1]{0:T(128)} %bitcast.1.me_ref, bf16[768,1024]{1,0:T(8,128)(2,1)S(1)} %get-tuple-element.21.unit_ref, s32[1,768]{1,0:T(1,128)S(1)} %bitcast.10, s32[1,768]{1,0:T(1,128)S(1)} %get-tuple-element.20.pos_ref, ...), custom_call_target="tpu_custom_call" | custom-call | flops 30000001024 | bytes 1 | tf_op jit(solution)/shard_map/pack_far/pallas_call | solution.py:224
  7.9 1.4 %collective-permute-start.3 = (bf16[1552,128]{1,0:T(8,128)(2,1)S(1)}, bf16[1552,128]{1,0:T(8,128)(2,1)S(1)}, u32[]{:S(2)}, u32[]{:S(2)}) collective-permute-start(bf16[1552,128]{1,0:T(8,128)(2,1)S(1)} %get-tuple-element.25), channel_id=1, source_target_pairs={{0,10},{2,8},{4,14},{6,12},{8,2},{10,0},{12,6},{14,4},{1,11},{3,9}... | collective-permute-start | bytes 1191944 | tf_op jit(solution)/shard_map/ppermute | solution.py:218
  9.2 1.4 %pack_near.1 = (bf16[1552,128]{1,0:T(8,128)(2,1)S(1)}, bf16[1552,128]{1,0:T(8,128)(2,1)S(1)}, bf16[1552,128]{1,0:T(8,128)(2,1)S(1)}, bf16[1552,128]{1,0:T(8,128)(2,1)S(1)}) custom-call(s32[1]{0:T(128)} %bitcast.1.me_ref, bf16[768,1024]{1,0:T(8,128)(2,1)S(1)} %get-tuple-element.21.unit_ref, s32[1,768]{1,0:T(1,128)S(1)} %bitcast.11, ...), custom_call_target="tpu_custom_call" | custom-call | flops 30000001024 | bytes 1 | tf_op jit(solution)/shard_map/pack_near/pallas_call | solution.py:224
  10.7 0.3 collective-permute-start.4
  11.0 1.8 %collective-permute-start.5 = (bf16[1552,128]{1,0:T(8,128)(2,1)S(1)}, bf16[1552,128]{1,0:T(8,128)(2,1)S(1)}, u32[]{:S(2)}, u32[]{:S(2)}) collective-permute-start(bf16[1552,128]{1,0:T(8,128)(2,1)S(1)} %get-tuple-element.27), channel_id=1, source_target_pairs={{0,4},{2,6},{4,0},{6,2},{8,12},{10,14},{12,8},{14,10},{1,5},{3,7},... | collective-permute-start | bytes 1191944 | tf_op jit(solution)/shard_map/ppermute | solution.py:218
  12.8 1.4 %collective-permute-start.6 = (bf16[1552,128]{1,0:T(8,128)(2,1)S(1)}, bf16[1552,128]{1,0:T(8,128)(2,1)S(1)}, u32[]{:S(2)}, u32[]{:S(2)}) collective-permute-start(bf16[1552,128]{1,0:T(8,128)(2,1)S(1)} %get-tuple-element.28), channel_id=1, source_target_pairs={{0,6},{2,4},{4,2},{6,0},{8,14},{10,12},{12,10},{14,8},{1,7},{3,5},... | collective-permute-start | bytes 1191944 | tf_op jit(solution)/shard_map/ppermute | solution.py:218
  14.2 19.7 %collective-permute-done.rest_1_ = bf16[1552,128]{1,0:T(8,128)(2,1)S(1)} collective-permute-done((bf16[1552,128]{1,0:T(8,128)(2,1)S(1)}, bf16[1552,128]{1,0:T(8,128)(2,1)S(1)}, u32[]{:S(2)}, u32[]{:S(2)}) %collective-permute-start) | collective-permute-done | bytes 397344 | tf_op jit(solution)/shard_map/ppermute | solution.py:218
  33.9 8.7 %collective-permute-done.3.rest_2_ = bf16[1552,128]{1,0:T(8,128)(2,1)S(1)} collective-permute-done((bf16[1552,128]{1,0:T(8,128)(2,1)S(1)}, bf16[1552,128]{1,0:T(8,128)(2,1)S(1)}, u32[]{:S(2)}, u32[]{:S(2)}) %collective-permute-start.3) | collective-permute-done | bytes 397344 | tf_op jit(solution)/shard_map/ppermute | solution.py:218
  42.6 3.5 %collective-permute-start.11 = (bf16[1552,128]{1,0:T(8,128)(2,1)S(1)}, bf16[1552,128]{1,0:T(8,128)(2,1)S(1)}, u32[]{:S(2)}, u32[]{:S(2)}) collective-permute-start(bf16[1552,128]{1,0:T(8,128)(2,1)S(1)} %get-tuple-element.30), channel_id=1, source_target_pairs={{0,12},{2,14},{4,8},{6,10},{8,4},{10,6},{12,0},{14,2},{1,13},{3,15... | collective-permute-start | bytes 1191944 | tf_op jit(solution)/shard_map/ppermute | solution.py:218
  46.3 0.4 collective-permute-done.6.rest_5_
  46.7 0.5 collective-permute-start.9
  47.3 1.1 %score_0.1.prev_ref = f32[8,192]{1,0:T(8,128)S(1)} custom-call(s32[1]{0:T(128)} %bitcast.1.me_ref, f32[8,192]{1,0:T(8,128)S(1)} %broadcast_in_dim.3.prev_ref, bf16[1552,128]{1,0:T(8,128)(2,1)S(1)} %get-tuple-element.23.rest_0_, bf16[1552,128]{1,0:T(8,128)(2,1)S(1)} %collective-permute-done.rest_1_, ...), custom_call_target="tpu_custom_call" | custom-call | flops 10000000000 | bytes 1 | tf_op jit(solution)/shard_map/score_0/pallas_call | solution.py:263
  48.4 4.6 %collective-permute-start.14 = (bf16[1552,128]{1,0:T(8,128)(2,1)S(1)}, bf16[1552,128]{1,0:T(8,128)(2,1)S(1)}, u32[]{:S(2)}, u32[]{:S(2)}) collective-permute-start(bf16[1552,128]{1,0:T(8,128)(2,1)S(1)} %get-tuple-element.33), channel_id=1, source_target_pairs={{0,14},{2,12},{4,10},{6,8},{8,6},{10,4},{12,2},{14,0},{1,15},{3,13... | collective-permute-start | bytes 1191944 | tf_op jit(solution)/shard_map/ppermute | solution.py:218
  53.1 5.8 %score_1.1.prev_ref = f32[8,192]{1,0:T(8,128)S(1)} custom-call(s32[1]{0:T(128)} %bitcast.1.me_ref, f32[8,192]{1,0:T(8,128)S(1)} %score_0.1.prev_ref, bf16[1552,128]{1,0:T(8,128)(2,1)S(1)} %get-tuple-element.23.rest_0_, bf16[1552,128]{1,0:T(8,128)(2,1)S(1)} %collective-permute-done.rest_1_, bf16[1552,128]{1,0:T(8,128)(2,1)S(1)} %collective-permute-done.3.rest_2_, ...), custom_call_target="tpu_custom_call" | custom-call | flops 30000001024 | bytes 1 | tf_op jit(solution)/shard_map/score_1/pallas_call | solution.py:263
  59.0 0.5 collective-permute-start.12
  59.5 1.1 %collective-permute-done.12.rest_13_.rest_14_ = bf16[768,128]{1,0:T(8,128)(2,1)S(1)} collective-permute-done((bf16[768,128]{1,0:T(8,128)(2,1)S(1)}, bf16[768,128]{1,0:T(8,128)(2,1)S(1)}, u32[]{:S(2)}, u32[]{:S(2)}) %collective-permute-start.12) | collective-permute-done | bytes 196640 | tf_op jit(solution)/shard_map/ppermute | solution.py:215
  60.7 3.1 %score_2.1.prev_ref = f32[8,192]{1,0:T(8,128)S(1)} custom-call(s32[1]{0:T(128)} %bitcast.1.me_ref, f32[8,192]{1,0:T(8,128)S(1)} %score_1.1.prev_ref, bf16[1552,128]{1,0:T(8,128)(2,1)S(1)} %get-tuple-element.23.rest_0_, bf16[1552,128]{1,0:T(8,128)(2,1)S(1)} %collective-permute-done.rest_1_, bf16[1552,128]{1,0:T(8,128)(2,1)S(1)} %collective-permute-done.3.rest_2_, ...), custom_call_target="tpu_custom_call" | custom-call | flops 1 | bytes 1 | tf_op jit(solution)/shard_map/score_2/pallas_call | solution.py:263
  63.7 0.8 collective-permute-done.14.rest_7_
  64.6 1.7 %collective-permute-done.15.rest_16_ = bf16[1552,128]{1,0:T(8,128)(2,1)S(1)} collective-permute-done((bf16[1552,128]{1,0:T(8,128)(2,1)S(1)}, bf16[1552,128]{1,0:T(8,128)(2,1)S(1)}, u32[]{:S(2)}, u32[]{:S(2)}) %collective-permute-start.15) | collective-permute-done | bytes 397344 | tf_op jit(solution)/shard_map/ppermute | solution.py:215
  66.3 3.2 %score_3.1 = f32[8,192]{1,0:T(8,128)S(1)} custom-call(s32[1]{0:T(128)} %bitcast.1.me_ref, f32[8,192]{1,0:T(8,128)S(1)} %score_2.1.prev_ref, bf16[1552,128]{1,0:T(8,128)(2,1)S(1)} %get-tuple-element.23.rest_0_, bf16[1552,128]{1,0:T(8,128)(2,1)S(1)} %collective-permute-done.rest_1_, bf16[1552,128]{1,0:T(8,128)(2,1)S(1)} %collective-permute-done.3.rest_2_, ...), custom_call_target="tpu_custom_call" | custom-call | flops 1 | bytes 1 | tf_op jit(solution)/shard_map/score_3/pallas_call | solution.py:263
  69.5 23.4 %all_to_all.11 = f32[8,1,192]{2,1,0:T(1,128)S(1)} all-to-all(f32[8,1,192]{2,1,0:T(1,128)S(1)} %copy.4), channel_id=1, replica_groups=mesh['parts'=2,'wide'=8,'narrow'=2] {'wide'}, dimensions={0} | all-to-all | bytes 12288 | tf_op jit(solution)/shard_map/all_to_all | solution.py:277
  92.9 0.8 select.1
  (24 shorter events, 0.6 us)
Async XLA Ops:
  0.0 6.8 %copy-start = (s32[768,1]{0,1:T(1,128)S(1)}, s32[768,1]{0,1:T(1,128)}, u32[]{:S(2)}) copy-start(s32[768,1]{0,1:T(1,128)} %param.4) | copy-start | bytes 9220
  2.7 31.3 %collective-permute-start = (bf16[1552,128]{1,0:T(8,128)(2,1)S(1)}, bf16[1552,128]{1,0:T(8,128)(2,1)S(1)}, u32[]{:S(2)}, u32[]{:S(2)}) collective-permute-start(bf16[1552,128]{1,0:T(8,128)(2,1)S(1)} %get-tuple-element.24), channel_id=1, source_target_pairs={{0,8},{2,10},{4,12},{6,14},{8,0},{10,2},{12,4},{14,6},{1,9},{3,11}... | collective-permute-start | bytes 1191944 | tf_op jit(solution)/shard_map/ppermute | solution.py:218
  7.9 34.7 %collective-permute-start.3 = (bf16[1552,128]{1,0:T(8,128)(2,1)S(1)}, bf16[1552,128]{1,0:T(8,128)(2,1)S(1)}, u32[]{:S(2)}, u32[]{:S(2)}) collective-permute-start(bf16[1552,128]{1,0:T(8,128)(2,1)S(1)} %get-tuple-element.25), channel_id=1, source_target_pairs={{0,10},{2,8},{4,14},{6,12},{8,2},{10,0},{12,6},{14,4},{1,11},{3,9}... | collective-permute-start | bytes 1191944 | tf_op jit(solution)/shard_map/ppermute | solution.py:218
  10.7 32.0 %collective-permute-start.4 = (bf16[1552,128]{1,0:T(8,128)(2,1)S(1)}, bf16[1552,128]{1,0:T(8,128)(2,1)S(1)}, u32[]{:S(2)}, u32[]{:S(2)}) collective-permute-start(bf16[1552,128]{1,0:T(8,128)(2,1)S(1)} %get-tuple-element.26), channel_id=1, source_target_pairs={{0,2},{2,0},{4,6},{6,4},{8,10},{10,8},{12,14},{14,12},{1,3},{3,1},... | collective-permute-start | bytes 1191944 | tf_op jit(solution)/shard_map/ppermute | solution.py:218
  11.0 35.1 %collective-permute-start.5 = (bf16[1552,128]{1,0:T(8,128)(2,1)S(1)}, bf16[1552,128]{1,0:T(8,128)(2,1)S(1)}, u32[]{:S(2)}, u32[]{:S(2)}) collective-permute-start(bf16[1552,128]{1,0:T(8,128)(2,1)S(1)} %get-tuple-element.27), channel_id=1, source_target_pairs={{0,4},{2,6},{4,0},{6,2},{8,12},{10,14},{12,8},{14,10},{1,5},{3,7},... | collective-permute-start | bytes 1191944 | tf_op jit(solution)/shard_map/ppermute | solution.py:218
  12.8 33.9 %collective-permute-start.6 = (bf16[1552,128]{1,0:T(8,128)(2,1)S(1)}, bf16[1552,128]{1,0:T(8,128)(2,1)S(1)}, u32[]{:S(2)}, u32[]{:S(2)}) collective-permute-start(bf16[1552,128]{1,0:T(8,128)(2,1)S(1)} %get-tuple-element.28), channel_id=1, source_target_pairs={{0,6},{2,4},{4,2},{6,0},{8,14},{10,12},{12,10},{14,8},{1,7},{3,5},... | collective-permute-start | bytes 1191944 | tf_op jit(solution)/shard_map/ppermute | solution.py:218
  33.9 12.8 %collective-permute-start.1 = (bf16[1552,128]{1,0:T(8,128)(2,1)S(1)}, bf16[1552,128]{1,0:T(8,128)(2,1)S(1)}, u32[]{:S(2)}, u32[]{:S(2)}) collective-permute-start(bf16[1552,128]{1,0:T(8,128)(2,1)S(1)} %get-tuple-element.23.rest_0_), channel_id=1, source_target_pairs={{0,1},{1,0},{2,3},{3,2},{4,5},{5,4},{6,7},{7,6},{8,9},{9,8},{10,11... | collective-permute-start | bytes 1191944 | tf_op jit(solution)/shard_map/ppermute | solution.py:215
  42.6 4.6 %collective-permute-start.2 = (bf16[1552,128]{1,0:T(8,128)(2,1)S(1)}, bf16[1552,128]{1,0:T(8,128)(2,1)S(1)}, u32[]{:S(2)}, u32[]{:S(2)}) collective-permute-start(bf16[1552,128]{1,0:T(8,128)(2,1)S(1)} %collective-permute-done.rest_1_), channel_id=1, source_target_pairs={{0,1},{1,0},{2,3},{3,2},{4,5},{5,4},{6,7},{7,6},{8,9},{9,8},{10,11... | collective-permute-start | bytes 1191944 | tf_op jit(solution)/shard_map/ppermute | solution.py:215
  42.6 16.2 %collective-permute-start.11 = (bf16[1552,128]{1,0:T(8,128)(2,1)S(1)}, bf16[1552,128]{1,0:T(8,128)(2,1)S(1)}, u32[]{:S(2)}, u32[]{:S(2)}) collective-permute-start(bf16[1552,128]{1,0:T(8,128)(2,1)S(1)} %get-tuple-element.30), channel_id=1, source_target_pairs={{0,12},{2,14},{4,8},{6,10},{8,4},{10,6},{12,0},{14,2},{1,13},{3,15... | collective-permute-start | bytes 1191944 | tf_op jit(solution)/shard_map/ppermute | solution.py:218
  46.1 6.9 %collective-permute-start.7 = (bf16[1552,128]{1,0:T(8,128)(2,1)S(1)}, bf16[1552,128]{1,0:T(8,128)(2,1)S(1)}, u32[]{:S(2)}, u32[]{:S(2)}) collective-permute-start(bf16[1552,128]{1,0:T(8,128)(2,1)S(1)} %collective-permute-done.3.rest_2_), channel_id=1, source_target_pairs={{0,1},{1,0},{2,3},{3,2},{4,5},{5,4},{6,7},{7,6},{8,9},{9,8},{10,11... | collective-permute-start | bytes 1191944 | tf_op jit(solution)/shard_map/ppermute | solution.py:215
  46.7 1.7 %collective-permute-start.8 = (bf16[1552,128]{1,0:T(8,128)(2,1)S(1)}, bf16[1552,128]{1,0:T(8,128)(2,1)S(1)}, u32[]{:S(2)}, u32[]{:S(2)}) collective-permute-start(bf16[1552,128]{1,0:T(8,128)(2,1)S(1)} %collective-permute-done.4.rest_3_), channel_id=1, source_target_pairs={{0,1},{1,0},{2,3},{3,2},{4,5},{5,4},{6,7},{7,6},{8,9},{9,8},{10,11... | collective-permute-start | bytes 1191944 | tf_op jit(solution)/shard_map/ppermute | solution.py:215
  46.7 6.3 %collective-permute-start.9 = (bf16[1552,128]{1,0:T(8,128)(2,1)S(1)}, bf16[1552,128]{1,0:T(8,128)(2,1)S(1)}, u32[]{:S(2)}, u32[]{:S(2)}) collective-permute-start(bf16[1552,128]{1,0:T(8,128)(2,1)S(1)} %collective-permute-done.5.rest_4_), channel_id=1, source_target_pairs={{0,1},{1,0},{2,3},{3,2},{4,5},{5,4},{6,7},{7,6},{8,9},{9,8},{10,11... | collective-permute-start | bytes 1191944 | tf_op jit(solution)/shard_map/ppermute | solution.py:215
  47.2 5.8 %collective-permute-start.10 = (bf16[1552,128]{1,0:T(8,128)(2,1)S(1)}, bf16[1552,128]{1,0:T(8,128)(2,1)S(1)}, u32[]{:S(2)}, u32[]{:S(2)}) collective-permute-start(bf16[1552,128]{1,0:T(8,128)(2,1)S(1)} %collective-permute-done.6.rest_5_), channel_id=1, source_target_pairs={{0,1},{1,0},{2,3},{3,2},{4,5},{5,4},{6,7},{7,6},{8,9},{9,8},{10,11... | collective-permute-start | bytes 1191944 | tf_op jit(solution)/shard_map/ppermute | solution.py:215
  48.4 16.1 %collective-permute-start.14 = (bf16[1552,128]{1,0:T(8,128)(2,1)S(1)}, bf16[1552,128]{1,0:T(8,128)(2,1)S(1)}, u32[]{:S(2)}, u32[]{:S(2)}) collective-permute-start(bf16[1552,128]{1,0:T(8,128)(2,1)S(1)} %get-tuple-element.33), channel_id=1, source_target_pairs={{0,14},{2,12},{4,10},{6,8},{8,6},{10,4},{12,2},{14,0},{1,15},{3,13... | collective-permute-start | bytes 1191944 | tf_op jit(solution)/shard_map/ppermute | solution.py:218
  58.9 1.8 %collective-permute-start.13 = (bf16[784,128]{1,0:T(8,128)(2,1)S(1)}, bf16[784,128]{1,0:T(8,128)(2,1)S(1)}, u32[]{:S(2)}, u32[]{:S(2)}) collective-permute-start(bf16[784,128]{1,0:T(8,128)(2,1)S(1)} %slice.7), channel_id=1, source_target_pairs={{0,1},{1,0},{2,3},{3,2},{4,5},{5,4},{6,7},{7,6},{8,9},{9,8},{10,11... | collective-permute-start | bytes 602120 | tf_op jit(solution)/shard_map/ppermute | solution.py:215
  59.0 1.6 %collective-permute-start.12 = (bf16[768,128]{1,0:T(8,128)(2,1)S(1)}, bf16[768,128]{1,0:T(8,128)(2,1)S(1)}, u32[]{:S(2)}, u32[]{:S(2)}) collective-permute-start(bf16[768,128]{1,0:T(8,128)(2,1)S(1)} %slice.6), channel_id=1, source_target_pairs={{0,1},{1,0},{2,3},{3,2},{4,5},{5,4},{6,7},{7,6},{8,9},{9,8},{10,11... | collective-permute-start | bytes 589832 | tf_op jit(solution)/shard_map/ppermute | solution.py:215
  64.6 1.7 %collective-permute-start.15 = (bf16[1552,128]{1,0:T(8,128)(2,1)S(1)}, bf16[1552,128]{1,0:T(8,128)(2,1)S(1)}, u32[]{:S(2)}, u32[]{:S(2)}) collective-permute-start(bf16[1552,128]{1,0:T(8,128)(2,1)S(1)} %collective-permute-done.14.rest_7_), channel_id=1, source_target_pairs={{0,1},{1,0},{2,3},{3,2},{4,5},{5,4},{6,7},{7,6},{8,9},{9,8},{10,11... | collective-permute-start | bytes 1191944 | tf_op jit(solution)/shard_map/ppermute | solution.py:215

commit v5 on v4

--- a/solution.py
+++ b/solution.py
@@ -11,9 +11,8 @@
 VMEM_LIMIT = 40 * 1024 * 1024
 LANES = 128
 CHUNKS = 4
-COSTS = (10000000000, 30000000000, 1, 1)
-HALVES = (2,)
-SPLIT = 1024
+PACK_COST, SCORE_COSTS = 3 * 10**10, (10**10, 3 * 10**10, 1, 3 * 10**10)
+HALVED = 2
 TAIL = 16
 
 
@@ -108,39 +107,38 @@
         _write_block(out, pick, unit_ref[...], high, low, last - first)
 
 
-def _score(pieces, n_old, final, me_ref, prev_ref, *rest):
+def _score(pieces, jobs, n_sib, n_old, final, me_ref, prev_ref, *rest):
     n = len(pieces)
     out_ref, rest = rest[-1], list(rest[:-1])
-    sizes = [last - first for _, first, last in pieces]
+    sib_pieces = pieces[n - n_sib :] if final else pieces[:n_sib]
+    sizes = [last - first for _, first, last in list(pieces) + list(sib_pieces)]
     blocks = []
     while rest:
         parts = [rest.pop(0)]
-        whole = parts[0].shape[0] % sizes[len(blocks) % n] == TAIL
+        whole = parts[0].shape[0] % sizes[len(blocks)] == TAIL
         blocks.append(parts if whole else parts + [rest.pop(0)])
-    own, sib = blocks[:n], blocks[n:]
-    refs = [ref for j in range(n) for ref in (own[j], sib[j])]
-    ranks = [_ranks(ref, sizes[i // 2]) for i, ref in enumerate(refs)]
+    ranks = [_ranks(parts, size) for parts, size in zip(blocks, sizes)]
     lanes = max(rank.shape[1] for rank in ranks)
     padded = [jnp.concatenate([rank] * (lanes // rank.shape[1]), axis=1) for rank in ranks]
     columns = jnp.transpose(jnp.concatenate(padded, axis=0))
 
-    def best_of(keys, queries):
+    rows = [None] * n
+    for j in range(n_old):
+        r, first, last = pieces[j]
+        rows[j] = prev_ref[r : r + 1, first:last]
+    for keys, queries in jobs:
         sim = _nt(
-            jnp.concatenate([_block(refs[i], sizes[i // 2]) for i in keys], axis=0),
-            jnp.concatenate([_block(own[j], sizes[j]) for j in queries], axis=0),
+            jnp.concatenate([_block(blocks[i], sizes[i]) for i in keys], axis=0),
+            jnp.concatenate([_block(blocks[j], sizes[j]) for j in queries], axis=0),
         )
-        key_ranks = jnp.concatenate([columns[: sizes[i // 2], i : i + 1] for i in keys], axis=0)
-        query_ranks = jnp.concatenate([ranks[2 * j][:, : sizes[j]] for j in queries], axis=1)
+        key_ranks = jnp.concatenate([columns[: sizes[i], i : i + 1] for i in keys], axis=0)
+        query_ranks = jnp.concatenate([ranks[j][:, : sizes[j]] for j in queries], axis=1)
         best = jnp.max(jnp.where(key_ranks < query_ranks, sim, -1.0), axis=0, keepdims=True)
-        starts = [sum(sizes[j] for j in queries[:i]) for i in range(len(queries) + 1)]
-        return [best[:, starts[i] : starts[i + 1]] for i in range(len(queries))]
-
-    rows = []
-    if n_old:
-        old = best_of(range(2 * n_old, 2 * n), range(n_old))
-        for (r, first, last), row in zip(pieces, old):
-            rows.append(jnp.maximum(row, prev_ref[r : r + 1, first:last]))
-    rows += best_of(range(2 * n), range(n_old, n))
+        start = 0
+        for j in queries:
+            row = best[:, start : start + sizes[j]]
+            rows[j] = row if rows[j] is None else jnp.maximum(rows[j], row)
+            start += sizes[j]
     if not final:
         for (r, first, last), row in zip(pieces, rows):
             out_ref[r : r + 1, first:last] = row
@@ -178,14 +176,13 @@
     half = groups // 2
     me = lax.axis_index("wide").astype(jnp.int32).reshape(1)
     lab = labels.reshape(1, rows)
+
     def block(piece):
         return jax.ShapeDtypeStruct((width // LANES * (piece[2] - piece[1]) + TAIL, LANES), jnp.bfloat16)
 
     quarter = max(1, half // 4)
     near = [(r, 0, slots) for r in range(half)]
     far = [(r, 0, slots) for r in range(half, groups)]
-    if SPLIT < slots:
-        far[-1:] = [(groups - 1, 0, SPLIT), (groups - 1, SPLIT, slots)]
     params = pltpu.CompilerParams(vmem_limit_bytes=VMEM_LIMIT)
 
     def in_hbm(x):
@@ -211,6 +208,7 @@
         compiler_params=params,
         name="pack_first",
     )(me, in_hbm(embeddings), in_hbm(lab), in_hbm(priority.reshape(rows // LANES, LANES)))
+
     def swap(x):
         return lax.ppermute(x, "narrow", [(0, 1), (1, 0)])
 
@@ -227,7 +225,7 @@
             in_specs=[SMEM] + [VMEM] * 4,
             out_specs=[VMEM] * len(pieces),
             compiler_params=params,
-            cost_estimate=pl.CostEstimate(flops=30000000000, bytes_accessed=1, transcendentals=0),
+            cost_estimate=pl.CostEstimate(flops=PACK_COST, bytes_accessed=1, transcendentals=0),
             name=name,
         )(me, unit, lab, pos, ranks)
 
@@ -246,33 +244,39 @@
         near[:1] + far[:quarter],
         far[quarter : 2 * quarter] + near[1:],
         far[2 * quarter : 3 * quarter],
-        far[3 * quarter : 4 * quarter],
-        far[4 * quarter :],
+        far[3 * quarter :],
     ]
-    steps = [step for step in steps if step]
+
+    def score(pieces, partners, jobs, n_old, best, name, number, final=False):
+        others = [part for piece in partners for part in sib[piece]]
+        return pl.pallas_call(
+            functools.partial(_score, pieces, jobs, len(partners), n_old, final),
+            out_shape=jax.ShapeDtypeStruct((groups, slots), jnp.float32),
+            in_specs=[SMEM] + [VMEM] * (1 + len(pieces) + len(others)),
+            out_specs=VMEM,
+            compiler_params=params,
+            cost_estimate=pl.CostEstimate(flops=SCORE_COSTS[number], bytes_accessed=1, transcendentals=0),
+            name=name,
+        )(me, best, *[own[piece] for piece in pieces], *others)
+
     order, best, sib = [], jnp.zeros((groups, slots), jnp.float32), {}
     for number, step in enumerate(steps):
         for piece in step:
-            ready = after(own[piece], best) if number >= 2 else own[piece]
+            ready = after(own[piece], best) if number >= HALVED else own[piece]
             cut = width // LANES // 2 * (piece[2] - piece[1])
-            sib[piece] = [swap(part) for part in ((ready[:cut], ready[cut:]) if number in HALVES else (ready,))]
+            sib[piece] = [swap(part) for part in ((ready[:cut], ready[cut:]) if number == HALVED else (ready,))]
         n_old = len(order)
         order = order + step
-        old, new = (sum(piece[2] - piece[1] for piece in part) for part in (order[:n_old], step))
-        partners = [part for piece in order for part in sib[piece]]
-        best = pl.pallas_call(
-            functools.partial(_score, order, n_old, number == len(steps) - 1),
-            out_shape=jax.ShapeDtypeStruct((groups, slots), jnp.float32),
-            in_specs=[SMEM] + [VMEM] * (1 + len(order) + len(partners)),
-            out_specs=VMEM,
-            compiler_params=params,
-            cost_estimate=pl.CostEstimate(
-                flops=COSTS[number],
-                bytes_accessed=1,
-                transcendentals=0,
-            ),
-            name=f"score_{number}",
-        )(me, best, *[own[piece] for piece in order], *partners)
+        n = len(order)
+        old, new = list(range(n_old)), list(range(n_old, n))
+        if number < len(steps) - 1:
+            jobs = [(new + [n + j for j in new], old)] if old else []
+            best = score(order, order, jobs + [(list(range(2 * n)), new)], n_old, best, f"score_{number}", number)
+        else:
+            jobs = [(list(range(n + n_old)), new)]
+            best = score(order, order[:n_old], jobs, n_old, best, f"score_{number}", number)
+            jobs = [(new + list(range(n, 2 * n - n_old)), old + new)]
+            best = score(order, step, jobs, n, best, "score_final", number, final=True)
 
     returned = lax.all_to_all(best, "wide", split_axis=0, concat_axis=0, tiled=True)
     return pl.pallas_call(

time: 93.9 us -> 92.3 us (0.983)
  waiting for transfers between devices: 32.5 us -> 30.9 us
    ppermute x9, waiting for transfers between devices: 2.93 us -> 1.21 us  [swap(): return lax.ppermute(x, 'narrow', [(0, 1), (1, 0)])]
    pallas_call x4 -> x5, Pallas kernels: 13.1 us -> 13.2 us  [score(): pl.pallas_call(functools.partial(_score, pieces, jobs, len(partners), n_o...]
  transfers between devices with their start and end apart: 16 -> 16, of which waited for: 7 -> 6; matrix products, arithmetic and copies ran while one was open for 0% -> 0% of each run, Pallas kernels for 13% -> 15%
where the time goes in v5:
time: 92.3 us; the launch traced here: 92.2 us
  waiting for transfers between devices  30.9 us (33%)
  blocking collectives  23.4 us (25%)
  Pallas kernels  19.2 us (21%)
  starting transfers between devices  18.5 us (20%)
    ppermute x7, waiting for transfers between devices, send(): return lax.ppermute(x, 'wide', [(s, s ^ r) for s in range(groups)])  29.6 us
    all_to_all x1, blocking collectives, local(): lax.all_to_all(best, 'wide', split_axis=0, concat_axis=0, tiled=True)  23.4 us
    ppermute x7, starting transfers between devices, send(): return lax.ppermute(x, 'wide', [(s, s ^ r) for s in range(groups)])  17.1 us
    pallas_call x5, Pallas kernels, score(): pl.pallas_call(functools.partial(_score, pieces, jobs, len(partners), n_o...  13.2 us
    pallas_call x1, Pallas kernels, local(): pl.pallas_call(functools.partial(_pack_first, far[:quarter], groups, slot...  2.66 us
    pallas_call x2, Pallas kernels, pack_rest(): pl.pallas_call(functools.partial(_pack_rest, pieces, groups), out_shape=[...  2.5 us
  transfers between devices with their start and end apart: 16, of which 6 were waited for; matrix products, arithmetic and copies ran while one was open for 0% of the time, Pallas kernels for 15%

profile of v5, /device:TPU:0, one launch (start us, length us, event | category | flops | bytes accessed | tf_op | source)
XLA Modules:
  0.0 92.2 jit_solution(2343942622261039660)
XLA Ops:
  0.0 2.7 %pack_first.1 = (bf16[768,1024]{1,0:T(8,128)(2,1)S(1)}, s32[1,768]{1,0:T(1,128)S(1)}, f32[16,256]{1,0:T(8,128)S(1)}, bf16[1552,128]{1,0:T(8,128)(2,1)S(1)}) custom-call(s32[1]{0:T(128)} %bitcast.1.me_ref, bf16[768,1024]{1,0:T(8,128)(2,1)} %emb_hbm.1, s32[1,768]{1,0:T(1,128)} %bitcast.8, s32[6,128]{1,0:T(8,128)} %bitcast.13), custom_call_target="tpu_custom_call" | custom-call | tf_op jit(solution)/shard_map/pack_first/pallas_call | solution.py:191
  2.7 4.1 %collective-permute-start = (bf16[1552,128]{1,0:T(8,128)(2,1)S(1)}, bf16[1552,128]{1,0:T(8,128)(2,1)S(1)}, u32[]{:S(2)}, u32[]{:S(2)}) collective-permute-start(bf16[1552,128]{1,0:T(8,128)(2,1)S(1)} %get-tuple-element.24), channel_id=1, source_target_pairs={{0,8},{2,10},{4,12},{6,14},{8,0},{10,2},{12,4},{14,6},{1,9},{3,11}... | collective-permute-start | bytes 1191944 | tf_op jit(solution)/shard_map/ppermute | solution.py:216
  6.8 1.1 %pack_far.1 = (bf16[1552,128]{1,0:T(8,128)(2,1)S(1)}, bf16[1552,128]{1,0:T(8,128)(2,1)S(1)}, bf16[1552,128]{1,0:T(8,128)(2,1)S(1)}) custom-call(s32[1]{0:T(128)} %bitcast.1.me_ref, bf16[768,1024]{1,0:T(8,128)(2,1)S(1)} %get-tuple-element.21.unit_ref, s32[1,768]{1,0:T(1,128)S(1)} %bitcast.9, s32[1,768]{1,0:T(1,128)S(1)} %get-tuple-element.20.pos_ref, ...), custom_call_target="tpu_custom_call" | custom-call | flops 30000001024 | bytes 1 | tf_op jit(solution)/shard_map/pack_far/pallas_call | solution.py:222
  7.9 1.4 %collective-permute-start.3 = (bf16[1552,128]{1,0:T(8,128)(2,1)S(1)}, bf16[1552,128]{1,0:T(8,128)(2,1)S(1)}, u32[]{:S(2)}, u32[]{:S(2)}) collective-permute-start(bf16[1552,128]{1,0:T(8,128)(2,1)S(1)} %get-tuple-element.25), channel_id=1, source_target_pairs={{0,10},{2,8},{4,14},{6,12},{8,2},{10,0},{12,6},{14,4},{1,11},{3,9}... | collective-permute-start | bytes 1191944 | tf_op jit(solution)/shard_map/ppermute | solution.py:216
  9.2 1.4 %pack_near.1 = (bf16[1552,128]{1,0:T(8,128)(2,1)S(1)}, bf16[1552,128]{1,0:T(8,128)(2,1)S(1)}, bf16[1552,128]{1,0:T(8,128)(2,1)S(1)}, bf16[1552,128]{1,0:T(8,128)(2,1)S(1)}) custom-call(s32[1]{0:T(128)} %bitcast.1.me_ref, bf16[768,1024]{1,0:T(8,128)(2,1)S(1)} %get-tuple-element.21.unit_ref, s32[1,768]{1,0:T(1,128)S(1)} %bitcast.10, ...), custom_call_target="tpu_custom_call" | custom-call | flops 30000001024 | bytes 1 | tf_op jit(solution)/shard_map/pack_near/pallas_call | solution.py:222
  10.7 0.3 collective-permute-start.4
  11.0 1.8 %collective-permute-start.5 = (bf16[1552,128]{1,0:T(8,128)(2,1)S(1)}, bf16[1552,128]{1,0:T(8,128)(2,1)S(1)}, u32[]{:S(2)}, u32[]{:S(2)}) collective-permute-start(bf16[1552,128]{1,0:T(8,128)(2,1)S(1)} %get-tuple-element.27), channel_id=1, source_target_pairs={{0,4},{2,6},{4,0},{6,2},{8,12},{10,14},{12,8},{14,10},{1,5},{3,7},... | collective-permute-start | bytes 1191944 | tf_op jit(solution)/shard_map/ppermute | solution.py:216
  12.8 1.4 %collective-permute-start.6 = (bf16[1552,128]{1,0:T(8,128)(2,1)S(1)}, bf16[1552,128]{1,0:T(8,128)(2,1)S(1)}, u32[]{:S(2)}, u32[]{:S(2)}) collective-permute-start(bf16[1552,128]{1,0:T(8,128)(2,1)S(1)} %get-tuple-element.28), channel_id=1, source_target_pairs={{0,6},{2,4},{4,2},{6,0},{8,14},{10,12},{12,10},{14,8},{1,7},{3,5},... | collective-permute-start | bytes 1191944 | tf_op jit(solution)/shard_map/ppermute | solution.py:216
  14.2 19.7 %collective-permute-done.rest_1_ = bf16[1552,128]{1,0:T(8,128)(2,1)S(1)} collective-permute-done((bf16[1552,128]{1,0:T(8,128)(2,1)S(1)}, bf16[1552,128]{1,0:T(8,128)(2,1)S(1)}, u32[]{:S(2)}, u32[]{:S(2)}) %collective-permute-start) | collective-permute-done | bytes 397344 | tf_op jit(solution)/shard_map/ppermute | solution.py:216
  33.9 8.7 %collective-permute-done.3.rest_2_ = bf16[1552,128]{1,0:T(8,128)(2,1)S(1)} collective-permute-done((bf16[1552,128]{1,0:T(8,128)(2,1)S(1)}, bf16[1552,128]{1,0:T(8,128)(2,1)S(1)}, u32[]{:S(2)}, u32[]{:S(2)}) %collective-permute-start.3) | collective-permute-done | bytes 397344 | tf_op jit(solution)/shard_map/ppermute | solution.py:216
  42.6 3.5 %collective-permute-start.11 = (bf16[1552,128]{1,0:T(8,128)(2,1)S(1)}, bf16[1552,128]{1,0:T(8,128)(2,1)S(1)}, u32[]{:S(2)}, u32[]{:S(2)}) collective-permute-start(bf16[1552,128]{1,0:T(8,128)(2,1)S(1)} %get-tuple-element.30), channel_id=1, source_target_pairs={{0,12},{2,14},{4,8},{6,10},{8,4},{10,6},{12,0},{14,2},{1,13},{3,15... | collective-permute-start | bytes 1191944 | tf_op jit(solution)/shard_map/ppermute | solution.py:216
  46.3 0.4 collective-permute-done.6.rest_5_
  46.7 0.5 collective-permute-start.9
  47.3 1.1 %score_0.1.prev_ref = f32[8,192]{1,0:T(8,128)S(1)} custom-call(s32[1]{0:T(128)} %bitcast.1.me_ref, f32[8,192]{1,0:T(8,128)S(1)} %broadcast_in_dim.3.prev_ref, bf16[1552,128]{1,0:T(8,128)(2,1)S(1)} %get-tuple-element.23.rest_0_, bf16[1552,128]{1,0:T(8,128)(2,1)S(1)} %collective-permute-done.rest_1_, ...), custom_call_target="tpu_custom_call" | custom-call | flops 10000000000 | bytes 1 | tf_op jit(solution)/shard_map/score_0/pallas_call | solution.py:252
  48.4 4.6 %collective-permute-start.14 = (bf16[1552,128]{1,0:T(8,128)(2,1)S(1)}, bf16[1552,128]{1,0:T(8,128)(2,1)S(1)}, u32[]{:S(2)}, u32[]{:S(2)}) collective-permute-start(bf16[1552,128]{1,0:T(8,128)(2,1)S(1)} %get-tuple-element.33), channel_id=1, source_target_pairs={{0,14},{2,12},{4,10},{6,8},{8,6},{10,4},{12,2},{14,0},{1,15},{3,13... | collective-permute-start | bytes 1191944 | tf_op jit(solution)/shard_map/ppermute | solution.py:216
  53.0 5.8 %score_1.1.prev_ref = f32[8,192]{1,0:T(8,128)S(1)} custom-call(s32[1]{0:T(128)} %bitcast.1.me_ref, f32[8,192]{1,0:T(8,128)S(1)} %score_0.1.prev_ref, bf16[1552,128]{1,0:T(8,128)(2,1)S(1)} %get-tuple-element.23.rest_0_, bf16[1552,128]{1,0:T(8,128)(2,1)S(1)} %collective-permute-done.rest_1_, bf16[1552,128]{1,0:T(8,128)(2,1)S(1)} %collective-permute-done.3.rest_2_, ...), custom_call_target="tpu_custom_call" | custom-call | flops 30000001024 | bytes 1 | tf_op jit(solution)/shard_map/score_1/pallas_call | solution.py:252
  59.0 0.5 collective-permute-start.12
  59.5 1.1 %collective-permute-done.12.rest_13_.rest_14_ = bf16[768,128]{1,0:T(8,128)(2,1)S(1)} collective-permute-done((bf16[768,128]{1,0:T(8,128)(2,1)S(1)}, bf16[768,128]{1,0:T(8,128)(2,1)S(1)}, u32[]{:S(2)}, u32[]{:S(2)}) %collective-permute-start.12) | collective-permute-done | bytes 196640 | tf_op jit(solution)/shard_map/ppermute | solution.py:213
  60.6 3.0 %score_2.1.prev_ref = f32[8,192]{1,0:T(8,128)S(1)} custom-call(s32[1]{0:T(128)} %bitcast.1.me_ref, f32[8,192]{1,0:T(8,128)S(1)} %score_1.1.prev_ref, bf16[1552,128]{1,0:T(8,128)(2,1)S(1)} %get-tuple-element.23.rest_0_, bf16[1552,128]{1,0:T(8,128)(2,1)S(1)} %collective-permute-done.rest_1_, bf16[1552,128]{1,0:T(8,128)(2,1)S(1)} %collective-permute-done.3.rest_2_, ...), custom_call_target="tpu_custom_call" | custom-call | flops 1 | bytes 1 | tf_op jit(solution)/shard_map/score_2/pallas_call | solution.py:252
  63.7 0.9 collective-permute-done.14.rest_7_
  64.6 1.8 %score_3.1.prev_ref = f32[8,192]{1,0:T(8,128)S(1)} custom-call(s32[1]{0:T(128)} %bitcast.1.me_ref, f32[8,192]{1,0:T(8,128)S(1)} %score_2.1.prev_ref, bf16[1552,128]{1,0:T(8,128)(2,1)S(1)} %get-tuple-element.23.rest_0_, bf16[1552,128]{1,0:T(8,128)(2,1)S(1)} %collective-permute-done.rest_1_, bf16[1552,128]{1,0:T(8,128)(2,1)S(1)} %collective-permute-done.3.rest_2_, ...), custom_call_target="tpu_custom_call" | custom-call | flops 30000001024 | bytes 1 | tf_op jit(solution)/shard_map/score_3/pallas_call | solution.py:252
  66.4 1.5 %score_final.1 = f32[8,192]{1,0:T(8,128)S(1)} custom-call(s32[1]{0:T(128)} %bitcast.1.me_ref, f32[8,192]{1,0:T(8,128)S(1)} %score_3.1.prev_ref, bf16[1552,128]{1,0:T(8,128)(2,1)S(1)} %get-tuple-element.23.rest_0_, bf16[1552,128]{1,0:T(8,128)(2,1)S(1)} %collective-permute-done.rest_1_, bf16[1552,128]{1,0:T(8,128)(2,1)S(1)} %collective-permute-done.3.rest_2_, ...), custom_call_target="tpu_custom_call" | custom-call | flops 30000001024 | bytes 1 | tf_op jit(solution)/shard_map/score_final/pallas_call | solution.py:252
  67.9 23.4 %all_to_all.11 = f32[8,1,192]{2,1,0:T(1,128)S(1)} all-to-all(f32[8,1,192]{2,1,0:T(1,128)S(1)} %copy.4), channel_id=1, replica_groups=mesh['parts'=2,'wide'=8,'narrow'=2] {'wide'}, dimensions={0} | all-to-all | bytes 12288 | tf_op jit(solution)/shard_map/all_to_all | solution.py:281
  91.3 0.8 select.1
  (25 shorter events, 0.6 us)
Async XLA Ops:
  0.0 6.8 %copy-start = (s32[768,1]{0,1:T(1,128)S(1)}, s32[768,1]{0,1:T(1,128)}, u32[]{:S(2)}) copy-start(s32[768,1]{0,1:T(1,128)} %param.4) | copy-start | bytes 9220
  2.7 31.2 %collective-permute-start = (bf16[1552,128]{1,0:T(8,128)(2,1)S(1)}, bf16[1552,128]{1,0:T(8,128)(2,1)S(1)}, u32[]{:S(2)}, u32[]{:S(2)}) collective-permute-start(bf16[1552,128]{1,0:T(8,128)(2,1)S(1)} %get-tuple-element.24), channel_id=1, source_target_pairs={{0,8},{2,10},{4,12},{6,14},{8,0},{10,2},{12,4},{14,6},{1,9},{3,11}... | collective-permute-start | bytes 1191944 | tf_op jit(solution)/shard_map/ppermute | solution.py:216
  7.9 34.7 %collective-permute-start.3 = (bf16[1552,128]{1,0:T(8,128)(2,1)S(1)}, bf16[1552,128]{1,0:T(8,128)(2,1)S(1)}, u32[]{:S(2)}, u32[]{:S(2)}) collective-permute-start(bf16[1552,128]{1,0:T(8,128)(2,1)S(1)} %get-tuple-element.25), channel_id=1, source_target_pairs={{0,10},{2,8},{4,14},{6,12},{8,2},{10,0},{12,6},{14,4},{1,11},{3,9}... | collective-permute-start | bytes 1191944 | tf_op jit(solution)/shard_map/ppermute | solution.py:216
  10.7 32.0 %collective-permute-start.4 = (bf16[1552,128]{1,0:T(8,128)(2,1)S(1)}, bf16[1552,128]{1,0:T(8,128)(2,1)S(1)}, u32[]{:S(2)}, u32[]{:S(2)}) collective-permute-start(bf16[1552,128]{1,0:T(8,128)(2,1)S(1)} %get-tuple-element.26), channel_id=1, source_target_pairs={{0,2},{2,0},{4,6},{6,4},{8,10},{10,8},{12,14},{14,12},{1,3},{3,1},... | collective-permute-start | bytes 1191944 | tf_op jit(solution)/shard_map/ppermute | solution.py:216
  11.0 35.2 %collective-permute-start.5 = (bf16[1552,128]{1,0:T(8,128)(2,1)S(1)}, bf16[1552,128]{1,0:T(8,128)(2,1)S(1)}, u32[]{:S(2)}, u32[]{:S(2)}) collective-permute-start(bf16[1552,128]{1,0:T(8,128)(2,1)S(1)} %get-tuple-element.27), channel_id=1, source_target_pairs={{0,4},{2,6},{4,0},{6,2},{8,12},{10,14},{12,8},{14,10},{1,5},{3,7},... | collective-permute-start | bytes 1191944 | tf_op jit(solution)/shard_map/ppermute | solution.py:216
  12.8 33.9 %collective-permute-start.6 = (bf16[1552,128]{1,0:T(8,128)(2,1)S(1)}, bf16[1552,128]{1,0:T(8,128)(2,1)S(1)}, u32[]{:S(2)}, u32[]{:S(2)}) collective-permute-start(bf16[1552,128]{1,0:T(8,128)(2,1)S(1)} %get-tuple-element.28), channel_id=1, source_target_pairs={{0,6},{2,4},{4,2},{6,0},{8,14},{10,12},{12,10},{14,8},{1,7},{3,5},... | collective-permute-start | bytes 1191944 | tf_op jit(solution)/shard_map/ppermute | solution.py:216
  33.9 12.8 %collective-permute-start.1 = (bf16[1552,128]{1,0:T(8,128)(2,1)S(1)}, bf16[1552,128]{1,0:T(8,128)(2,1)S(1)}, u32[]{:S(2)}, u32[]{:S(2)}) collective-permute-start(bf16[1552,128]{1,0:T(8,128)(2,1)S(1)} %get-tuple-element.23.rest_0_), channel_id=1, source_target_pairs={{0,1},{1,0},{2,3},{3,2},{4,5},{5,4},{6,7},{7,6},{8,9},{9,8},{10,11... | collective-permute-start | bytes 1191944 | tf_op jit(solution)/shard_map/ppermute | solution.py:213
  42.6 4.6 %collective-permute-start.2 = (bf16[1552,128]{1,0:T(8,128)(2,1)S(1)}, bf16[1552,128]{1,0:T(8,128)(2,1)S(1)}, u32[]{:S(2)}, u32[]{:S(2)}) collective-permute-start(bf16[1552,128]{1,0:T(8,128)(2,1)S(1)} %collective-permute-done.rest_1_), channel_id=1, source_target_pairs={{0,1},{1,0},{2,3},{3,2},{4,5},{5,4},{6,7},{7,6},{8,9},{9,8},{10,11... | collective-permute-start | bytes 1191944 | tf_op jit(solution)/shard_map/ppermute | solution.py:213
  42.6 16.2 %collective-permute-start.11 = (bf16[1552,128]{1,0:T(8,128)(2,1)S(1)}, bf16[1552,128]{1,0:T(8,128)(2,1)S(1)}, u32[]{:S(2)}, u32[]{:S(2)}) collective-permute-start(bf16[1552,128]{1,0:T(8,128)(2,1)S(1)} %get-tuple-element.30), channel_id=1, source_target_pairs={{0,12},{2,14},{4,8},{6,10},{8,4},{10,6},{12,0},{14,2},{1,13},{3,15... | collective-permute-start | bytes 1191944 | tf_op jit(solution)/shard_map/ppermute | solution.py:216
  46.1 6.9 %collective-permute-start.7 = (bf16[1552,128]{1,0:T(8,128)(2,1)S(1)}, bf16[1552,128]{1,0:T(8,128)(2,1)S(1)}, u32[]{:S(2)}, u32[]{:S(2)}) collective-permute-start(bf16[1552,128]{1,0:T(8,128)(2,1)S(1)} %collective-permute-done.3.rest_2_), channel_id=1, source_target_pairs={{0,1},{1,0},{2,3},{3,2},{4,5},{5,4},{6,7},{7,6},{8,9},{9,8},{10,11... | collective-permute-start | bytes 1191944 | tf_op jit(solution)/shard_map/ppermute | solution.py:213
  46.7 1.7 %collective-permute-start.8 = (bf16[1552,128]{1,0:T(8,128)(2,1)S(1)}, bf16[1552,128]{1,0:T(8,128)(2,1)S(1)}, u32[]{:S(2)}, u32[]{:S(2)}) collective-permute-start(bf16[1552,128]{1,0:T(8,128)(2,1)S(1)} %collective-permute-done.4.rest_3_), channel_id=1, source_target_pairs={{0,1},{1,0},{2,3},{3,2},{4,5},{5,4},{6,7},{7,6},{8,9},{9,8},{10,11... | collective-permute-start | bytes 1191944 | tf_op jit(solution)/shard_map/ppermute | solution.py:213
  46.7 6.3 %collective-permute-start.9 = (bf16[1552,128]{1,0:T(8,128)(2,1)S(1)}, bf16[1552,128]{1,0:T(8,128)(2,1)S(1)}, u32[]{:S(2)}, u32[]{:S(2)}) collective-permute-start(bf16[1552,128]{1,0:T(8,128)(2,1)S(1)} %collective-permute-done.5.rest_4_), channel_id=1, source_target_pairs={{0,1},{1,0},{2,3},{3,2},{4,5},{5,4},{6,7},{7,6},{8,9},{9,8},{10,11... | collective-permute-start | bytes 1191944 | tf_op jit(solution)/shard_map/ppermute | solution.py:213
  47.2 5.8 %collective-permute-start.10 = (bf16[1552,128]{1,0:T(8,128)(2,1)S(1)}, bf16[1552,128]{1,0:T(8,128)(2,1)S(1)}, u32[]{:S(2)}, u32[]{:S(2)}) collective-permute-start(bf16[1552,128]{1,0:T(8,128)(2,1)S(1)} %collective-permute-done.6.rest_5_), channel_id=1, source_target_pairs={{0,1},{1,0},{2,3},{3,2},{4,5},{5,4},{6,7},{7,6},{8,9},{9,8},{10,11... | collective-permute-start | bytes 1191944 | tf_op jit(solution)/shard_map/ppermute | solution.py:213
  48.4 16.1 %collective-permute-start.14 = (bf16[1552,128]{1,0:T(8,128)(2,1)S(1)}, bf16[1552,128]{1,0:T(8,128)(2,1)S(1)}, u32[]{:S(2)}, u32[]{:S(2)}) collective-permute-start(bf16[1552,128]{1,0:T(8,128)(2,1)S(1)} %get-tuple-element.33), channel_id=1, source_target_pairs={{0,14},{2,12},{4,10},{6,8},{8,6},{10,4},{12,2},{14,0},{1,15},{3,13... | collective-permute-start | bytes 1191944 | tf_op jit(solution)/shard_map/ppermute | solution.py:216
  58.8 1.8 %collective-permute-start.13 = (bf16[784,128]{1,0:T(8,128)(2,1)S(1)}, bf16[784,128]{1,0:T(8,128)(2,1)S(1)}, u32[]{:S(2)}, u32[]{:S(2)}) collective-permute-start(bf16[784,128]{1,0:T(8,128)(2,1)S(1)} %slice.7), channel_id=1, source_target_pairs={{0,1},{1,0},{2,3},{3,2},{4,5},{5,4},{6,7},{7,6},{8,9},{9,8},{10,11... | collective-permute-start | bytes 602120 | tf_op jit(solution)/shard_map/ppermute | solution.py:213
  59.0 1.6 %collective-permute-start.12 = (bf16[768,128]{1,0:T(8,128)(2,1)S(1)}, bf16[768,128]{1,0:T(8,128)(2,1)S(1)}, u32[]{:S(2)}, u32[]{:S(2)}) collective-permute-start(bf16[768,128]{1,0:T(8,128)(2,1)S(1)} %slice.6), channel_id=1, source_target_pairs={{0,1},{1,0},{2,3},{3,2},{4,5},{5,4},{6,7},{7,6},{8,9},{9,8},{10,11... | collective-permute-start | bytes 589832 | tf_op jit(solution)/shard_map/ppermute | solution.py:213
  64.5 1.8 %collective-permute-start.15 = (bf16[1552,128]{1,0:T(8,128)(2,1)S(1)}, bf16[1552,128]{1,0:T(8,128)(2,1)S(1)}, u32[]{:S(2)}, u32[]{:S(2)}) collective-permute-start(bf16[1552,128]{1,0:T(8,128)(2,1)S(1)} %collective-permute-done.14.rest_7_), channel_id=1, source_target_pairs={{0,1},{1,0},{2,3},{3,2},{4,5},{5,4},{6,7},{7,6},{8,9},{9,8},{10,11... | collective-permute-start | bytes 1191944 | tf_op jit(solution)/shard_map/ppermute | solution.py:213

commit v6 on v5

--- a/solution.py
+++ b/solution.py
@@ -10,7 +10,7 @@
 EMPTY = 2.0**22
 VMEM_LIMIT = 40 * 1024 * 1024
 LANES = 128
-CHUNKS = 4
+CHUNKS = 1
 PACK_COST, SCORE_COSTS = 3 * 10**10, (10**10, 3 * 10**10, 1, 3 * 10**10)
 HALVED = 2
 TAIL = 16
@@ -28,8 +28,9 @@
     return -(-slots // LANES)
 
 
-def _write_block(out, pick, unit, high, low, slots):
-    block = jnp.dot(pick, unit, preferred_element_type=jnp.float32).astype(jnp.bfloat16)
+def _write_block(out, block, high, low, slots):
+    scale = lax.rsqrt(jnp.sum(block * block, axis=1, keepdims=True) + 1e-06)
+    block = (block * scale).astype(jnp.bfloat16)
     pieces = block.shape[1] // LANES
     for k in range(pieces):
         out[k * slots : (k + 1) * slots, :] = block[:, k * LANES : (k + 1) * LANES]
@@ -58,7 +59,7 @@
 
 
 def _pack_first(pieces, groups, slots, me_ref, emb_hbm, lab_hbm, prio_hbm, *rest):
-    unit_ref, pos_ref, ranks_ref, *outs = rest[:-5]
+    pos_ref, ranks_ref, *outs = rest[:-5]
     emb_ref, lab_ref, prio_ref, sems, word_sems = rest[-5:]
     rows = emb_ref.shape[0]
     words = [
@@ -70,13 +71,14 @@
     copies = [pltpu.make_async_copy(emb_hbm.at[span], emb_ref.at[span], sems.at[i]) for i, span in enumerate(spans)]
     for copy in words + copies:
         copy.start()
+    earlier_rows = lax.broadcasted_iota(jnp.int32, (rows, rows), 0)
+    before = _as_bf16(earlier_rows < lax.broadcasted_iota(jnp.int32, (rows, rows), 1))
     for copy in words:
         copy.wait()
     lab = lab_ref[...]
     away = jnp.bitwise_xor(lax.broadcasted_iota(jnp.int32, (groups, rows), 0), me_ref[0])
     onehot = (away == lab).astype(jnp.float32)
-    before = lax.broadcasted_iota(jnp.int32, (rows, rows), 0) < lax.broadcasted_iota(jnp.int32, (rows, rows), 1)
-    earlier = jnp.dot(onehot.astype(jnp.bfloat16), _as_bf16(before), preferred_element_type=jnp.float32)
+    earlier = jnp.dot(onehot.astype(jnp.bfloat16), before, preferred_element_type=jnp.float32)
     pos = jnp.sum(onehot * earlier, axis=0, keepdims=True).astype(jnp.int32)
     pos_ref[...] = pos
     prio = jnp.concatenate([prio_ref[i : i + 1, :] for i in range(rows // LANES)], axis=1)
@@ -88,23 +90,24 @@
     high = jnp.where(placed[2 * groups :] > 0.5, placed[:groups], EMPTY)
     low = placed[groups : 2 * groups]
     ranks_ref[...] = jnp.concatenate([high, low], axis=0)
-    for copy, span in zip(copies, spans):
+    picks = [_pick(lab, pos, jnp.bitwise_xor(me_ref[0], r), first, last) for r, first, last in pieces]
+    sums = [0.0] * len(pieces)
+    for i, copy in enumerate(copies):
         copy.wait()
-        emb = emb_ref[span, :].astype(jnp.float32)
-        scale = lax.rsqrt(jnp.sum(emb * emb, axis=1, keepdims=True) + 1e-06)
-        unit_ref[span, :] = (emb * scale).astype(jnp.bfloat16)
-    unit = unit_ref[...]
-    for (r, first, last), out in zip(pieces, outs):
-        pick = _pick(lab, pos, jnp.bitwise_xor(me_ref[0], r), first, last)
-        _write_block(out, pick, unit, high[r : r + 1, first:], low[r : r + 1, first:], last - first)
-
-
-def _pack_rest(pieces, groups, me_ref, unit_ref, lab_ref, pos_ref, ranks_ref, *outs):
+        part = emb_ref[spans[i], :]
+        for j, pick in enumerate(picks):
+            sums[j] += jnp.dot(pick[:, i * chunk : (i + 1) * chunk], part, preferred_element_type=jnp.float32)
+    for (r, first, last), out, block in zip(pieces, outs, sums):
+        _write_block(out, block, high[r : r + 1, first:], low[r : r + 1, first:], last - first)
+
+
+def _pack_rest(pieces, groups, me_ref, emb_ref, lab_ref, pos_ref, ranks_ref, *outs):
     for (r, first, last), out in zip(pieces, outs):
         pick = _pick(lab_ref[...], pos_ref[...], jnp.bitwise_xor(me_ref[0], r), first, last)
         high = ranks_ref[r : r + 1, first:]
         low = ranks_ref[groups + r : groups + r + 1, first:]
-        _write_block(out, pick, unit_ref[...], high, low, last - first)
+        block = jnp.dot(pick, emb_ref[...], preferred_element_type=jnp.float32)
+        _write_block(out, block, high, low, last - first)
 
 
 def _score(pieces, jobs, n_sib, n_old, final, me_ref, prev_ref, *rest):
@@ -188,16 +191,15 @@
     def in_hbm(x):
         return pltpu.with_memory_space_constraint(x, pltpu.HBM)
 
-    unit, pos, ranks, *far_blocks = pl.pallas_call(
+    pos, ranks, *far_blocks = pl.pallas_call(
         functools.partial(_pack_first, far[:quarter], groups, slots),
         out_shape=[
-            jax.ShapeDtypeStruct((rows, width), jnp.bfloat16),
             jax.ShapeDtypeStruct((1, rows), jnp.int32),
             jax.ShapeDtypeStruct((2 * groups, _spans(slots) * LANES), jnp.float32),
         ]
         + [block(piece) for piece in far[:quarter]],
         in_specs=[SMEM, HBM, HBM, HBM],
-        out_specs=[VMEM] * (3 + quarter),
+        out_specs=[VMEM] * (2 + quarter),
         scratch_shapes=[
             pltpu.VMEM((rows, width), jnp.bfloat16),
             pltpu.VMEM((1, rows), jnp.int32),
@@ -227,7 +229,7 @@
             compiler_params=params,
             cost_estimate=pl.CostEstimate(flops=PACK_COST, bytes_accessed=1, transcendentals=0),
             name=name,
-        )(me, unit, lab, pos, ranks)
+        )(me, embeddings, lab, pos, ranks)
 
     far_blocks += pack_rest(far[quarter:], "pack_far")
     near_blocks = pack_rest(near, "pack_near")

time: 92.3 us -> 91.9 us (level)
  transfers between devices with their start and end apart: 16 -> 16, of which waited for: 6 -> 5; matrix products, arithmetic and copies ran while one was open for 0% -> 0% of each run, Pallas kernels for 15% -> 16%
where the time goes in v6:
time: 91.9 us; the launch traced here: 91.7 us
  waiting for transfers between devices  30.7 us (33%)
  blocking collectives  23.4 us (25%)
  Pallas kernels  18.9 us (21%)
  starting transfers between devices  18.5 us (20%)
    ppermute x7, waiting for transfers between devices, send(): return lax.ppermute(x, 'wide', [(s, s ^ r) for s in range(groups)])  29.5 us
    all_to_all x1, blocking collectives, local(): lax.all_to_all(best, 'wide', split_axis=0, concat_axis=0, tiled=True)  23.4 us
    ppermute x7, starting transfers between devices, send(): return lax.ppermute(x, 'wide', [(s, s ^ r) for s in range(groups)])  17.1 us
    pallas_call x5, Pallas kernels, score(): pl.pallas_call(functools.partial(_score, pieces, jobs, len(partners), n_o...  13.2 us
    pallas_call x2, Pallas kernels, pack_rest(): pl.pallas_call(functools.partial(_pack_rest, pieces, groups), out_shape=[...  2.74 us
    pallas_call x1, Pallas kernels, local(): pl.pallas_call(functools.partial(_pack_first, far[:quarter], groups, slot...  2.16 us
  transfers between devices with their start and end apart: 16, of which 5 were waited for; matrix products, arithmetic and copies ran while one was open for 0% of the time, Pallas kernels for 16%

profile of v6, /device:TPU:0, one launch (start us, length us, event | category | flops | bytes accessed | tf_op | source)
XLA Modules:
  0.0 91.7 jit_solution(15191408532981972124)
XLA Ops:
  0.0 2.2 %pack_first.1 = (s32[1,768]{1,0:T(1,128)S(1)}, f32[16,256]{1,0:T(8,128)S(1)}, bf16[1552,128]{1,0:T(8,128)(2,1)S(1)}) custom-call(s32[1]{0:T(128)} %bitcast.1.me_ref, bf16[768,1024]{1,0:T(8,128)(2,1)} %emb_ref.3, s32[1,768]{1,0:T(1,128)} %bitcast.8, s32[6,128]{1,0:T(8,128)} %bitcast.13), custom_call_target="tpu_custom_call" | custom-call | tf_op jit(solution)/shard_map/pack_first/pallas_call | solution.py:194
  2.2 4.1 %collective-permute-start = (bf16[1552,128]{1,0:T(8,128)(2,1)S(1)}, bf16[1552,128]{1,0:T(8,128)(2,1)S(1)}, u32[]{:S(2)}, u32[]{:S(2)}) collective-permute-start(bf16[1552,128]{1,0:T(8,128)(2,1)S(1)} %get-tuple-element.22), channel_id=1, source_target_pairs={{0,8},{2,10},{4,12},{6,14},{8,0},{10,2},{12,4},{14,6},{1,9},{3,11}... | collective-permute-start | bytes 1191944 | tf_op jit(solution)/shard_map/ppermute | solution.py:218
  6.3 1.2 %pack_far.1 = (bf16[1552,128]{1,0:T(8,128)(2,1)S(1)}, bf16[1552,128]{1,0:T(8,128)(2,1)S(1)}, bf16[1552,128]{1,0:T(8,128)(2,1)S(1)}) custom-call(s32[1]{0:T(128)} %bitcast.1.me_ref, bf16[768,1024]{1,0:T(8,128)(2,1)S(1)} %copy-done, s32[1,768]{1,0:T(1,128)S(1)} %bitcast.9, s32[1,768]{1,0:T(1,128)S(1)} %get-tuple-element.19.pos_ref, ...), custom_call_target="tpu_custom_call" | custom-call | flops 30000001024 | bytes 1 | tf_op jit(solution)/shard_map/pack_far/pallas_call | solution.py:224
  7.5 1.4 %collective-permute-start.3 = (bf16[1552,128]{1,0:T(8,128)(2,1)S(1)}, bf16[1552,128]{1,0:T(8,128)(2,1)S(1)}, u32[]{:S(2)}, u32[]{:S(2)}) collective-permute-start(bf16[1552,128]{1,0:T(8,128)(2,1)S(1)} %get-tuple-element.23), channel_id=1, source_target_pairs={{0,10},{2,8},{4,14},{6,12},{8,2},{10,0},{12,6},{14,4},{1,11},{3,9}... | collective-permute-start | bytes 1191944 | tf_op jit(solution)/shard_map/ppermute | solution.py:218
  8.9 1.5 %pack_near.1 = (bf16[1552,128]{1,0:T(8,128)(2,1)S(1)}, bf16[1552,128]{1,0:T(8,128)(2,1)S(1)}, bf16[1552,128]{1,0:T(8,128)(2,1)S(1)}, bf16[1552,128]{1,0:T(8,128)(2,1)S(1)}) custom-call(s32[1]{0:T(128)} %bitcast.1.me_ref, bf16[768,1024]{1,0:T(8,128)(2,1)S(1)} %copy-done, s32[1,768]{1,0:T(1,128)S(1)} %bitcast.10, s32[1,768]{1,0:T(1,128)S(1)} %get-tuple-element.19.pos_ref, ...), custom_call_target="tpu_custom_call" | custom-call | flops 30000001024 | bytes 1 | tf_op jit(solution)/shard_map/pack_near/pallas_call | solution.py:224
  10.4 0.3 collective-permute-start.4
  10.7 1.8 %collective-permute-start.5 = (bf16[1552,128]{1,0:T(8,128)(2,1)S(1)}, bf16[1552,128]{1,0:T(8,128)(2,1)S(1)}, u32[]{:S(2)}, u32[]{:S(2)}) collective-permute-start(bf16[1552,128]{1,0:T(8,128)(2,1)S(1)} %get-tuple-element.25), channel_id=1, source_target_pairs={{0,4},{2,6},{4,0},{6,2},{8,12},{10,14},{12,8},{14,10},{1,5},{3,7},... | collective-permute-start | bytes 1191944 | tf_op jit(solution)/shard_map/ppermute | solution.py:218
  12.5 1.4 %collective-permute-start.6 = (bf16[1552,128]{1,0:T(8,128)(2,1)S(1)}, bf16[1552,128]{1,0:T(8,128)(2,1)S(1)}, u32[]{:S(2)}, u32[]{:S(2)}) collective-permute-start(bf16[1552,128]{1,0:T(8,128)(2,1)S(1)} %get-tuple-element.26), channel_id=1, source_target_pairs={{0,6},{2,4},{4,2},{6,0},{8,14},{10,12},{12,10},{14,8},{1,7},{3,5},... | collective-permute-start | bytes 1191944 | tf_op jit(solution)/shard_map/ppermute | solution.py:218
  13.9 19.5 %collective-permute-done.rest_1_ = bf16[1552,128]{1,0:T(8,128)(2,1)S(1)} collective-permute-done((bf16[1552,128]{1,0:T(8,128)(2,1)S(1)}, bf16[1552,128]{1,0:T(8,128)(2,1)S(1)}, u32[]{:S(2)}, u32[]{:S(2)}) %collective-permute-start) | collective-permute-done | bytes 397344 | tf_op jit(solution)/shard_map/ppermute | solution.py:218
  33.4 8.7 %collective-permute-done.3.rest_2_ = bf16[1552,128]{1,0:T(8,128)(2,1)S(1)} collective-permute-done((bf16[1552,128]{1,0:T(8,128)(2,1)S(1)}, bf16[1552,128]{1,0:T(8,128)(2,1)S(1)}, u32[]{:S(2)}, u32[]{:S(2)}) %collective-permute-start.3) | collective-permute-done | bytes 397344 | tf_op jit(solution)/shard_map/ppermute | solution.py:218
  42.1 3.5 %collective-permute-start.11 = (bf16[1552,128]{1,0:T(8,128)(2,1)S(1)}, bf16[1552,128]{1,0:T(8,128)(2,1)S(1)}, u32[]{:S(2)}, u32[]{:S(2)}) collective-permute-start(bf16[1552,128]{1,0:T(8,128)(2,1)S(1)} %get-tuple-element.28), channel_id=1, source_target_pairs={{0,12},{2,14},{4,8},{6,10},{8,4},{10,6},{12,0},{14,2},{1,13},{3,15... | collective-permute-start | bytes 1191944 | tf_op jit(solution)/shard_map/ppermute | solution.py:218
  45.9 0.6 collective-permute-done.6.rest_5_
  46.5 0.5 collective-permute-start.9
  47.0 1.1 %score_0.1.prev_ref = f32[8,192]{1,0:T(8,128)S(1)} custom-call(s32[1]{0:T(128)} %bitcast.1.me_ref, f32[8,192]{1,0:T(8,128)S(1)} %broadcast_in_dim.3.prev_ref, bf16[1552,128]{1,0:T(8,128)(2,1)S(1)} %get-tuple-element.21.rest_0_, bf16[1552,128]{1,0:T(8,128)(2,1)S(1)} %collective-permute-done.rest_1_, ...), custom_call_target="tpu_custom_call" | custom-call | flops 10000000000 | bytes 1 | tf_op jit(solution)/shard_map/score_0/pallas_call | solution.py:254
  48.1 4.6 %collective-permute-start.14 = (bf16[1552,128]{1,0:T(8,128)(2,1)S(1)}, bf16[1552,128]{1,0:T(8,128)(2,1)S(1)}, u32[]{:S(2)}, u32[]{:S(2)}) collective-permute-start(bf16[1552,128]{1,0:T(8,128)(2,1)S(1)} %get-tuple-element.31), channel_id=1, source_target_pairs={{0,14},{2,12},{4,10},{6,8},{8,6},{10,4},{12,2},{14,0},{1,15},{3,13... | collective-permute-start | bytes 1191944 | tf_op jit(solution)/shard_map/ppermute | solution.py:218
  52.7 5.8 %score_1.1.prev_ref = f32[8,192]{1,0:T(8,128)S(1)} custom-call(s32[1]{0:T(128)} %bitcast.1.me_ref, f32[8,192]{1,0:T(8,128)S(1)} %score_0.1.prev_ref, bf16[1552,128]{1,0:T(8,128)(2,1)S(1)} %get-tuple-element.21.rest_0_, bf16[1552,128]{1,0:T(8,128)(2,1)S(1)} %collective-permute-done.rest_1_, bf16[1552,128]{1,0:T(8,128)(2,1)S(1)} %collective-permute-done.3.rest_2_, ...), custom_call_target="tpu_custom_call" | custom-call | flops 30000001024 | bytes 1 | tf_op jit(solution)/shard_map/score_1/pallas_call | solution.py:254
  58.7 0.4 collective-permute-start.12
  59.2 1.1 %collective-permute-done.12.rest_13_.rest_14_ = bf16[768,128]{1,0:T(8,128)(2,1)S(1)} collective-permute-done((bf16[768,128]{1,0:T(8,128)(2,1)S(1)}, bf16[768,128]{1,0:T(8,128)(2,1)S(1)}, u32[]{:S(2)}, u32[]{:S(2)}) %collective-permute-start.12) | collective-permute-done | bytes 196640 | tf_op jit(solution)/shard_map/ppermute | solution.py:215
  60.3 3.0 %score_2.1.prev_ref = f32[8,192]{1,0:T(8,128)S(1)} custom-call(s32[1]{0:T(128)} %bitcast.1.me_ref, f32[8,192]{1,0:T(8,128)S(1)} %score_1.1.prev_ref, bf16[1552,128]{1,0:T(8,128)(2,1)S(1)} %get-tuple-element.21.rest_0_, bf16[1552,128]{1,0:T(8,128)(2,1)S(1)} %collective-permute-done.rest_1_, bf16[1552,128]{1,0:T(8,128)(2,1)S(1)} %collective-permute-done.3.rest_2_, ...), custom_call_target="tpu_custom_call" | custom-call | flops 1 | bytes 1 | tf_op jit(solution)/shard_map/score_2/pallas_call | solution.py:254
  63.3 0.7 collective-permute-done.14.rest_7_
  64.1 1.8 %score_3.1.prev_ref = f32[8,192]{1,0:T(8,128)S(1)} custom-call(s32[1]{0:T(128)} %bitcast.1.me_ref, f32[8,192]{1,0:T(8,128)S(1)} %score_2.1.prev_ref, bf16[1552,128]{1,0:T(8,128)(2,1)S(1)} %get-tuple-element.21.rest_0_, bf16[1552,128]{1,0:T(8,128)(2,1)S(1)} %collective-permute-done.rest_1_, bf16[1552,128]{1,0:T(8,128)(2,1)S(1)} %collective-permute-done.3.rest_2_, ...), custom_call_target="tpu_custom_call" | custom-call | flops 30000001024 | bytes 1 | tf_op jit(solution)/shard_map/score_3/pallas_call | solution.py:254
  65.9 1.5 %score_final.1 = f32[8,192]{1,0:T(8,128)S(1)} custom-call(s32[1]{0:T(128)} %bitcast.1.me_ref, f32[8,192]{1,0:T(8,128)S(1)} %score_3.1.prev_ref, bf16[1552,128]{1,0:T(8,128)(2,1)S(1)} %get-tuple-element.21.rest_0_, bf16[1552,128]{1,0:T(8,128)(2,1)S(1)} %collective-permute-done.rest_1_, bf16[1552,128]{1,0:T(8,128)(2,1)S(1)} %collective-permute-done.3.rest_2_, ...), custom_call_target="tpu_custom_call" | custom-call | flops 30000001024 | bytes 1 | tf_op jit(solution)/shard_map/score_final/pallas_call | solution.py:254
  67.4 23.4 %all_to_all.11 = f32[8,1,192]{2,1,0:T(1,128)S(1)} all-to-all(f32[8,1,192]{2,1,0:T(1,128)S(1)} %copy.4), channel_id=1, replica_groups=mesh['parts'=2,'wide'=8,'narrow'=2] {'wide'}, dimensions={0} | all-to-all | bytes 12288 | tf_op jit(solution)/shard_map/all_to_all | solution.py:283
  90.9 0.8 select.1
  (27 shorter events, 0.6 us)
Async XLA Ops:
  0.0 6.3 %copy-start = (bf16[768,1024]{1,0:T(8,128)(2,1)S(1)}, bf16[768,1024]{1,0:T(8,128)(2,1)}, u32[]{:S(2)}) copy-start(bf16[768,1024]{1,0:T(8,128)(2,1)} %emb_ref.3) | copy-start | bytes 4718596
  0.0 6.3 %copy-start.1 = (s32[768,1]{0,1:T(1,128)S(1)}, s32[768,1]{0,1:T(1,128)}, u32[]{:S(2)}) copy-start(s32[768,1]{0,1:T(1,128)} %param.4) | copy-start | bytes 9220
  2.2 31.3 %collective-permute-start = (bf16[1552,128]{1,0:T(8,128)(2,1)S(1)}, bf16[1552,128]{1,0:T(8,128)(2,1)S(1)}, u32[]{:S(2)}, u32[]{:S(2)}) collective-permute-start(bf16[1552,128]{1,0:T(8,128)(2,1)S(1)} %get-tuple-element.22), channel_id=1, source_target_pairs={{0,8},{2,10},{4,12},{6,14},{8,0},{10,2},{12,4},{14,6},{1,9},{3,11}... | collective-permute-start | bytes 1191944 | tf_op jit(solution)/shard_map/ppermute | solution.py:218
  7.5 34.6 %collective-permute-start.3 = (bf16[1552,128]{1,0:T(8,128)(2,1)S(1)}, bf16[1552,128]{1,0:T(8,128)(2,1)S(1)}, u32[]{:S(2)}, u32[]{:S(2)}) collective-permute-start(bf16[1552,128]{1,0:T(8,128)(2,1)S(1)} %get-tuple-element.23), channel_id=1, source_target_pairs={{0,10},{2,8},{4,14},{6,12},{8,2},{10,0},{12,6},{14,4},{1,11},{3,9}... | collective-permute-start | bytes 1191944 | tf_op jit(solution)/shard_map/ppermute | solution.py:218
  10.4 31.7 %collective-permute-start.4 = (bf16[1552,128]{1,0:T(8,128)(2,1)S(1)}, bf16[1552,128]{1,0:T(8,128)(2,1)S(1)}, u32[]{:S(2)}, u32[]{:S(2)}) collective-permute-start(bf16[1552,128]{1,0:T(8,128)(2,1)S(1)} %get-tuple-element.24), channel_id=1, source_target_pairs={{0,2},{2,0},{4,6},{6,4},{8,10},{10,8},{12,14},{14,12},{1,3},{3,1},... | collective-permute-start | bytes 1191944 | tf_op jit(solution)/shard_map/ppermute | solution.py:218
  10.7 34.9 %collective-permute-start.5 = (bf16[1552,128]{1,0:T(8,128)(2,1)S(1)}, bf16[1552,128]{1,0:T(8,128)(2,1)S(1)}, u32[]{:S(2)}, u32[]{:S(2)}) collective-permute-start(bf16[1552,128]{1,0:T(8,128)(2,1)S(1)} %get-tuple-element.25), channel_id=1, source_target_pairs={{0,4},{2,6},{4,0},{6,2},{8,12},{10,14},{12,8},{14,10},{1,5},{3,7},... | collective-permute-start | bytes 1191944 | tf_op jit(solution)/shard_map/ppermute | solution.py:218
  12.5 33.9 %collective-permute-start.6 = (bf16[1552,128]{1,0:T(8,128)(2,1)S(1)}, bf16[1552,128]{1,0:T(8,128)(2,1)S(1)}, u32[]{:S(2)}, u32[]{:S(2)}) collective-permute-start(bf16[1552,128]{1,0:T(8,128)(2,1)S(1)} %get-tuple-element.26), channel_id=1, source_target_pairs={{0,6},{2,4},{4,2},{6,0},{8,14},{10,12},{12,10},{14,8},{1,7},{3,5},... | collective-permute-start | bytes 1191944 | tf_op jit(solution)/shard_map/ppermute | solution.py:218
  33.4 13.0 %collective-permute-start.1 = (bf16[1552,128]{1,0:T(8,128)(2,1)S(1)}, bf16[1552,128]{1,0:T(8,128)(2,1)S(1)}, u32[]{:S(2)}, u32[]{:S(2)}) collective-permute-start(bf16[1552,128]{1,0:T(8,128)(2,1)S(1)} %get-tuple-element.21.rest_0_), channel_id=1, source_target_pairs={{0,1},{1,0},{2,3},{3,2},{4,5},{5,4},{6,7},{7,6},{8,9},{9,8},{10,11... | collective-permute-start | bytes 1191944 | tf_op jit(solution)/shard_map/ppermute | solution.py:215
  42.1 4.8 %collective-permute-start.2 = (bf16[1552,128]{1,0:T(8,128)(2,1)S(1)}, bf16[1552,128]{1,0:T(8,128)(2,1)S(1)}, u32[]{:S(2)}, u32[]{:S(2)}) collective-permute-start(bf16[1552,128]{1,0:T(8,128)(2,1)S(1)} %collective-permute-done.rest_1_), channel_id=1, source_target_pairs={{0,1},{1,0},{2,3},{3,2},{4,5},{5,4},{6,7},{7,6},{8,9},{9,8},{10,11... | collective-permute-start | bytes 1191944 | tf_op jit(solution)/shard_map/ppermute | solution.py:215
  42.1 16.3 %collective-permute-start.11 = (bf16[1552,128]{1,0:T(8,128)(2,1)S(1)}, bf16[1552,128]{1,0:T(8,128)(2,1)S(1)}, u32[]{:S(2)}, u32[]{:S(2)}) collective-permute-start(bf16[1552,128]{1,0:T(8,128)(2,1)S(1)} %get-tuple-element.28), channel_id=1, source_target_pairs={{0,12},{2,14},{4,8},{6,10},{8,4},{10,6},{12,0},{14,2},{1,13},{3,15... | collective-permute-start | bytes 1191944 | tf_op jit(solution)/shard_map/ppermute | solution.py:218
  45.6 2.5 %collective-permute-start.7 = (bf16[1552,128]{1,0:T(8,128)(2,1)S(1)}, bf16[1552,128]{1,0:T(8,128)(2,1)S(1)}, u32[]{:S(2)}, u32[]{:S(2)}) collective-permute-start(bf16[1552,128]{1,0:T(8,128)(2,1)S(1)} %collective-permute-done.3.rest_2_), channel_id=1, source_target_pairs={{0,1},{1,0},{2,3},{3,2},{4,5},{5,4},{6,7},{7,6},{8,9},{9,8},{10,11... | collective-permute-start | bytes 1191944 | tf_op jit(solution)/shard_map/ppermute | solution.py:215
  46.5 6.2 %collective-permute-start.8 = (bf16[1552,128]{1,0:T(8,128)(2,1)S(1)}, bf16[1552,128]{1,0:T(8,128)(2,1)S(1)}, u32[]{:S(2)}, u32[]{:S(2)}) collective-permute-start(bf16[1552,128]{1,0:T(8,128)(2,1)S(1)} %collective-permute-done.4.rest_3_), channel_id=1, source_target_pairs={{0,1},{1,0},{2,3},{3,2},{4,5},{5,4},{6,7},{7,6},{8,9},{9,8},{10,11... | collective-permute-start | bytes 1191944 | tf_op jit(solution)/shard_map/ppermute | solution.py:215
  46.5 6.2 %collective-permute-start.9 = (bf16[1552,128]{1,0:T(8,128)(2,1)S(1)}, bf16[1552,128]{1,0:T(8,128)(2,1)S(1)}, u32[]{:S(2)}, u32[]{:S(2)}) collective-permute-start(bf16[1552,128]{1,0:T(8,128)(2,1)S(1)} %collective-permute-done.5.rest_4_), channel_id=1, source_target_pairs={{0,1},{1,0},{2,3},{3,2},{4,5},{5,4},{6,7},{7,6},{8,9},{9,8},{10,11... | collective-permute-start | bytes 1191944 | tf_op jit(solution)/shard_map/ppermute | solution.py:215
  47.0 5.7 %collective-permute-start.10 = (bf16[1552,128]{1,0:T(8,128)(2,1)S(1)}, bf16[1552,128]{1,0:T(8,128)(2,1)S(1)}, u32[]{:S(2)}, u32[]{:S(2)}) collective-permute-start(bf16[1552,128]{1,0:T(8,128)(2,1)S(1)} %collective-permute-done.6.rest_5_), channel_id=1, source_target_pairs={{0,1},{1,0},{2,3},{3,2},{4,5},{5,4},{6,7},{7,6},{8,9},{9,8},{10,11... | collective-permute-start | bytes 1191944 | tf_op jit(solution)/shard_map/ppermute | solution.py:215
  48.1 15.9 %collective-permute-start.14 = (bf16[1552,128]{1,0:T(8,128)(2,1)S(1)}, bf16[1552,128]{1,0:T(8,128)(2,1)S(1)}, u32[]{:S(2)}, u32[]{:S(2)}) collective-permute-start(bf16[1552,128]{1,0:T(8,128)(2,1)S(1)} %get-tuple-element.31), channel_id=1, source_target_pairs={{0,14},{2,12},{4,10},{6,8},{8,6},{10,4},{12,2},{14,0},{1,15},{3,13... | collective-permute-start | bytes 1191944 | tf_op jit(solution)/shard_map/ppermute | solution.py:218
  58.5 1.8 %collective-permute-start.13 = (bf16[784,128]{1,0:T(8,128)(2,1)S(1)}, bf16[784,128]{1,0:T(8,128)(2,1)S(1)}, u32[]{:S(2)}, u32[]{:S(2)}) collective-permute-start(bf16[784,128]{1,0:T(8,128)(2,1)S(1)} %slice.7), channel_id=1, source_target_pairs={{0,1},{1,0},{2,3},{3,2},{4,5},{5,4},{6,7},{7,6},{8,9},{9,8},{10,11... | collective-permute-start | bytes 602120 | tf_op jit(solution)/shard_map/ppermute | solution.py:215
  58.7 1.5 %collective-permute-start.12 = (bf16[768,128]{1,0:T(8,128)(2,1)S(1)}, bf16[768,128]{1,0:T(8,128)(2,1)S(1)}, u32[]{:S(2)}, u32[]{:S(2)}) collective-permute-start(bf16[768,128]{1,0:T(8,128)(2,1)S(1)} %slice.6), channel_id=1, source_target_pairs={{0,1},{1,0},{2,3},{3,2},{4,5},{5,4},{6,7},{7,6},{8,9},{9,8},{10,11... | collective-permute-start | bytes 589832 | tf_op jit(solution)/shard_map/ppermute | solution.py:215
  64.1 1.8 %collective-permute-start.15 = (bf16[1552,128]{1,0:T(8,128)(2,1)S(1)}, bf16[1552,128]{1,0:T(8,128)(2,1)S(1)}, u32[]{:S(2)}, u32[]{:S(2)}) collective-permute-start(bf16[1552,128]{1,0:T(8,128)(2,1)S(1)} %collective-permute-done.14.rest_7_), channel_id=1, source_target_pairs={{0,1},{1,0},{2,3},{3,2},{4,5},{5,4},{6,7},{7,6},{8,9},{9,8},{10,11... | collective-permute-start | bytes 1191944 | tf_op jit(solution)/shard_map/ppermute | solution.py:215

commit v7 on v6

--- a/solution.py
+++ b/solution.py
@@ -231,8 +231,9 @@
             name=name,
         )(me, embeddings, lab, pos, ranks)
 
-    far_blocks += pack_rest(far[quarter:], "pack_far")
-    near_blocks = pack_rest(near, "pack_near")
+    later = pack_rest(far[quarter:] + near, "pack_rest")
+    far_blocks += later[: -len(near)]
+    near_blocks = later[-len(near) :]
     own = {}
     for i, piece in enumerate(far):
         out = far_blocks[i]

time: 91.9 us -> 91.9 us (level)
    pallas_call x2 -> x1, Pallas kernels: 2.74 us -> 2.47 us  [pack_rest(): pl.pallas_call(functools.partial(_pack_rest, pieces, groups), out_shape=[...]
  transfers between devices with their start and end apart: 16 -> 16, of which waited for: 5 -> 5; matrix products, arithmetic and copies ran while one was open for 0% -> 0% of each run, Pallas kernels for 16% -> 15%
where the time goes in v7:
time: 91.9 us; the launch traced here: 91.7 us
  waiting for transfers between devices  31 us (34%)
  blocking collectives  23.4 us (25%)
  Pallas kernels  18.7 us (20%)
  starting transfers between devices  18.5 us (20%)
    ppermute x7, waiting for transfers between devices, send(): return lax.ppermute(x, 'wide', [(s, s ^ r) for s in range(groups)])  29.8 us
    all_to_all x1, blocking collectives, local(): lax.all_to_all(best, 'wide', split_axis=0, concat_axis=0, tiled=True)  23.4 us
    ppermute x7, starting transfers between devices, send(): return lax.ppermute(x, 'wide', [(s, s ^ r) for s in range(groups)])  17 us
    pallas_call x5, Pallas kernels, score(): pl.pallas_call(functools.partial(_score, pieces, jobs, len(partners), n_o...  13.2 us
    pallas_call x1, Pallas kernels, pack_rest(): pl.pallas_call(functools.partial(_pack_rest, pieces, groups), out_shape=[...  2.47 us
    pallas_call x1, Pallas kernels, local(): pl.pallas_call(functools.partial(_pack_first, far[:quarter], groups, slot...  2.16 us
  transfers between devices with their start and end apart: 16, of which 5 were waited for; matrix products, arithmetic and copies ran while one was open for 0% of the time, Pallas kernels for 15%

profile of v7, /device:TPU:0, one launch (start us, length us, event | category | flops | bytes accessed | tf_op | source)
XLA Modules:
  0.0 91.7 jit_solution(10494868537972024019)
XLA Ops:
  0.0 2.2 %pack_first.1 = (s32[1,768]{1,0:T(1,128)S(1)}, f32[16,256]{1,0:T(8,128)S(1)}, bf16[1552,128]{1,0:T(8,128)(2,1)S(1)}) custom-call(s32[1]{0:T(128)} %bitcast.1.me_ref, bf16[768,1024]{1,0:T(8,128)(2,1)} %emb_ref.1, s32[1,768]{1,0:T(1,128)} %bitcast.8, s32[6,128]{1,0:T(8,128)} %bitcast.12), custom_call_target="tpu_custom_call" | custom-call | tf_op jit(solution)/shard_map/pack_first/pallas_call | solution.py:194
  2.2 4.1 %collective-permute-start = (bf16[1552,128]{1,0:T(8,128)(2,1)S(1)}, bf16[1552,128]{1,0:T(8,128)(2,1)S(1)}, u32[]{:S(2)}, u32[]{:S(2)}) collective-permute-start(bf16[1552,128]{1,0:T(8,128)(2,1)S(1)} %get-tuple-element.22), channel_id=1, source_target_pairs={{0,8},{2,10},{4,12},{6,14},{8,0},{10,2},{12,4},{14,6},{1,9},{3,11}... | collective-permute-start | bytes 1191944 | tf_op jit(solution)/shard_map/ppermute | solution.py:218
  6.3 2.5 %pack_rest.1 = (bf16[1552,128]{1,0:T(8,128)(2,1)S(1)}, bf16[1552,128]{1,0:T(8,128)(2,1)S(1)}, bf16[1552,128]{1,0:T(8,128)(2,1)S(1)}, bf16[1552,128]{1,0:T(8,128)...) custom-call(s32[1]{0:T(128)} %bitcast.1.me_ref, ...), custom_call_target="tpu_custom_call" | custom-call | flops 30000001024 | bytes 1 | tf_op jit(solution)/shard_map/pack_rest/pallas_call | solution.py:224
  8.8 1.4 %collective-permute-start.3 = (bf16[1552,128]{1,0:T(8,128)(2,1)S(1)}, bf16[1552,128]{1,0:T(8,128)(2,1)S(1)}, u32[]{:S(2)}, u32[]{:S(2)}) collective-permute-start(bf16[1552,128]{1,0:T(8,128)(2,1)S(1)} %get-tuple-element.23), channel_id=1, source_target_pairs={{0,10},{2,8},{4,14},{6,12},{8,2},{10,0},{12,6},{14,4},{1,11},{3,9}... | collective-permute-start | bytes 1191944 | tf_op jit(solution)/shard_map/ppermute | solution.py:218
  10.1 0.3 collective-permute-start.4
  10.4 1.8 %collective-permute-start.5 = (bf16[1552,128]{1,0:T(8,128)(2,1)S(1)}, bf16[1552,128]{1,0:T(8,128)(2,1)S(1)}, u32[]{:S(2)}, u32[]{:S(2)}) collective-permute-start(bf16[1552,128]{1,0:T(8,128)(2,1)S(1)} %get-tuple-element.25), channel_id=1, source_target_pairs={{0,4},{2,6},{4,0},{6,2},{8,12},{10,14},{12,8},{14,10},{1,5},{3,7},... | collective-permute-start | bytes 1191944 | tf_op jit(solution)/shard_map/ppermute | solution.py:218
  12.2 1.4 %collective-permute-start.6 = (bf16[1552,128]{1,0:T(8,128)(2,1)S(1)}, bf16[1552,128]{1,0:T(8,128)(2,1)S(1)}, u32[]{:S(2)}, u32[]{:S(2)}) collective-permute-start(bf16[1552,128]{1,0:T(8,128)(2,1)S(1)} %get-tuple-element.26), channel_id=1, source_target_pairs={{0,6},{2,4},{4,2},{6,0},{8,14},{10,12},{12,10},{14,8},{1,7},{3,5},... | collective-permute-start | bytes 1191944 | tf_op jit(solution)/shard_map/ppermute | solution.py:218
  13.6 19.8 %collective-permute-done.rest_1_ = bf16[1552,128]{1,0:T(8,128)(2,1)S(1)} collective-permute-done((bf16[1552,128]{1,0:T(8,128)(2,1)S(1)}, bf16[1552,128]{1,0:T(8,128)(2,1)S(1)}, u32[]{:S(2)}, u32[]{:S(2)}) %collective-permute-start) | collective-permute-done | bytes 397344 | tf_op jit(solution)/shard_map/ppermute | solution.py:218
  33.4 8.7 %collective-permute-done.3.rest_2_ = bf16[1552,128]{1,0:T(8,128)(2,1)S(1)} collective-permute-done((bf16[1552,128]{1,0:T(8,128)(2,1)S(1)}, bf16[1552,128]{1,0:T(8,128)(2,1)S(1)}, u32[]{:S(2)}, u32[]{:S(2)}) %collective-permute-start.3) | collective-permute-done | bytes 397344 | tf_op jit(solution)/shard_map/ppermute | solution.py:218
  42.1 3.5 %collective-permute-start.11 = (bf16[1552,128]{1,0:T(8,128)(2,1)S(1)}, bf16[1552,128]{1,0:T(8,128)(2,1)S(1)}, u32[]{:S(2)}, u32[]{:S(2)}) collective-permute-start(bf16[1552,128]{1,0:T(8,128)(2,1)S(1)} %get-tuple-element.28), channel_id=1, source_target_pairs={{0,12},{2,14},{4,8},{6,10},{8,4},{10,6},{12,0},{14,2},{1,13},{3,15... | collective-permute-start | bytes 1191944 | tf_op jit(solution)/shard_map/ppermute | solution.py:218
  45.9 0.3 collective-permute-done.6.rest_5_
  46.1 0.5 collective-permute-start.9
  46.7 1.1 %score_0.1.prev_ref = f32[8,192]{1,0:T(8,128)S(1)} custom-call(s32[1]{0:T(128)} %bitcast.1.me_ref, f32[8,192]{1,0:T(8,128)S(1)} %broadcast_in_dim.3.prev_ref, bf16[1552,128]{1,0:T(8,128)(2,1)S(1)} %get-tuple-element.21.rest_0_, bf16[1552,128]{1,0:T(8,128)(2,1)S(1)} %collective-permute-done.rest_1_, ...), custom_call_target="tpu_custom_call" | custom-call | flops 10000000000 | bytes 1 | tf_op jit(solution)/shard_map/score_0/pallas_call | solution.py:255
  47.8 4.6 %collective-permute-start.14 = (bf16[1552,128]{1,0:T(8,128)(2,1)S(1)}, bf16[1552,128]{1,0:T(8,128)(2,1)S(1)}, u32[]{:S(2)}, u32[]{:S(2)}) collective-permute-start(bf16[1552,128]{1,0:T(8,128)(2,1)S(1)} %get-tuple-element.31), channel_id=1, source_target_pairs={{0,14},{2,12},{4,10},{6,8},{8,6},{10,4},{12,2},{14,0},{1,15},{3,13... | collective-permute-start | bytes 1191944 | tf_op jit(solution)/shard_map/ppermute | solution.py:218
  52.4 5.8 %score_1.1.prev_ref = f32[8,192]{1,0:T(8,128)S(1)} custom-call(s32[1]{0:T(128)} %bitcast.1.me_ref, f32[8,192]{1,0:T(8,128)S(1)} %score_0.1.prev_ref, bf16[1552,128]{1,0:T(8,128)(2,1)S(1)} %get-tuple-element.21.rest_0_, bf16[1552,128]{1,0:T(8,128)(2,1)S(1)} %collective-permute-done.rest_1_, bf16[1552,128]{1,0:T(8,128)(2,1)S(1)} %collective-permute-done.3.rest_2_, ...), custom_call_target="tpu_custom_call" | custom-call | flops 30000001024 | bytes 1 | tf_op jit(solution)/shard_map/score_1/pallas_call | solution.py:255
  58.2 0.2 collective-permute-start.13
  58.4 0.4 collective-permute-start.12
  58.8 1.1 %collective-permute-done.12.rest_13_.rest_14_ = bf16[768,128]{1,0:T(8,128)(2,1)S(1)} collective-permute-done((bf16[768,128]{1,0:T(8,128)(2,1)S(1)}, bf16[768,128]{1,0:T(8,128)(2,1)S(1)}, u32[]{:S(2)}, u32[]{:S(2)}) %collective-permute-start.12) | collective-permute-done | bytes 196640 | tf_op jit(solution)/shard_map/ppermute | solution.py:215
  60.0 3.0 %score_2.1.prev_ref = f32[8,192]{1,0:T(8,128)S(1)} custom-call(s32[1]{0:T(128)} %bitcast.1.me_ref, f32[8,192]{1,0:T(8,128)S(1)} %score_1.1.prev_ref, bf16[1552,128]{1,0:T(8,128)(2,1)S(1)} %get-tuple-element.21.rest_0_, bf16[1552,128]{1,0:T(8,128)(2,1)S(1)} %collective-permute-done.rest_1_, bf16[1552,128]{1,0:T(8,128)(2,1)S(1)} %collective-permute-done.3.rest_2_, ...), custom_call_target="tpu_custom_call" | custom-call | flops 1 | bytes 1 | tf_op jit(solution)/shard_map/score_2/pallas_call | solution.py:255
  63.0 1.0 %collective-permute-done.14.rest_7_ = bf16[1552,128]{1,0:T(8,128)(2,1)S(1)} collective-permute-done((bf16[1552,128]{1,0:T(8,128)(2,1)S(1)}, bf16[1552,128]{1,0:T(8,128)(2,1)S(1)}, u32[]{:S(2)}, u32[]{:S(2)}) %collective-permute-start.14) | collective-permute-done | bytes 397344 | tf_op jit(solution)/shard_map/ppermute | solution.py:218
  64.1 1.8 %score_3.1.prev_ref = f32[8,192]{1,0:T(8,128)S(1)} custom-call(s32[1]{0:T(128)} %bitcast.1.me_ref, f32[8,192]{1,0:T(8,128)S(1)} %score_2.1.prev_ref, bf16[1552,128]{1,0:T(8,128)(2,1)S(1)} %get-tuple-element.21.rest_0_, bf16[1552,128]{1,0:T(8,128)(2,1)S(1)} %collective-permute-done.rest_1_, bf16[1552,128]{1,0:T(8,128)(2,1)S(1)} %collective-permute-done.3.rest_2_, ...), custom_call_target="tpu_custom_call" | custom-call | flops 30000001024 | bytes 1 | tf_op jit(solution)/shard_map/score_3/pallas_call | solution.py:255
  65.9 1.5 %score_final.1 = f32[8,192]{1,0:T(8,128)S(1)} custom-call(s32[1]{0:T(128)} %bitcast.1.me_ref, f32[8,192]{1,0:T(8,128)S(1)} %score_3.1.prev_ref, bf16[1552,128]{1,0:T(8,128)(2,1)S(1)} %get-tuple-element.21.rest_0_, bf16[1552,128]{1,0:T(8,128)(2,1)S(1)} %collective-permute-done.rest_1_, bf16[1552,128]{1,0:T(8,128)(2,1)S(1)} %collective-permute-done.3.rest_2_, ...), custom_call_target="tpu_custom_call" | custom-call | flops 30000001024 | bytes 1 | tf_op jit(solution)/shard_map/score_final/pallas_call | solution.py:255
  67.4 23.4 %all_to_all.11 = f32[8,1,192]{2,1,0:T(1,128)S(1)} all-to-all(f32[8,1,192]{2,1,0:T(1,128)S(1)} %copy.4), channel_id=1, replica_groups=mesh['parts'=2,'wide'=8,'narrow'=2] {'wide'}, dimensions={0} | all-to-all | bytes 12288 | tf_op jit(solution)/shard_map/all_to_all | solution.py:284
  90.8 0.8 select.1
  (26 shorter events, 0.4 us)
Async XLA Ops:
  0.0 6.3 %copy-start = (bf16[768,1024]{1,0:T(8,128)(2,1)S(1)}, bf16[768,1024]{1,0:T(8,128)(2,1)}, u32[]{:S(2)}) copy-start(bf16[768,1024]{1,0:T(8,128)(2,1)} %emb_ref.1) | copy-start | bytes 4718596
  0.0 6.3 %copy-start.1 = (s32[768,1]{0,1:T(1,128)S(1)}, s32[768,1]{0,1:T(1,128)}, u32[]{:S(2)}) copy-start(s32[768,1]{0,1:T(1,128)} %param.4) | copy-start | bytes 9220
  2.2 31.3 %collective-permute-start = (bf16[1552,128]{1,0:T(8,128)(2,1)S(1)}, bf16[1552,128]{1,0:T(8,128)(2,1)S(1)}, u32[]{:S(2)}, u32[]{:S(2)}) collective-permute-start(bf16[1552,128]{1,0:T(8,128)(2,1)S(1)} %get-tuple-element.22), channel_id=1, source_target_pairs={{0,8},{2,10},{4,12},{6,14},{8,0},{10,2},{12,4},{14,6},{1,9},{3,11}... | collective-permute-start | bytes 1191944 | tf_op jit(solution)/shard_map/ppermute | solution.py:218
  8.8 33.4 %collective-permute-start.3 = (bf16[1552,128]{1,0:T(8,128)(2,1)S(1)}, bf16[1552,128]{1,0:T(8,128)(2,1)S(1)}, u32[]{:S(2)}, u32[]{:S(2)}) collective-permute-start(bf16[1552,128]{1,0:T(8,128)(2,1)S(1)} %get-tuple-element.23), channel_id=1, source_target_pairs={{0,10},{2,8},{4,14},{6,12},{8,2},{10,0},{12,6},{14,4},{1,11},{3,9}... | collective-permute-start | bytes 1191944 | tf_op jit(solution)/shard_map/ppermute | solution.py:218
  10.1 32.0 %collective-permute-start.4 = (bf16[1552,128]{1,0:T(8,128)(2,1)S(1)}, bf16[1552,128]{1,0:T(8,128)(2,1)S(1)}, u32[]{:S(2)}, u32[]{:S(2)}) collective-permute-start(bf16[1552,128]{1,0:T(8,128)(2,1)S(1)} %get-tuple-element.24), channel_id=1, source_target_pairs={{0,2},{2,0},{4,6},{6,4},{8,10},{10,8},{12,14},{14,12},{1,3},{3,1},... | collective-permute-start | bytes 1191944 | tf_op jit(solution)/shard_map/ppermute | solution.py:218
  10.4 35.2 %collective-permute-start.5 = (bf16[1552,128]{1,0:T(8,128)(2,1)S(1)}, bf16[1552,128]{1,0:T(8,128)(2,1)S(1)}, u32[]{:S(2)}, u32[]{:S(2)}) collective-permute-start(bf16[1552,128]{1,0:T(8,128)(2,1)S(1)} %get-tuple-element.25), channel_id=1, source_target_pairs={{0,4},{2,6},{4,0},{6,2},{8,12},{10,14},{12,8},{14,10},{1,5},{3,7},... | collective-permute-start | bytes 1191944 | tf_op jit(solution)/shard_map/ppermute | solution.py:218
  12.2 33.9 %collective-permute-start.6 = (bf16[1552,128]{1,0:T(8,128)(2,1)S(1)}, bf16[1552,128]{1,0:T(8,128)(2,1)S(1)}, u32[]{:S(2)}, u32[]{:S(2)}) collective-permute-start(bf16[1552,128]{1,0:T(8,128)(2,1)S(1)} %get-tuple-element.26), channel_id=1, source_target_pairs={{0,6},{2,4},{4,2},{6,0},{8,14},{10,12},{12,10},{14,8},{1,7},{3,5},... | collective-permute-start | bytes 1191944 | tf_op jit(solution)/shard_map/ppermute | solution.py:218
  33.4 12.7 %collective-permute-start.1 = (bf16[1552,128]{1,0:T(8,128)(2,1)S(1)}, bf16[1552,128]{1,0:T(8,128)(2,1)S(1)}, u32[]{:S(2)}, u32[]{:S(2)}) collective-permute-start(bf16[1552,128]{1,0:T(8,128)(2,1)S(1)} %get-tuple-element.21.rest_0_), channel_id=1, source_target_pairs={{0,1},{1,0},{2,3},{3,2},{4,5},{5,4},{6,7},{7,6},{8,9},{9,8},{10,11... | collective-permute-start | bytes 1191944 | tf_op jit(solution)/shard_map/ppermute | solution.py:215
  42.1 4.5 %collective-permute-start.2 = (bf16[1552,128]{1,0:T(8,128)(2,1)S(1)}, bf16[1552,128]{1,0:T(8,128)(2,1)S(1)}, u32[]{:S(2)}, u32[]{:S(2)}) collective-permute-start(bf16[1552,128]{1,0:T(8,128)(2,1)S(1)} %collective-permute-done.rest_1_), channel_id=1, source_target_pairs={{0,1},{1,0},{2,3},{3,2},{4,5},{5,4},{6,7},{7,6},{8,9},{9,8},{10,11... | collective-permute-start | bytes 1191944 | tf_op jit(solution)/shard_map/ppermute | solution.py:215
  42.1 16.0 %collective-permute-start.11 = (bf16[1552,128]{1,0:T(8,128)(2,1)S(1)}, bf16[1552,128]{1,0:T(8,128)(2,1)S(1)}, u32[]{:S(2)}, u32[]{:S(2)}) collective-permute-start(bf16[1552,128]{1,0:T(8,128)(2,1)S(1)} %get-tuple-element.28), channel_id=1, source_target_pairs={{0,12},{2,14},{4,8},{6,10},{8,4},{10,6},{12,0},{14,2},{1,13},{3,15... | collective-permute-start | bytes 1191944 | tf_op jit(solution)/shard_map/ppermute | solution.py:218
  45.6 2.2 %collective-permute-start.7 = (bf16[1552,128]{1,0:T(8,128)(2,1)S(1)}, bf16[1552,128]{1,0:T(8,128)(2,1)S(1)}, u32[]{:S(2)}, u32[]{:S(2)}) collective-permute-start(bf16[1552,128]{1,0:T(8,128)(2,1)S(1)} %collective-permute-done.3.rest_2_), channel_id=1, source_target_pairs={{0,1},{1,0},{2,3},{3,2},{4,5},{5,4},{6,7},{7,6},{8,9},{9,8},{10,11... | collective-permute-start | bytes 1191944 | tf_op jit(solution)/shard_map/ppermute | solution.py:215
  46.1 6.2 %collective-permute-start.8 = (bf16[1552,128]{1,0:T(8,128)(2,1)S(1)}, bf16[1552,128]{1,0:T(8,128)(2,1)S(1)}, u32[]{:S(2)}, u32[]{:S(2)}) collective-permute-start(bf16[1552,128]{1,0:T(8,128)(2,1)S(1)} %collective-permute-done.4.rest_3_), channel_id=1, source_target_pairs={{0,1},{1,0},{2,3},{3,2},{4,5},{5,4},{6,7},{7,6},{8,9},{9,8},{10,11... | collective-permute-start | bytes 1191944 | tf_op jit(solution)/shard_map/ppermute | solution.py:215
  46.1 6.2 %collective-permute-start.9 = (bf16[1552,128]{1,0:T(8,128)(2,1)S(1)}, bf16[1552,128]{1,0:T(8,128)(2,1)S(1)}, u32[]{:S(2)}, u32[]{:S(2)}) collective-permute-start(bf16[1552,128]{1,0:T(8,128)(2,1)S(1)} %collective-permute-done.5.rest_4_), channel_id=1, source_target_pairs={{0,1},{1,0},{2,3},{3,2},{4,5},{5,4},{6,7},{7,6},{8,9},{9,8},{10,11... | collective-permute-start | bytes 1191944 | tf_op jit(solution)/shard_map/ppermute | solution.py:215
  46.6 5.7 %collective-permute-start.10 = (bf16[1552,128]{1,0:T(8,128)(2,1)S(1)}, bf16[1552,128]{1,0:T(8,128)(2,1)S(1)}, u32[]{:S(2)}, u32[]{:S(2)}) collective-permute-start(bf16[1552,128]{1,0:T(8,128)(2,1)S(1)} %collective-permute-done.6.rest_5_), channel_id=1, source_target_pairs={{0,1},{1,0},{2,3},{3,2},{4,5},{5,4},{6,7},{7,6},{8,9},{9,8},{10,11... | collective-permute-start | bytes 1191944 | tf_op jit(solution)/shard_map/ppermute | solution.py:215
  47.8 16.3 %collective-permute-start.14 = (bf16[1552,128]{1,0:T(8,128)(2,1)S(1)}, bf16[1552,128]{1,0:T(8,128)(2,1)S(1)}, u32[]{:S(2)}, u32[]{:S(2)}) collective-permute-start(bf16[1552,128]{1,0:T(8,128)(2,1)S(1)} %get-tuple-element.31), channel_id=1, source_target_pairs={{0,14},{2,12},{4,10},{6,8},{8,6},{10,4},{12,2},{14,0},{1,15},{3,13... | collective-permute-start | bytes 1191944 | tf_op jit(solution)/shard_map/ppermute | solution.py:218
  58.2 1.8 %collective-permute-start.13 = (bf16[784,128]{1,0:T(8,128)(2,1)S(1)}, bf16[784,128]{1,0:T(8,128)(2,1)S(1)}, u32[]{:S(2)}, u32[]{:S(2)}) collective-permute-start(bf16[784,128]{1,0:T(8,128)(2,1)S(1)} %slice.7), channel_id=1, source_target_pairs={{0,1},{1,0},{2,3},{3,2},{4,5},{5,4},{6,7},{7,6},{8,9},{9,8},{10,11... | collective-permute-start | bytes 602120 | tf_op jit(solution)/shard_map/ppermute | solution.py:215
  58.4 1.5 %collective-permute-start.12 = (bf16[768,128]{1,0:T(8,128)(2,1)S(1)}, bf16[768,128]{1,0:T(8,128)(2,1)S(1)}, u32[]{:S(2)}, u32[]{:S(2)}) collective-permute-start(bf16[768,128]{1,0:T(8,128)(2,1)S(1)} %slice.6), channel_id=1, source_target_pairs={{0,1},{1,0},{2,3},{3,2},{4,5},{5,4},{6,7},{7,6},{8,9},{9,8},{10,11... | collective-permute-start | bytes 589832 | tf_op jit(solution)/shard_map/ppermute | solution.py:215
  64.1 1.8 %collective-permute-start.15 = (bf16[1552,128]{1,0:T(8,128)(2,1)S(1)}, bf16[1552,128]{1,0:T(8,128)(2,1)S(1)}, u32[]{:S(2)}, u32[]{:S(2)}) collective-permute-start(bf16[1552,128]{1,0:T(8,128)(2,1)S(1)} %collective-permute-done.14.rest_7_), channel_id=1, source_target_pairs={{0,1},{1,0},{2,3},{3,2},{4,5},{5,4},{6,7},{7,6},{8,9},{9,8},{10,11... | collective-permute-start | bytes 1191944 | tf_op jit(solution)/shard_map/ppermute | solution.py:215

commit v8 on v7

--- a/solution.py
+++ b/solution.py
@@ -160,9 +160,8 @@
     b = rest.astype(jnp.bfloat16)
     c = (rest - b.astype(jnp.float32)).astype(jnp.bfloat16)
     pick = _as_bf16(lax.broadcasted_iota(jnp.int32, (slots, rows), 0) == pos_ref[...])
-    value = jnp.dot(a, pick, preferred_element_type=jnp.float32)
-    value += jnp.dot(b, pick, preferred_element_type=jnp.float32)
-    value += jnp.dot(c, pick, preferred_element_type=jnp.float32)
+    parts = jnp.dot(jnp.concatenate([a, b, c], axis=0), pick, preferred_element_type=jnp.float32)
+    value = parts[:groups] + parts[groups : 2 * groups] + parts[2 * groups :]
     mine = lax.broadcasted_iota(jnp.int32, (groups, rows), 0) == lab_ref[...]
     out_ref[...] = jnp.sum(jnp.where(mine, value, 0.0), axis=0)
 

time: 91.9 us -> 91.8 us (level)
  no operation moved by 1% of the time
where the time goes in v8:
time: 91.8 us; the launch traced here: 91.6 us
  waiting for transfers between devices  31 us (34%)
  blocking collectives  23.4 us (25%)
  Pallas kernels  18.6 us (20%)
  starting transfers between devices  18.5 us (20%)
    ppermute x7, waiting for transfers between devices, send(): return lax.ppermute(x, 'wide', [(s, s ^ r) for s in range(groups)])  29.8 us
    all_to_all x1, blocking collectives, local(): lax.all_to_all(best, 'wide', split_axis=0, concat_axis=0, tiled=True)  23.4 us
    ppermute x7, starting transfers between devices, send(): return lax.ppermute(x, 'wide', [(s, s ^ r) for s in range(groups)])  17 us
    pallas_call x5, Pallas kernels, score(): pl.pallas_call(functools.partial(_score, pieces, jobs, len(partners), n_o...  13.2 us
    pallas_call x1, Pallas kernels, pack_rest(): pl.pallas_call(functools.partial(_pack_rest, pieces, groups), out_shape=[...  2.47 us
    pallas_call x1, Pallas kernels, local(): pl.pallas_call(functools.partial(_pack_first, far[:quarter], groups, slot...  2.16 us
  transfers between devices with their start and end apart: 16, of which 5 were waited for; matrix products, arithmetic and copies ran while one was open for 0% of the time, Pallas kernels for 15%

profile of v8, /device:TPU:0, one launch (start us, length us, event | category | flops | bytes accessed | tf_op | source)
XLA Modules:
  0.0 91.6 jit_solution(13730269126986733445)
XLA Ops:
  0.0 2.2 %pack_first.1 = (s32[1,768]{1,0:T(1,128)S(1)}, f32[16,256]{1,0:T(8,128)S(1)}, bf16[1552,128]{1,0:T(8,128)(2,1)S(1)}) custom-call(s32[1]{0:T(128)} %bitcast.1.me_ref, bf16[768,1024]{1,0:T(8,128)(2,1)} %emb_ref.1, s32[1,768]{1,0:T(1,128)} %bitcast.8, s32[6,128]{1,0:T(8,128)} %bitcast.12), custom_call_target="tpu_custom_call" | custom-call | tf_op jit(solution)/shard_map/pack_first/pallas_call | solution.py:193
  2.2 4.1 %collective-permute-start = (bf16[1552,128]{1,0:T(8,128)(2,1)S(1)}, bf16[1552,128]{1,0:T(8,128)(2,1)S(1)}, u32[]{:S(2)}, u32[]{:S(2)}) collective-permute-start(bf16[1552,128]{1,0:T(8,128)(2,1)S(1)} %get-tuple-element.22), channel_id=1, source_target_pairs={{0,8},{2,10},{4,12},{6,14},{8,0},{10,2},{12,4},{14,6},{1,9},{3,11}... | collective-permute-start | bytes 1191944 | tf_op jit(solution)/shard_map/ppermute | solution.py:217
  6.3 2.5 %pack_rest.1 = (bf16[1552,128]{1,0:T(8,128)(2,1)S(1)}, bf16[1552,128]{1,0:T(8,128)(2,1)S(1)}, bf16[1552,128]{1,0:T(8,128)(2,1)S(1)}, bf16[1552,128]{1,0:T(8,128)...) custom-call(s32[1]{0:T(128)} %bitcast.1.me_ref, ...), custom_call_target="tpu_custom_call" | custom-call | flops 30000001024 | bytes 1 | tf_op jit(solution)/shard_map/pack_rest/pallas_call | solution.py:223
  8.8 1.4 %collective-permute-start.3 = (bf16[1552,128]{1,0:T(8,128)(2,1)S(1)}, bf16[1552,128]{1,0:T(8,128)(2,1)S(1)}, u32[]{:S(2)}, u32[]{:S(2)}) collective-permute-start(bf16[1552,128]{1,0:T(8,128)(2,1)S(1)} %get-tuple-element.23), channel_id=1, source_target_pairs={{0,10},{2,8},{4,14},{6,12},{8,2},{10,0},{12,6},{14,4},{1,11},{3,9}... | collective-permute-start | bytes 1191944 | tf_op jit(solution)/shard_map/ppermute | solution.py:217
  10.1 0.3 collective-permute-start.4
  10.4 1.8 %collective-permute-start.5 = (bf16[1552,128]{1,0:T(8,128)(2,1)S(1)}, bf16[1552,128]{1,0:T(8,128)(2,1)S(1)}, u32[]{:S(2)}, u32[]{:S(2)}) collective-permute-start(bf16[1552,128]{1,0:T(8,128)(2,1)S(1)} %get-tuple-element.25), channel_id=1, source_target_pairs={{0,4},{2,6},{4,0},{6,2},{8,12},{10,14},{12,8},{14,10},{1,5},{3,7},... | collective-permute-start | bytes 1191944 | tf_op jit(solution)/shard_map/ppermute | solution.py:217
  12.2 1.4 %collective-permute-start.6 = (bf16[1552,128]{1,0:T(8,128)(2,1)S(1)}, bf16[1552,128]{1,0:T(8,128)(2,1)S(1)}, u32[]{:S(2)}, u32[]{:S(2)}) collective-permute-start(bf16[1552,128]{1,0:T(8,128)(2,1)S(1)} %get-tuple-element.26), channel_id=1, source_target_pairs={{0,6},{2,4},{4,2},{6,0},{8,14},{10,12},{12,10},{14,8},{1,7},{3,5},... | collective-permute-start | bytes 1191944 | tf_op jit(solution)/shard_map/ppermute | solution.py:217
  13.6 19.8 %collective-permute-done.rest_1_ = bf16[1552,128]{1,0:T(8,128)(2,1)S(1)} collective-permute-done((bf16[1552,128]{1,0:T(8,128)(2,1)S(1)}, bf16[1552,128]{1,0:T(8,128)(2,1)S(1)}, u32[]{:S(2)}, u32[]{:S(2)}) %collective-permute-start) | collective-permute-done | bytes 397344 | tf_op jit(solution)/shard_map/ppermute | solution.py:217
  33.4 8.7 %collective-permute-done.3.rest_2_ = bf16[1552,128]{1,0:T(8,128)(2,1)S(1)} collective-permute-done((bf16[1552,128]{1,0:T(8,128)(2,1)S(1)}, bf16[1552,128]{1,0:T(8,128)(2,1)S(1)}, u32[]{:S(2)}, u32[]{:S(2)}) %collective-permute-start.3) | collective-permute-done | bytes 397344 | tf_op jit(solution)/shard_map/ppermute | solution.py:217
  42.1 3.5 %collective-permute-start.11 = (bf16[1552,128]{1,0:T(8,128)(2,1)S(1)}, bf16[1552,128]{1,0:T(8,128)(2,1)S(1)}, u32[]{:S(2)}, u32[]{:S(2)}) collective-permute-start(bf16[1552,128]{1,0:T(8,128)(2,1)S(1)} %get-tuple-element.28), channel_id=1, source_target_pairs={{0,12},{2,14},{4,8},{6,10},{8,4},{10,6},{12,0},{14,2},{1,13},{3,15... | collective-permute-start | bytes 1191944 | tf_op jit(solution)/shard_map/ppermute | solution.py:217
  45.9 0.3 collective-permute-done.6.rest_5_
  46.1 0.5 collective-permute-start.9
  46.7 1.1 %score_0.1.prev_ref = f32[8,192]{1,0:T(8,128)S(1)} custom-call(s32[1]{0:T(128)} %bitcast.1.me_ref, f32[8,192]{1,0:T(8,128)S(1)} %broadcast_in_dim.3.prev_ref, bf16[1552,128]{1,0:T(8,128)(2,1)S(1)} %get-tuple-element.21.rest_0_, bf16[1552,128]{1,0:T(8,128)(2,1)S(1)} %collective-permute-done.rest_1_, ...), custom_call_target="tpu_custom_call" | custom-call | flops 10000000000 | bytes 1 | tf_op jit(solution)/shard_map/score_0/pallas_call | solution.py:254
  47.8 4.6 %collective-permute-start.14 = (bf16[1552,128]{1,0:T(8,128)(2,1)S(1)}, bf16[1552,128]{1,0:T(8,128)(2,1)S(1)}, u32[]{:S(2)}, u32[]{:S(2)}) collective-permute-start(bf16[1552,128]{1,0:T(8,128)(2,1)S(1)} %get-tuple-element.31), channel_id=1, source_target_pairs={{0,14},{2,12},{4,10},{6,8},{8,6},{10,4},{12,2},{14,0},{1,15},{3,13... | collective-permute-start | bytes 1191944 | tf_op jit(solution)/shard_map/ppermute | solution.py:217
  52.4 5.8 %score_1.1.prev_ref = f32[8,192]{1,0:T(8,128)S(1)} custom-call(s32[1]{0:T(128)} %bitcast.1.me_ref, f32[8,192]{1,0:T(8,128)S(1)} %score_0.1.prev_ref, bf16[1552,128]{1,0:T(8,128)(2,1)S(1)} %get-tuple-element.21.rest_0_, bf16[1552,128]{1,0:T(8,128)(2,1)S(1)} %collective-permute-done.rest_1_, bf16[1552,128]{1,0:T(8,128)(2,1)S(1)} %collective-permute-done.3.rest_2_, ...), custom_call_target="tpu_custom_call" | custom-call | flops 30000001024 | bytes 1 | tf_op jit(solution)/shard_map/score_1/pallas_call | solution.py:254
  58.2 0.2 collective-permute-start.13
  58.4 0.4 collective-permute-start.12
  58.8 1.1 %collective-permute-done.12.rest_13_.rest_14_ = bf16[768,128]{1,0:T(8,128)(2,1)S(1)} collective-permute-done((bf16[768,128]{1,0:T(8,128)(2,1)S(1)}, bf16[768,128]{1,0:T(8,128)(2,1)S(1)}, u32[]{:S(2)}, u32[]{:S(2)}) %collective-permute-start.12) | collective-permute-done | bytes 196640 | tf_op jit(solution)/shard_map/ppermute | solution.py:214
  60.0 3.0 %score_2.1.prev_ref = f32[8,192]{1,0:T(8,128)S(1)} custom-call(s32[1]{0:T(128)} %bitcast.1.me_ref, f32[8,192]{1,0:T(8,128)S(1)} %score_1.1.prev_ref, bf16[1552,128]{1,0:T(8,128)(2,1)S(1)} %get-tuple-element.21.rest_0_, bf16[1552,128]{1,0:T(8,128)(2,1)S(1)} %collective-permute-done.rest_1_, bf16[1552,128]{1,0:T(8,128)(2,1)S(1)} %collective-permute-done.3.rest_2_, ...), custom_call_target="tpu_custom_call" | custom-call | flops 1 | bytes 1 | tf_op jit(solution)/shard_map/score_2/pallas_call | solution.py:254
  63.0 1.0 %collective-permute-done.14.rest_7_ = bf16[1552,128]{1,0:T(8,128)(2,1)S(1)} collective-permute-done((bf16[1552,128]{1,0:T(8,128)(2,1)S(1)}, bf16[1552,128]{1,0:T(8,128)(2,1)S(1)}, u32[]{:S(2)}, u32[]{:S(2)}) %collective-permute-start.14) | collective-permute-done | bytes 397344 | tf_op jit(solution)/shard_map/ppermute | solution.py:217
  64.1 1.8 %score_3.1.prev_ref = f32[8,192]{1,0:T(8,128)S(1)} custom-call(s32[1]{0:T(128)} %bitcast.1.me_ref, f32[8,192]{1,0:T(8,128)S(1)} %score_2.1.prev_ref, bf16[1552,128]{1,0:T(8,128)(2,1)S(1)} %get-tuple-element.21.rest_0_, bf16[1552,128]{1,0:T(8,128)(2,1)S(1)} %collective-permute-done.rest_1_, bf16[1552,128]{1,0:T(8,128)(2,1)S(1)} %collective-permute-done.3.rest_2_, ...), custom_call_target="tpu_custom_call" | custom-call | flops 30000001024 | bytes 1 | tf_op jit(solution)/shard_map/score_3/pallas_call | solution.py:254
  65.9 1.5 %score_final.1 = f32[8,192]{1,0:T(8,128)S(1)} custom-call(s32[1]{0:T(128)} %bitcast.1.me_ref, f32[8,192]{1,0:T(8,128)S(1)} %score_3.1.prev_ref, bf16[1552,128]{1,0:T(8,128)(2,1)S(1)} %get-tuple-element.21.rest_0_, bf16[1552,128]{1,0:T(8,128)(2,1)S(1)} %collective-permute-done.rest_1_, bf16[1552,128]{1,0:T(8,128)(2,1)S(1)} %collective-permute-done.3.rest_2_, ...), custom_call_target="tpu_custom_call" | custom-call | flops 30000001024 | bytes 1 | tf_op jit(solution)/shard_map/score_final/pallas_call | solution.py:254
  67.4 23.4 %all_to_all.11 = f32[8,1,192]{2,1,0:T(1,128)S(1)} all-to-all(f32[8,1,192]{2,1,0:T(1,128)S(1)} %copy.4), channel_id=1, replica_groups=mesh['parts'=2,'wide'=8,'narrow'=2] {'wide'}, dimensions={0} | all-to-all | bytes 12288 | tf_op jit(solution)/shard_map/all_to_all | solution.py:283
  90.8 0.8 select.1
  (26 shorter events, 0.4 us)
Async XLA Ops:
  0.0 6.3 %copy-start = (bf16[768,1024]{1,0:T(8,128)(2,1)S(1)}, bf16[768,1024]{1,0:T(8,128)(2,1)}, u32[]{:S(2)}) copy-start(bf16[768,1024]{1,0:T(8,128)(2,1)} %emb_ref.1) | copy-start | bytes 4718596
  0.0 6.3 %copy-start.1 = (s32[768,1]{0,1:T(1,128)S(1)}, s32[768,1]{0,1:T(1,128)}, u32[]{:S(2)}) copy-start(s32[768,1]{0,1:T(1,128)} %param.4) | copy-start | bytes 9220
  2.2 31.3 %collective-permute-start = (bf16[1552,128]{1,0:T(8,128)(2,1)S(1)}, bf16[1552,128]{1,0:T(8,128)(2,1)S(1)}, u32[]{:S(2)}, u32[]{:S(2)}) collective-permute-start(bf16[1552,128]{1,0:T(8,128)(2,1)S(1)} %get-tuple-element.22), channel_id=1, source_target_pairs={{0,8},{2,10},{4,12},{6,14},{8,0},{10,2},{12,4},{14,6},{1,9},{3,11}... | collective-permute-start | bytes 1191944 | tf_op jit(solution)/shard_map/ppermute | solution.py:217
  8.8 33.4 %collective-permute-start.3 = (bf16[1552,128]{1,0:T(8,128)(2,1)S(1)}, bf16[1552,128]{1,0:T(8,128)(2,1)S(1)}, u32[]{:S(2)}, u32[]{:S(2)}) collective-permute-start(bf16[1552,128]{1,0:T(8,128)(2,1)S(1)} %get-tuple-element.23), channel_id=1, source_target_pairs={{0,10},{2,8},{4,14},{6,12},{8,2},{10,0},{12,6},{14,4},{1,11},{3,9}... | collective-permute-start | bytes 1191944 | tf_op jit(solution)/shard_map/ppermute | solution.py:217
  10.1 32.0 %collective-permute-start.4 = (bf16[1552,128]{1,0:T(8,128)(2,1)S(1)}, bf16[1552,128]{1,0:T(8,128)(2,1)S(1)}, u32[]{:S(2)}, u32[]{:S(2)}) collective-permute-start(bf16[1552,128]{1,0:T(8,128)(2,1)S(1)} %get-tuple-element.24), channel_id=1, source_target_pairs={{0,2},{2,0},{4,6},{6,4},{8,10},{10,8},{12,14},{14,12},{1,3},{3,1},... | collective-permute-start | bytes 1191944 | tf_op jit(solution)/shard_map/ppermute | solution.py:217
  10.4 35.2 %collective-permute-start.5 = (bf16[1552,128]{1,0:T(8,128)(2,1)S(1)}, bf16[1552,128]{1,0:T(8,128)(2,1)S(1)}, u32[]{:S(2)}, u32[]{:S(2)}) collective-permute-start(bf16[1552,128]{1,0:T(8,128)(2,1)S(1)} %get-tuple-element.25), channel_id=1, source_target_pairs={{0,4},{2,6},{4,0},{6,2},{8,12},{10,14},{12,8},{14,10},{1,5},{3,7},... | collective-permute-start | bytes 1191944 | tf_op jit(solution)/shard_map/ppermute | solution.py:217
  12.2 33.9 %collective-permute-start.6 = (bf16[1552,128]{1,0:T(8,128)(2,1)S(1)}, bf16[1552,128]{1,0:T(8,128)(2,1)S(1)}, u32[]{:S(2)}, u32[]{:S(2)}) collective-permute-start(bf16[1552,128]{1,0:T(8,128)(2,1)S(1)} %get-tuple-element.26), channel_id=1, source_target_pairs={{0,6},{2,4},{4,2},{6,0},{8,14},{10,12},{12,10},{14,8},{1,7},{3,5},... | collective-permute-start | bytes 1191944 | tf_op jit(solution)/shard_map/ppermute | solution.py:217
  33.4 12.7 %collective-permute-start.1 = (bf16[1552,128]{1,0:T(8,128)(2,1)S(1)}, bf16[1552,128]{1,0:T(8,128)(2,1)S(1)}, u32[]{:S(2)}, u32[]{:S(2)}) collective-permute-start(bf16[1552,128]{1,0:T(8,128)(2,1)S(1)} %get-tuple-element.21.rest_0_), channel_id=1, source_target_pairs={{0,1},{1,0},{2,3},{3,2},{4,5},{5,4},{6,7},{7,6},{8,9},{9,8},{10,11... | collective-permute-start | bytes 1191944 | tf_op jit(solution)/shard_map/ppermute | solution.py:214
  42.1 4.5 %collective-permute-start.2 = (bf16[1552,128]{1,0:T(8,128)(2,1)S(1)}, bf16[1552,128]{1,0:T(8,128)(2,1)S(1)}, u32[]{:S(2)}, u32[]{:S(2)}) collective-permute-start(bf16[1552,128]{1,0:T(8,128)(2,1)S(1)} %collective-permute-done.rest_1_), channel_id=1, source_target_pairs={{0,1},{1,0},{2,3},{3,2},{4,5},{5,4},{6,7},{7,6},{8,9},{9,8},{10,11... | collective-permute-start | bytes 1191944 | tf_op jit(solution)/shard_map/ppermute | solution.py:214
  42.1 16.0 %collective-permute-start.11 = (bf16[1552,128]{1,0:T(8,128)(2,1)S(1)}, bf16[1552,128]{1,0:T(8,128)(2,1)S(1)}, u32[]{:S(2)}, u32[]{:S(2)}) collective-permute-start(bf16[1552,128]{1,0:T(8,128)(2,1)S(1)} %get-tuple-element.28), channel_id=1, source_target_pairs={{0,12},{2,14},{4,8},{6,10},{8,4},{10,6},{12,0},{14,2},{1,13},{3,15... | collective-permute-start | bytes 1191944 | tf_op jit(solution)/shard_map/ppermute | solution.py:217
  45.6 2.2 %collective-permute-start.7 = (bf16[1552,128]{1,0:T(8,128)(2,1)S(1)}, bf16[1552,128]{1,0:T(8,128)(2,1)S(1)}, u32[]{:S(2)}, u32[]{:S(2)}) collective-permute-start(bf16[1552,128]{1,0:T(8,128)(2,1)S(1)} %collective-permute-done.3.rest_2_), channel_id=1, source_target_pairs={{0,1},{1,0},{2,3},{3,2},{4,5},{5,4},{6,7},{7,6},{8,9},{9,8},{10,11... | collective-permute-start | bytes 1191944 | tf_op jit(solution)/shard_map/ppermute | solution.py:214
  46.1 6.2 %collective-permute-start.8 = (bf16[1552,128]{1,0:T(8,128)(2,1)S(1)}, bf16[1552,128]{1,0:T(8,128)(2,1)S(1)}, u32[]{:S(2)}, u32[]{:S(2)}) collective-permute-start(bf16[1552,128]{1,0:T(8,128)(2,1)S(1)} %collective-permute-done.4.rest_3_), channel_id=1, source_target_pairs={{0,1},{1,0},{2,3},{3,2},{4,5},{5,4},{6,7},{7,6},{8,9},{9,8},{10,11... | collective-permute-start | bytes 1191944 | tf_op jit(solution)/shard_map/ppermute | solution.py:214
  46.1 6.2 %collective-permute-start.9 = (bf16[1552,128]{1,0:T(8,128)(2,1)S(1)}, bf16[1552,128]{1,0:T(8,128)(2,1)S(1)}, u32[]{:S(2)}, u32[]{:S(2)}) collective-permute-start(bf16[1552,128]{1,0:T(8,128)(2,1)S(1)} %collective-permute-done.5.rest_4_), channel_id=1, source_target_pairs={{0,1},{1,0},{2,3},{3,2},{4,5},{5,4},{6,7},{7,6},{8,9},{9,8},{10,11... | collective-permute-start | bytes 1191944 | tf_op jit(solution)/shard_map/ppermute | solution.py:214
  46.6 5.7 %collective-permute-start.10 = (bf16[1552,128]{1,0:T(8,128)(2,1)S(1)}, bf16[1552,128]{1,0:T(8,128)(2,1)S(1)}, u32[]{:S(2)}, u32[]{:S(2)}) collective-permute-start(bf16[1552,128]{1,0:T(8,128)(2,1)S(1)} %collective-permute-done.6.rest_5_), channel_id=1, source_target_pairs={{0,1},{1,0},{2,3},{3,2},{4,5},{5,4},{6,7},{7,6},{8,9},{9,8},{10,11... | collective-permute-start | bytes 1191944 | tf_op jit(solution)/shard_map/ppermute | solution.py:214
  47.8 16.3 %collective-permute-start.14 = (bf16[1552,128]{1,0:T(8,128)(2,1)S(1)}, bf16[1552,128]{1,0:T(8,128)(2,1)S(1)}, u32[]{:S(2)}, u32[]{:S(2)}) collective-permute-start(bf16[1552,128]{1,0:T(8,128)(2,1)S(1)} %get-tuple-element.31), channel_id=1, source_target_pairs={{0,14},{2,12},{4,10},{6,8},{8,6},{10,4},{12,2},{14,0},{1,15},{3,13... | collective-permute-start | bytes 1191944 | tf_op jit(solution)/shard_map/ppermute | solution.py:217
  58.2 1.8 %collective-permute-start.13 = (bf16[784,128]{1,0:T(8,128)(2,1)S(1)}, bf16[784,128]{1,0:T(8,128)(2,1)S(1)}, u32[]{:S(2)}, u32[]{:S(2)}) collective-permute-start(bf16[784,128]{1,0:T(8,128)(2,1)S(1)} %slice.7), channel_id=1, source_target_pairs={{0,1},{1,0},{2,3},{3,2},{4,5},{5,4},{6,7},{7,6},{8,9},{9,8},{10,11... | collective-permute-start | bytes 602120 | tf_op jit(solution)/shard_map/ppermute | solution.py:214
  58.4 1.5 %collective-permute-start.12 = (bf16[768,128]{1,0:T(8,128)(2,1)S(1)}, bf16[768,128]{1,0:T(8,128)(2,1)S(1)}, u32[]{:S(2)}, u32[]{:S(2)}) collective-permute-start(bf16[768,128]{1,0:T(8,128)(2,1)S(1)} %slice.6), channel_id=1, source_target_pairs={{0,1},{1,0},{2,3},{3,2},{4,5},{5,4},{6,7},{7,6},{8,9},{9,8},{10,11... | collective-permute-start | bytes 589832 | tf_op jit(solution)/shard_map/ppermute | solution.py:214
  64.1 1.8 %collective-permute-start.15 = (bf16[1552,128]{1,0:T(8,128)(2,1)S(1)}, bf16[1552,128]{1,0:T(8,128)(2,1)S(1)}, u32[]{:S(2)}, u32[]{:S(2)}) collective-permute-start(bf16[1552,128]{1,0:T(8,128)(2,1)S(1)} %collective-permute-done.14.rest_7_), channel_id=1, source_target_pairs={{0,1},{1,0},{2,3},{3,2},{4,5},{5,4},{6,7},{7,6},{8,9},{9,8},{10,11... | collective-permute-start | bytes 1191944 | tf_op jit(solution)/shard_map/ppermute | solution.py:214

commit v9 on v7

--- a/solution.py
+++ b/solution.py
@@ -10,7 +10,7 @@
 EMPTY = 2.0**22
 VMEM_LIMIT = 40 * 1024 * 1024
 LANES = 128
-CHUNKS = 1
+CHUNKS = 4
 PACK_COST, SCORE_COSTS = 3 * 10**10, (10**10, 3 * 10**10, 1, 3 * 10**10)
 HALVED = 2
 TAIL = 16
@@ -91,13 +91,10 @@
     low = placed[groups : 2 * groups]
     ranks_ref[...] = jnp.concatenate([high, low], axis=0)
     picks = [_pick(lab, pos, jnp.bitwise_xor(me_ref[0], r), first, last) for r, first, last in pieces]
-    sums = [0.0] * len(pieces)
-    for i, copy in enumerate(copies):
+    for copy in copies:
         copy.wait()
-        part = emb_ref[spans[i], :]
-        for j, pick in enumerate(picks):
-            sums[j] += jnp.dot(pick[:, i * chunk : (i + 1) * chunk], part, preferred_element_type=jnp.float32)
-    for (r, first, last), out, block in zip(pieces, outs, sums):
+    for (r, first, last), out, pick in zip(pieces, outs, picks):
+        block = jnp.dot(pick, emb_ref[...], preferred_element_type=jnp.float32)
         _write_block(out, block, high[r : r + 1, first:], low[r : r + 1, first:], last - first)
 
 

time: 91.9 us -> 92 us (level)
  no operation moved by 1% of the time
where the time goes in v9:
time: 92 us; the launch traced here: 91.8 us
  waiting for transfers between devices  31 us (34%)
  blocking collectives  23.4 us (25%)
  Pallas kernels  18.8 us (20%)
  starting transfers between devices  18.5 us (20%)
    ppermute x7, waiting for transfers between devices, send(): return lax.ppermute(x, 'wide', [(s, s ^ r) for s in range(groups)])  29.8 us
    all_to_all x1, blocking collectives, local(): lax.all_to_all(best, 'wide', split_axis=0, concat_axis=0, tiled=True)  23.4 us
    ppermute x7, starting transfers between devices, send(): return lax.ppermute(x, 'wide', [(s, s ^ r) for s in range(groups)])  17 us
    pallas_call x5, Pallas kernels, score(): pl.pallas_call(functools.partial(_score, pieces, jobs, len(partners), n_o...  13.2 us
    pallas_call x1, Pallas kernels, pack_rest(): pl.pallas_call(functools.partial(_pack_rest, pieces, groups), out_shape=[...  2.47 us
    pallas_call x1, Pallas kernels, local(): pl.pallas_call(functools.partial(_pack_first, far[:quarter], groups, slot...  2.32 us
  transfers between devices with their start and end apart: 16, of which 5 were waited for; matrix products, arithmetic and copies ran while one was open for 0% of the time, Pallas kernels for 15%

profile of v9, /device:TPU:0, one launch (start us, length us, event | category | flops | bytes accessed | tf_op | source)
XLA Modules:
  0.0 91.8 jit_solution(9663852811753928815)
XLA Ops:
  0.0 2.3 %pack_first.1 = (s32[1,768]{1,0:T(1,128)S(1)}, f32[16,256]{1,0:T(8,128)S(1)}, bf16[1552,128]{1,0:T(8,128)(2,1)S(1)}) custom-call(s32[1]{0:T(128)} %bitcast.1.me_ref, bf16[768,1024]{1,0:T(8,128)(2,1)} %emb_ref.1, s32[1,768]{1,0:T(1,128)} %bitcast.8, s32[6,128]{1,0:T(8,128)} %bitcast.12), custom_call_target="tpu_custom_call" | custom-call | tf_op jit(solution)/shard_map/pack_first/pallas_call | solution.py:191
  2.3 4.1 %collective-permute-start = (bf16[1552,128]{1,0:T(8,128)(2,1)S(1)}, bf16[1552,128]{1,0:T(8,128)(2,1)S(1)}, u32[]{:S(2)}, u32[]{:S(2)}) collective-permute-start(bf16[1552,128]{1,0:T(8,128)(2,1)S(1)} %get-tuple-element.22), channel_id=1, source_target_pairs={{0,8},{2,10},{4,12},{6,14},{8,0},{10,2},{12,4},{14,6},{1,9},{3,11}... | collective-permute-start | bytes 1191944 | tf_op jit(solution)/shard_map/ppermute | solution.py:215
  6.4 2.5 %pack_rest.1 = (bf16[1552,128]{1,0:T(8,128)(2,1)S(1)}, bf16[1552,128]{1,0:T(8,128)(2,1)S(1)}, bf16[1552,128]{1,0:T(8,128)(2,1)S(1)}, bf16[1552,128]{1,0:T(8,128)...) custom-call(s32[1]{0:T(128)} %bitcast.1.me_ref, ...), custom_call_target="tpu_custom_call" | custom-call | flops 30000001024 | bytes 1 | tf_op jit(solution)/shard_map/pack_rest/pallas_call | solution.py:221
  8.9 1.4 %collective-permute-start.3 = (bf16[1552,128]{1,0:T(8,128)(2,1)S(1)}, bf16[1552,128]{1,0:T(8,128)(2,1)S(1)}, u32[]{:S(2)}, u32[]{:S(2)}) collective-permute-start(bf16[1552,128]{1,0:T(8,128)(2,1)S(1)} %get-tuple-element.23), channel_id=1, source_target_pairs={{0,10},{2,8},{4,14},{6,12},{8,2},{10,0},{12,6},{14,4},{1,11},{3,9}... | collective-permute-start | bytes 1191944 | tf_op jit(solution)/shard_map/ppermute | solution.py:215
  10.3 0.3 collective-permute-start.4
  10.6 1.8 %collective-permute-start.5 = (bf16[1552,128]{1,0:T(8,128)(2,1)S(1)}, bf16[1552,128]{1,0:T(8,128)(2,1)S(1)}, u32[]{:S(2)}, u32[]{:S(2)}) collective-permute-start(bf16[1552,128]{1,0:T(8,128)(2,1)S(1)} %get-tuple-element.25), channel_id=1, source_target_pairs={{0,4},{2,6},{4,0},{6,2},{8,12},{10,14},{12,8},{14,10},{1,5},{3,7},... | collective-permute-start | bytes 1191944 | tf_op jit(solution)/shard_map/ppermute | solution.py:215
  12.4 1.4 %collective-permute-start.6 = (bf16[1552,128]{1,0:T(8,128)(2,1)S(1)}, bf16[1552,128]{1,0:T(8,128)(2,1)S(1)}, u32[]{:S(2)}, u32[]{:S(2)}) collective-permute-start(bf16[1552,128]{1,0:T(8,128)(2,1)S(1)} %get-tuple-element.26), channel_id=1, source_target_pairs={{0,6},{2,4},{4,2},{6,0},{8,14},{10,12},{12,10},{14,8},{1,7},{3,5},... | collective-permute-start | bytes 1191944 | tf_op jit(solution)/shard_map/ppermute | solution.py:215
  13.8 19.8 %collective-permute-done.rest_1_ = bf16[1552,128]{1,0:T(8,128)(2,1)S(1)} collective-permute-done((bf16[1552,128]{1,0:T(8,128)(2,1)S(1)}, bf16[1552,128]{1,0:T(8,128)(2,1)S(1)}, u32[]{:S(2)}, u32[]{:S(2)}) %collective-permute-start) | collective-permute-done | bytes 397344 | tf_op jit(solution)/shard_map/ppermute | solution.py:215
  33.6 8.7 %collective-permute-done.3.rest_2_ = bf16[1552,128]{1,0:T(8,128)(2,1)S(1)} collective-permute-done((bf16[1552,128]{1,0:T(8,128)(2,1)S(1)}, bf16[1552,128]{1,0:T(8,128)(2,1)S(1)}, u32[]{:S(2)}, u32[]{:S(2)}) %collective-permute-start.3) | collective-permute-done | bytes 397344 | tf_op jit(solution)/shard_map/ppermute | solution.py:215
  42.3 3.5 %collective-permute-start.11 = (bf16[1552,128]{1,0:T(8,128)(2,1)S(1)}, bf16[1552,128]{1,0:T(8,128)(2,1)S(1)}, u32[]{:S(2)}, u32[]{:S(2)}) collective-permute-start(bf16[1552,128]{1,0:T(8,128)(2,1)S(1)} %get-tuple-element.28), channel_id=1, source_target_pairs={{0,12},{2,14},{4,8},{6,10},{8,4},{10,6},{12,0},{14,2},{1,13},{3,15... | collective-permute-start | bytes 1191944 | tf_op jit(solution)/shard_map/ppermute | solution.py:215
  45.8 0.2 collective-permute-start.7
  46.0 0.3 collective-permute-done.6.rest_5_
  46.3 0.5 collective-permute-start.9
  46.9 1.1 %score_0.1.prev_ref = f32[8,192]{1,0:T(8,128)S(1)} custom-call(s32[1]{0:T(128)} %bitcast.1.me_ref, f32[8,192]{1,0:T(8,128)S(1)} %broadcast_in_dim.3.prev_ref, bf16[1552,128]{1,0:T(8,128)(2,1)S(1)} %get-tuple-element.21.rest_0_, bf16[1552,128]{1,0:T(8,128)(2,1)S(1)} %collective-permute-done.rest_1_, ...), custom_call_target="tpu_custom_call" | custom-call | flops 10000000000 | bytes 1 | tf_op jit(solution)/shard_map/score_0/pallas_call | solution.py:252
  48.0 4.6 %collective-permute-start.14 = (bf16[1552,128]{1,0:T(8,128)(2,1)S(1)}, bf16[1552,128]{1,0:T(8,128)(2,1)S(1)}, u32[]{:S(2)}, u32[]{:S(2)}) collective-permute-start(bf16[1552,128]{1,0:T(8,128)(2,1)S(1)} %get-tuple-element.31), channel_id=1, source_target_pairs={{0,14},{2,12},{4,10},{6,8},{8,6},{10,4},{12,2},{14,0},{1,15},{3,13... | collective-permute-start | bytes 1191944 | tf_op jit(solution)/shard_map/ppermute | solution.py:215
  52.5 5.8 %score_1.1.prev_ref = f32[8,192]{1,0:T(8,128)S(1)} custom-call(s32[1]{0:T(128)} %bitcast.1.me_ref, f32[8,192]{1,0:T(8,128)S(1)} %score_0.1.prev_ref, bf16[1552,128]{1,0:T(8,128)(2,1)S(1)} %get-tuple-element.21.rest_0_, bf16[1552,128]{1,0:T(8,128)(2,1)S(1)} %collective-permute-done.rest_1_, bf16[1552,128]{1,0:T(8,128)(2,1)S(1)} %collective-permute-done.3.rest_2_, ...), custom_call_target="tpu_custom_call" | custom-call | flops 30000001024 | bytes 1 | tf_op jit(solution)/shard_map/score_1/pallas_call | solution.py:252
  58.6 0.4 collective-permute-start.12
  59.0 1.1 %collective-permute-done.12.rest_13_.rest_14_ = bf16[768,128]{1,0:T(8,128)(2,1)S(1)} collective-permute-done((bf16[768,128]{1,0:T(8,128)(2,1)S(1)}, bf16[768,128]{1,0:T(8,128)(2,1)S(1)}, u32[]{:S(2)}, u32[]{:S(2)}) %collective-permute-start.12) | collective-permute-done | bytes 196640 | tf_op jit(solution)/shard_map/ppermute | solution.py:212
  60.1 3.0 %score_2.1.prev_ref = f32[8,192]{1,0:T(8,128)S(1)} custom-call(s32[1]{0:T(128)} %bitcast.1.me_ref, f32[8,192]{1,0:T(8,128)S(1)} %score_1.1.prev_ref, bf16[1552,128]{1,0:T(8,128)(2,1)S(1)} %get-tuple-element.21.rest_0_, bf16[1552,128]{1,0:T(8,128)(2,1)S(1)} %collective-permute-done.rest_1_, bf16[1552,128]{1,0:T(8,128)(2,1)S(1)} %collective-permute-done.3.rest_2_, ...), custom_call_target="tpu_custom_call" | custom-call | flops 1 | bytes 1 | tf_op jit(solution)/shard_map/score_2/pallas_call | solution.py:252
  63.2 1.0 %collective-permute-done.14.rest_7_ = bf16[1552,128]{1,0:T(8,128)(2,1)S(1)} collective-permute-done((bf16[1552,128]{1,0:T(8,128)(2,1)S(1)}, bf16[1552,128]{1,0:T(8,128)(2,1)S(1)}, u32[]{:S(2)}, u32[]{:S(2)}) %collective-permute-start.14) | collective-permute-done | bytes 397344 | tf_op jit(solution)/shard_map/ppermute | solution.py:215
  64.2 1.8 %score_3.1.prev_ref = f32[8,192]{1,0:T(8,128)S(1)} custom-call(s32[1]{0:T(128)} %bitcast.1.me_ref, f32[8,192]{1,0:T(8,128)S(1)} %score_2.1.prev_ref, bf16[1552,128]{1,0:T(8,128)(2,1)S(1)} %get-tuple-element.21.rest_0_, bf16[1552,128]{1,0:T(8,128)(2,1)S(1)} %collective-permute-done.rest_1_, bf16[1552,128]{1,0:T(8,128)(2,1)S(1)} %collective-permute-done.3.rest_2_, ...), custom_call_target="tpu_custom_call" | custom-call | flops 30000001024 | bytes 1 | tf_op jit(solution)/shard_map/score_3/pallas_call | solution.py:252
  66.0 1.5 %score_final.1 = f32[8,192]{1,0:T(8,128)S(1)} custom-call(s32[1]{0:T(128)} %bitcast.1.me_ref, f32[8,192]{1,0:T(8,128)S(1)} %score_3.1.prev_ref, bf16[1552,128]{1,0:T(8,128)(2,1)S(1)} %get-tuple-element.21.rest_0_, bf16[1552,128]{1,0:T(8,128)(2,1)S(1)} %collective-permute-done.rest_1_, bf16[1552,128]{1,0:T(8,128)(2,1)S(1)} %collective-permute-done.3.rest_2_, ...), custom_call_target="tpu_custom_call" | custom-call | flops 30000001024 | bytes 1 | tf_op jit(solution)/shard_map/score_final/pallas_call | solution.py:252
  67.6 23.4 %all_to_all.11 = f32[8,1,192]{2,1,0:T(1,128)S(1)} all-to-all(f32[8,1,192]{2,1,0:T(1,128)S(1)} %copy.4), channel_id=1, replica_groups=mesh['parts'=2,'wide'=8,'narrow'=2] {'wide'}, dimensions={0} | all-to-all | bytes 12288 | tf_op jit(solution)/shard_map/all_to_all | solution.py:281
  91.0 0.8 select.1
  (26 shorter events, 0.4 us)
Async XLA Ops:
  0.0 6.4 %copy-start = (bf16[768,1024]{1,0:T(8,128)(2,1)S(1)}, bf16[768,1024]{1,0:T(8,128)(2,1)}, u32[]{:S(2)}) copy-start(bf16[768,1024]{1,0:T(8,128)(2,1)} %emb_ref.1) | copy-start | bytes 4718596
  0.0 6.4 %copy-start.1 = (s32[768,1]{0,1:T(1,128)S(1)}, s32[768,1]{0,1:T(1,128)}, u32[]{:S(2)}) copy-start(s32[768,1]{0,1:T(1,128)} %param.4) | copy-start | bytes 9220
  2.3 31.3 %collective-permute-start = (bf16[1552,128]{1,0:T(8,128)(2,1)S(1)}, bf16[1552,128]{1,0:T(8,128)(2,1)S(1)}, u32[]{:S(2)}, u32[]{:S(2)}) collective-permute-start(bf16[1552,128]{1,0:T(8,128)(2,1)S(1)} %get-tuple-element.22), channel_id=1, source_target_pairs={{0,8},{2,10},{4,12},{6,14},{8,0},{10,2},{12,4},{14,6},{1,9},{3,11}... | collective-permute-start | bytes 1191944 | tf_op jit(solution)/shard_map/ppermute | solution.py:215
  8.9 33.4 %collective-permute-start.3 = (bf16[1552,128]{1,0:T(8,128)(2,1)S(1)}, bf16[1552,128]{1,0:T(8,128)(2,1)S(1)}, u32[]{:S(2)}, u32[]{:S(2)}) collective-permute-start(bf16[1552,128]{1,0:T(8,128)(2,1)S(1)} %get-tuple-element.23), channel_id=1, source_target_pairs={{0,10},{2,8},{4,14},{6,12},{8,2},{10,0},{12,6},{14,4},{1,11},{3,9}... | collective-permute-start | bytes 1191944 | tf_op jit(solution)/shard_map/ppermute | solution.py:215
  10.3 32.0 %collective-permute-start.4 = (bf16[1552,128]{1,0:T(8,128)(2,1)S(1)}, bf16[1552,128]{1,0:T(8,128)(2,1)S(1)}, u32[]{:S(2)}, u32[]{:S(2)}) collective-permute-start(bf16[1552,128]{1,0:T(8,128)(2,1)S(1)} %get-tuple-element.24), channel_id=1, source_target_pairs={{0,2},{2,0},{4,6},{6,4},{8,10},{10,8},{12,14},{14,12},{1,3},{3,1},... | collective-permute-start | bytes 1191944 | tf_op jit(solution)/shard_map/ppermute | solution.py:215
  10.6 35.2 %collective-permute-start.5 = (bf16[1552,128]{1,0:T(8,128)(2,1)S(1)}, bf16[1552,128]{1,0:T(8,128)(2,1)S(1)}, u32[]{:S(2)}, u32[]{:S(2)}) collective-permute-start(bf16[1552,128]{1,0:T(8,128)(2,1)S(1)} %get-tuple-element.25), channel_id=1, source_target_pairs={{0,4},{2,6},{4,0},{6,2},{8,12},{10,14},{12,8},{14,10},{1,5},{3,7},... | collective-permute-start | bytes 1191944 | tf_op jit(solution)/shard_map/ppermute | solution.py:215
  12.4 33.9 %collective-permute-start.6 = (bf16[1552,128]{1,0:T(8,128)(2,1)S(1)}, bf16[1552,128]{1,0:T(8,128)(2,1)S(1)}, u32[]{:S(2)}, u32[]{:S(2)}) collective-permute-start(bf16[1552,128]{1,0:T(8,128)(2,1)S(1)} %get-tuple-element.26), channel_id=1, source_target_pairs={{0,6},{2,4},{4,2},{6,0},{8,14},{10,12},{12,10},{14,8},{1,7},{3,5},... | collective-permute-start | bytes 1191944 | tf_op jit(solution)/shard_map/ppermute | solution.py:215
  33.6 12.7 %collective-permute-start.1 = (bf16[1552,128]{1,0:T(8,128)(2,1)S(1)}, bf16[1552,128]{1,0:T(8,128)(2,1)S(1)}, u32[]{:S(2)}, u32[]{:S(2)}) collective-permute-start(bf16[1552,128]{1,0:T(8,128)(2,1)S(1)} %get-tuple-element.21.rest_0_), channel_id=1, source_target_pairs={{0,1},{1,0},{2,3},{3,2},{4,5},{5,4},{6,7},{7,6},{8,9},{9,8},{10,11... | collective-permute-start | bytes 1191944 | tf_op jit(solution)/shard_map/ppermute | solution.py:212
  42.3 4.5 %collective-permute-start.2 = (bf16[1552,128]{1,0:T(8,128)(2,1)S(1)}, bf16[1552,128]{1,0:T(8,128)(2,1)S(1)}, u32[]{:S(2)}, u32[]{:S(2)}) collective-permute-start(bf16[1552,128]{1,0:T(8,128)(2,1)S(1)} %collective-permute-done.rest_1_), channel_id=1, source_target_pairs={{0,1},{1,0},{2,3},{3,2},{4,5},{5,4},{6,7},{7,6},{8,9},{9,8},{10,11... | collective-permute-start | bytes 1191944 | tf_op jit(solution)/shard_map/ppermute | solution.py:212
  42.3 16.0 %collective-permute-start.11 = (bf16[1552,128]{1,0:T(8,128)(2,1)S(1)}, bf16[1552,128]{1,0:T(8,128)(2,1)S(1)}, u32[]{:S(2)}, u32[]{:S(2)}) collective-permute-start(bf16[1552,128]{1,0:T(8,128)(2,1)S(1)} %get-tuple-element.28), channel_id=1, source_target_pairs={{0,12},{2,14},{4,8},{6,10},{8,4},{10,6},{12,0},{14,2},{1,13},{3,15... | collective-permute-start | bytes 1191944 | tf_op jit(solution)/shard_map/ppermute | solution.py:215
  45.8 2.2 %collective-permute-start.7 = (bf16[1552,128]{1,0:T(8,128)(2,1)S(1)}, bf16[1552,128]{1,0:T(8,128)(2,1)S(1)}, u32[]{:S(2)}, u32[]{:S(2)}) collective-permute-start(bf16[1552,128]{1,0:T(8,128)(2,1)S(1)} %collective-permute-done.3.rest_2_), channel_id=1, source_target_pairs={{0,1},{1,0},{2,3},{3,2},{4,5},{5,4},{6,7},{7,6},{8,9},{9,8},{10,11... | collective-permute-start | bytes 1191944 | tf_op jit(solution)/shard_map/ppermute | solution.py:212
  46.3 6.2 %collective-permute-start.8 = (bf16[1552,128]{1,0:T(8,128)(2,1)S(1)}, bf16[1552,128]{1,0:T(8,128)(2,1)S(1)}, u32[]{:S(2)}, u32[]{:S(2)}) collective-permute-start(bf16[1552,128]{1,0:T(8,128)(2,1)S(1)} %collective-permute-done.4.rest_3_), channel_id=1, source_target_pairs={{0,1},{1,0},{2,3},{3,2},{4,5},{5,4},{6,7},{7,6},{8,9},{9,8},{10,11... | collective-permute-start | bytes 1191944 | tf_op jit(solution)/shard_map/ppermute | solution.py:212
  46.3 6.2 %collective-permute-start.9 = (bf16[1552,128]{1,0:T(8,128)(2,1)S(1)}, bf16[1552,128]{1,0:T(8,128)(2,1)S(1)}, u32[]{:S(2)}, u32[]{:S(2)}) collective-permute-start(bf16[1552,128]{1,0:T(8,128)(2,1)S(1)} %collective-permute-done.5.rest_4_), channel_id=1, source_target_pairs={{0,1},{1,0},{2,3},{3,2},{4,5},{5,4},{6,7},{7,6},{8,9},{9,8},{10,11... | collective-permute-start | bytes 1191944 | tf_op jit(solution)/shard_map/ppermute | solution.py:212
  46.8 5.7 %collective-permute-start.10 = (bf16[1552,128]{1,0:T(8,128)(2,1)S(1)}, bf16[1552,128]{1,0:T(8,128)(2,1)S(1)}, u32[]{:S(2)}, u32[]{:S(2)}) collective-permute-start(bf16[1552,128]{1,0:T(8,128)(2,1)S(1)} %collective-permute-done.6.rest_5_), channel_id=1, source_target_pairs={{0,1},{1,0},{2,3},{3,2},{4,5},{5,4},{6,7},{7,6},{8,9},{9,8},{10,11... | collective-permute-start | bytes 1191944 | tf_op jit(solution)/shard_map/ppermute | solution.py:212
  48.0 16.3 %collective-permute-start.14 = (bf16[1552,128]{1,0:T(8,128)(2,1)S(1)}, bf16[1552,128]{1,0:T(8,128)(2,1)S(1)}, u32[]{:S(2)}, u32[]{:S(2)}) collective-permute-start(bf16[1552,128]{1,0:T(8,128)(2,1)S(1)} %get-tuple-element.31), channel_id=1, source_target_pairs={{0,14},{2,12},{4,10},{6,8},{8,6},{10,4},{12,2},{14,0},{1,15},{3,13... | collective-permute-start | bytes 1191944 | tf_op jit(solution)/shard_map/ppermute | solution.py:215
  58.3 1.8 %collective-permute-start.13 = (bf16[784,128]{1,0:T(8,128)(2,1)S(1)}, bf16[784,128]{1,0:T(8,128)(2,1)S(1)}, u32[]{:S(2)}, u32[]{:S(2)}) collective-permute-start(bf16[784,128]{1,0:T(8,128)(2,1)S(1)} %slice.7), channel_id=1, source_target_pairs={{0,1},{1,0},{2,3},{3,2},{4,5},{5,4},{6,7},{7,6},{8,9},{9,8},{10,11... | collective-permute-start | bytes 602120 | tf_op jit(solution)/shard_map/ppermute | solution.py:212
  58.6 1.6 %collective-permute-start.12 = (bf16[768,128]{1,0:T(8,128)(2,1)S(1)}, bf16[768,128]{1,0:T(8,128)(2,1)S(1)}, u32[]{:S(2)}, u32[]{:S(2)}) collective-permute-start(bf16[768,128]{1,0:T(8,128)(2,1)S(1)} %slice.6), channel_id=1, source_target_pairs={{0,1},{1,0},{2,3},{3,2},{4,5},{5,4},{6,7},{7,6},{8,9},{9,8},{10,11... | collective-permute-start | bytes 589832 | tf_op jit(solution)/shard_map/ppermute | solution.py:212
  64.2 1.8 %collective-permute-start.15 = (bf16[1552,128]{1,0:T(8,128)(2,1)S(1)}, bf16[1552,128]{1,0:T(8,128)(2,1)S(1)}, u32[]{:S(2)}, u32[]{:S(2)}) collective-permute-start(bf16[1552,128]{1,0:T(8,128)(2,1)S(1)} %collective-permute-done.14.rest_7_), channel_id=1, source_target_pairs={{0,1},{1,0},{2,3},{3,2},{4,5},{5,4},{6,7},{7,6},{8,9},{9,8},{10,11... | collective-permute-start | bytes 1191944 | tf_op jit(solution)/shard_map/ppermute | solution.py:212
